TPU v7x, 32 devices: a whole 2x2x4 slice. The times are simulated.
32 devices in a mesh: grp: 4 (over x, core), dev: 8 (over z, y).
Axes of the slice: x: 2, y: 2, z: 4, core: 2. Of those that a mesh axis runs over, the one named last changes fastest.
Arguments:
- key_tokens: bfloat16 [4096, 768], P(('grp', 'dev')), may hold values from -6 to 6
- value_tokens: bfloat16 [4096, 768], P(('grp', 'dev')), may hold values from -6 to 6
- queries: bfloat16 [4096, 768], P(('grp', 'dev')), may hold values from -192 to 192
- token_rate: float32 [4096], P(('grp', 'dev')), may hold values from 0.0005638186 to 0.004510549
- fast_weights: bfloat16 [3, 1536, 768], P(None, ('grp', 'dev')), may hold values from -0.21875 to 0.21875
Outputs:
- target_out: bfloat16 [4096, 768], P(('grp', 'dev'))
All inputs are finite; a program needn't handle non-finite values.
Results may differ from a plain program's by a relative error of at most 0.012.
The roundings to bfloat16 on the way count: a program that leaves them out, or rounds other values in their place, can miss the bound.
Values may be sent and summed in bfloat16 or wider, within the bound.
No kernel may reach another device: no remote copies, remote signals or barrier semaphores. Data moves between devices by JAX's collectives and lax.ppermute only.
A program may use at most 64 MiB of HBM per device.

v0:
```python
import jax
import jax.numpy as jnp
from jax import lax
from jax.experimental import pallas as pl
from jax.experimental.pallas import tpu as pltpu
from jax.sharding import PartitionSpec as P

D = 768
HEADS = 12
HEAD_DIM = 64
CORES = 2
NEAR = 2
BF = jnp.bfloat16
F32 = jnp.float32

epsilon = 1e-06
AXES = ("grp", "dev")


def moves(mesh):
    n_grp, n_dev = mesh.shape["grp"], mesh.shape["dev"]
    n_gx, n_far = n_grp // CORES, n_dev // NEAR

    def build(target):
        pairs = []
        for gx in range(n_gx):
            for core in range(CORES):
                for far in range(n_far):
                    for near in range(NEAR):
                        to = target(gx, core, far, near)
                        source = (gx * CORES + core) * n_dev + far * NEAR + near
                        dest = (to[0] * CORES + to[1]) * n_dev + to[2] * NEAR + to[3]
                        pairs.append((source, dest))
        return pairs

    def along(step):
        return build(lambda gx, core, far, near: (gx, core, far ^ step, near))

    def layer(dx, dn):
        return build(lambda gx, core, far, near: (gx ^ dx, core, far, near ^ dn))

    swap = build(lambda gx, core, far, near: (gx, 1 - core, far, near))
    return n_far, along, layer, swap


def send(array, pairs):
    return lax.ppermute(array, AXES, pairs)


def after(value, *others):
    return lax.optimization_barrier((value, *others))[0]


def call(kernel, outs, *args, flops=0, scratch=(), in_hbm=(), limit=32 * 1024 * 1024, name=None):
    vmem = pl.BlockSpec(memory_space=pltpu.VMEM)
    size = sum(a.size * a.dtype.itemsize for a in args) + sum(o.size * o.dtype.itemsize for o in outs)
    result = pl.pallas_call(
        kernel,
        out_shape=list(outs),
        in_specs=[pl.BlockSpec(memory_space=pltpu.HBM) if i in in_hbm else vmem for i in range(len(args))],
        out_specs=[vmem] * len(outs),
        scratch_shapes=list(scratch),
        compiler_params=pltpu.CompilerParams(vmem_limit_bytes=limit),
        cost_estimate=pl.CostEstimate(flops=flops, bytes_accessed=size, transcendentals=0),
        name=name,
    )(*args)
    return result


def struct(shape, dtype):
    return jax.ShapeDtypeStruct(shape, dtype)


def nt(a, b):
    return lax.dot_general(a, b, (((1,), (1,)), ((), ())), preferred_element_type=F32)


def nn(a, b):
    return lax.dot_general(a, b, (((1,), (0,)), ((), ())), preferred_element_type=F32)


def rms(matrix):
    return matrix / jnp.sqrt(jnp.mean(matrix * matrix, axis=-1, keepdims=True) + epsilon)


def prep_kernel(key_hbm, value_hbm, query_hbm, rate_hbm, pair_ref, query_out, key_ref, value_ref, query_ref, rate_ref, sems):
    count = key_ref.shape[0]
    sources = (key_hbm, rate_hbm, value_hbm, query_hbm)
    targets = (key_ref, rate_ref, value_ref, query_ref)
    copies = [pltpu.make_async_copy(a, b, sems.at[i]) for i, (a, b) in enumerate(zip(sources, targets))]
    for copy in copies:
        copy.start()
    copies[0].wait()
    pair_ref[0] = rms(key_ref[...].astype(F32)).astype(BF)
    copies[1].wait()
    copies[2].wait()
    spread = jnp.broadcast_to(rate_ref[...], (count, count))
    row = lax.broadcasted_iota(jnp.int32, (count, count), 0)
    col = lax.broadcasted_iota(jnp.int32, (count, count), 1)
    rate = jnp.sum(jnp.where(row == col, spread, 0.0), axis=1, keepdims=True)
    pair_ref[1] = (-(rate * value_ref[...].astype(F32))).astype(BF)
    copies[3].wait()
    query_out[...] = rms(query_ref[...].astype(F32)).astype(BF)


def prep(key_tokens, value_tokens, queries, token_rate):
    count = key_tokens.shape[0]
    return call(
        prep_kernel,
        [struct((2, count, D), BF), struct((count, D), BF)],
        key_tokens, value_tokens, queries, token_rate.reshape(1, count),
        scratch=[pltpu.VMEM((count, D), BF)] * 3 + [pltpu.VMEM((1, count), F32), pltpu.SemaphoreType.DMA((4,))],
        in_hbm=(0, 1, 2, 3),
        limit=62 * 1024 * 1024,
        name="prep",
    )


def cut(rows):
    return 16 * ((3 * rows + 31) // 32)


def pieces(rows):
    edge = cut(rows)
    found = []
    for m in range(3):
        for low, high, chunk in ((0, edge, 0), (edge, 3 * rows, 1)):
            first, last = max(low, m * rows), min(high, (m + 1) * rows)
            if first < last:
                found.append((m, first - m * rows, last - first, chunk, first - low))
    return found


def stage(*arrays):
    def kernel(*refs):
        for source, target in zip(refs[:len(arrays)], refs[len(arrays):]):
            target[...] = source[...]

    return call(kernel, [struct(a.shape, a.dtype) for a in arrays], *arrays, name="stage")


def gradient(tokens, blocks, before=None):
    flat = [array for token in tokens for array in token]
    places, at = [], 0
    for token in tokens:
        places.append(((at, 0), (at, 1)) if len(token) == 1 else ((at, None), (at + 1, None)))
        at += len(token)
    count = flat[0].shape[-2]
    number, rows = len(blocks), blocks[0].shape[1]
    aligned = rows % 16 == 0
    if not aligned:
        blocks = [jnp.concatenate(blocks, axis=1)]
    size = blocks[0].shape[1]
    units = number * rows
    given = before is not None

    def kernel(*refs):
        token_refs = refs[:len(flat)]
        block_refs = refs[len(flat):len(flat) + len(blocks)]
        weights = refs[-1]
        total = refs[-2]
        if given:
            base = refs[len(flat) + len(blocks)]
        for i, ref in enumerate(block_refs):
            for m in range(3):
                weights[m * units + i * size:m * units + (i + 1) * size] = ref[m]

        def read(place):
            ref, part = token_refs[place[0]], place[1]
            return ref[...] if part is None else ref[part]

        for j in range(0, len(tokens), 2):
            keys = jnp.concatenate([read(place[0]) for place in places[j:j + 2]], axis=0)
            signal = jnp.concatenate([read(place[1]) for place in places[j:j + 2]], axis=0)
            acts = nt(weights[:2 * units], keys)
            gate_act, up_act = acts[:units], acts[units:]
            sg = jax.nn.sigmoid(gate_act)
            silu = gate_act * sg
            hidden = (silu * up_act).astype(BF)
            hidden_grad = nt(weights[2 * units:], signal)
            gate_grad = (hidden_grad * up_act * sg * (1.0 + gate_act * (1.0 - sg))).astype(BF)
            up_grad = (hidden_grad * silu).astype(BF)
            first = nn(jnp.concatenate([gate_grad, up_grad], axis=0), keys)
            last = nn(hidden, signal)
            if j or given:
                source = total if j else base
                first, last = source[:2 * units] + first, source[2 * units:] + last
            total[:2 * units] = first
            total[2 * units:] = last
        if given and aligned:
            out_refs = refs[len(flat) + len(blocks) + 1:-2]
            for m, row, span, chunk, place in pieces(rows):
                for k in range(number):
                    source = total[m * units + k * rows + row:m * units + k * rows + row + span]
                    out = out_refs[2 * chunk + (k + 1) % 2]
                    out[k // 2, place:place + span] = source.astype(out.dtype)

    edges = (cut(rows), 3 * rows - cut(rows))
    scratch = [pltpu.VMEM((3 * units, D), BF)]
    outs = [struct((3 * units, D), F32)]
    if given and aligned:
        scratch = [pltpu.VMEM((3 * units, D), F32), *scratch]
        outs = [struct((number // 2, edge, D), kind) for edge in edges for kind in (BF, F32)]
    outs = call(
        kernel, outs, *flat, *blocks, *([before] if given else []),
        flops=12 * count * len(tokens) * units * D,
        scratch=scratch,
        name="gradient" if given else "gradient_part",
    )
    if not given:
        return outs[0]
    if aligned:
        return outs[:2], outs[2:]
    total = outs[0].reshape(3, number, rows, D).swapaxes(0, 1).reshape(number, 3 * rows, D)
    parts = total[:, :edges[0]], total[:, edges[0]:]
    return [(part[1::2].astype(BF), part[::2]) for part in parts]


def fold(keep, arrived):
    number, rows = keep.shape[:2]

    def kernel(keep_ref, arrived_ref, send_ref, kept_ref):
        for k in range(number):
            total = keep_ref[k] + arrived_ref[k].astype(F32)
            out = send_ref if k % 2 else kept_ref
            out[k // 2] = total.astype(out.dtype)

    shape = (number // 2, rows, D)
    return call(kernel, [struct(shape, BF), struct(shape, F32)], keep, arrived, name="fold")


def step(old, keep, arrived):
    def kernel(old_ref, keep_ref, arrived_ref, out_ref):
        old_rows = old_ref[...].astype(F32)
        stepped = old_rows - (keep_ref[0] + arrived_ref[0].astype(F32))
        out_ref[...] = (
            stepped
            * jnp.sqrt(jnp.mean(old_rows * old_rows, axis=-1, keepdims=True) + epsilon)
            / jnp.sqrt(jnp.mean(stepped * stepped, axis=-1, keepdims=True) + epsilon)
        ).astype(BF)

    return call(kernel, [struct(old.shape, BF)], old, keep, arrived, name="step")[0]


def attention_kernel(query_ref, key_ref, value_ref, out_ref):
    count = key_ref.shape[0]
    width = 2 * HEAD_DIM
    low = lax.broadcasted_iota(jnp.int32, (count, width), 1) < HEAD_DIM
    zero = jnp.zeros((count, width), BF)
    for h in range(HEADS // 2):
        cols = slice(h * width, (h + 1) * width)
        query, key, value = query_ref[:, cols], key_ref[:, cols], value_ref[:, cols]
        probs = []
        for keep in (low, ~low):
            scores = nt(query, jnp.where(keep, key, zero)) * HEAD_DIM ** (-0.5)
            weights = jnp.exp(scores - jnp.max(scores, axis=-1, keepdims=True))
            probs.append((weights / jnp.sum(weights, axis=-1, keepdims=True)).astype(BF))
        values = jnp.concatenate([jnp.where(low, value, zero), jnp.where(low, zero, value)], axis=0)
        out_ref[:, cols] = nn(jnp.concatenate(probs, axis=1), values)


def attention(queries, key_tokens, value_tokens):
    return call(
        attention_kernel, [struct(queries.shape, F32)], queries, key_tokens, value_tokens,
        flops=4 * queries.shape[0] * key_tokens.shape[0] * D, name="attention",
    )[0]


def apply_rows(queries, blocks, rows):
    count = queries[0].shape[0]
    number = len(blocks)
    aligned = rows % 16 == 0
    if not aligned:
        whole = [jnp.concatenate(chunks, axis=0).reshape(3, rows, D) for chunks in blocks]
        blocks = [[jnp.concatenate(whole, axis=1).reshape(3 * number * rows, D)]]
    chunks = [chunk for block in blocks for chunk in block]
    units = number * rows

    def kernel(*refs):
        query_refs = refs[:len(queries)]
        chunk_refs = list(refs[len(queries):len(queries) + len(chunks)])
        out_refs = refs[len(queries) + len(chunks):-1]
        weights = refs[-1]
        if aligned:
            for i, block in enumerate(blocks):
                own_refs = [chunk_refs.pop(0) for _ in block]
                for m, row, size, chunk, place in pieces(rows):
                    start = m * units + i * rows + row
                    if len(block) == 1:
                        weights[start:start + size] = own_refs[0][m * rows + row:m * rows + row + size]
                    else:
                        weights[start:start + size] = own_refs[chunk][place:place + size]
        else:
            weights[...] = chunk_refs[0][...]
        stacked = jnp.concatenate([ref[...] for ref in query_refs], axis=0)
        gate_act = nt(stacked, weights[:units])
        up_act = nt(stacked, weights[units:2 * units])
        hidden = (jax.nn.silu(gate_act) * up_act).astype(BF)
        result = nn(hidden, weights[2 * units:])
        for i, out in enumerate(out_refs):
            out[...] = result[i * count:(i + 1) * count].astype(out.dtype)

    outs = [struct((count, D), BF) for _ in queries[:-1]] + [struct((count, D), F32)]
    return call(
        kernel, outs, *queries, *chunks,
        flops=6 * count * len(queries) * units * D,
        scratch=[pltpu.VMEM((3 * units, D), BF)],
        name="apply",
    )


def total_kernel(*refs):
    result = refs[0][...] + refs[1][...]
    for ref in refs[2:-1]:
        result = result + ref[...].astype(F32)
    refs[-1][...] = result.astype(BF)


def solution(mesh):
    n_far, along, layer, swap = moves(mesh)
    bits = [1 << i for i in range(n_far.bit_length() - 1)]

    def line_gather(block, near_first=False):
        blocks = {0: block}
        for bit in reversed(bits):
            for k in list(blocks):
                source = after(blocks[k], blocks[1]) if near_first and k and bit == 1 else blocks[k]
                blocks[k ^ bit] = send(source, along(bit))
        return blocks

    def body(key_tokens, value_tokens, queries, token_rate, fast_weights):
        rows = fast_weights.shape[1]
        pair, query_normed = prep(key_tokens, value_tokens, queries, token_rate)
        at_x, at_y, corner = [send(pair, layer(*o)) for o in ((1, 0), (0, 1), (1, 1))]
        line = line_gather(fast_weights)
        own_weights, own_pair = stage(after(fast_weights, line[bits[-1]]), pair)
        own_there = send(after(own_pair, at_x, *[line[k] for k in range(1, n_far)]), swap)
        blocks = [own_weights] + [line[k] for k in range(1, n_far)]
        tokens = [own_pair, own_there, at_y, at_x, send(at_y, swap), send(at_x, swap)]
        part = gradient([(token,) for token in tokens], blocks)
        chunks = gradient([(corner,), (send(corner, swap),)], blocks, part)

        query_normed = after(query_normed, chunks[0][0])
        all_queries = [send(query_normed, layer(*o)) for o in ((1, 0), (0, 1))]
        mixed = attention(queries, key_tokens, value_tokens)

        flat = own_weights.reshape(3 * rows, D)
        olds = flat[:cut(rows)], flat[cut(rows):]
        stepped = []
        for old, (part, keep) in zip(olds, chunks):
            for bit in bits[:-1]:
                arrived = send(part, along(bit))
                if stepped:
                    keep = after(keep, *all_queries)
                part, keep = fold(keep, arrived)
            updated = step(old, keep, send(part, along(bits[-1])))
            stepped.append(line_gather(updated, near_first=not stepped))
        corner_query = send(after(query_normed, all_queries[0]), layer(1, 1))
        blocks = [[chunk[k] for chunk in stepped] for k in range(n_far)]
        there = [[send(array, swap) for array in block] for block in blocks[:-1]]
        there.append([send(after(array, corner_query), swap) for array in blocks[-1]])
        blocks += there

        outs = apply_rows(all_queries + [corner_query, query_normed], blocks, rows)
        back = [send(part, layer(*o)) for part, o in zip(outs[:-1], ((1, 0), (0, 1), (1, 1)))]
        return call(total_kernel, [struct(queries.shape, BF)], outs[-1], mixed, *back, name="total")[0]

    in_specs = (
        P(("grp", "dev"), None),
        P(("grp", "dev"), None),
        P(("grp", "dev"), None),
        P(("grp", "dev")),
        P(None, ("grp", "dev"), None),
    )
    out_specs = P(("grp", "dev"), None)
    return jax.shard_map(body, mesh=mesh, in_specs=in_specs, out_specs=out_specs, check_vma=False)
```

profile of v0, /device:TPU:0, one launch (start us, length us, event | category | flops | bytes accessed | tf_op | source)
XLA Modules:
  0.0 84.4 jit_solution(8350124278526177715)
XLA Ops:
  0.0 4.0 %collective-permute-start.2 = (bf16[3,48,768]{2,1,0:T(8,128)(2,1)}, bf16[3,48,768]{2,1,0:T(8,128)(2,1)S(1)}, u32[]{:S(2)}, u32[]{:S(2)}) collective-permute-start(bf16[3,48,768]{2,1,0:T(8,128)(2,1)} %refs_0_), channel_id=1, source_target_pairs={{0,4},{1,5},{2,6},{3,7},{4,0},{5,1},{6,2},{7,3},{8,12},{9,13},{10,... | collective-permute-start | bytes 663560 | tf_op jit(solution)/shard_map/ppermute | solution.py:47
  4.0 2.0 %prep.1 = (bf16[2,128,768]{2,1,0:T(8,128)(2,1)}, bf16[128,768]{1,0:T(8,128)(2,1)}) custom-call(bf16[128,768]{1,0:T(8,128)(2,1)} %key_ref.1, bf16[128,768]{1,0:T(8,128)(2,1)} %value_ref.1, bf16[128,768]{1,0:T(8,128)(2,1)} %query_ref.1, f32[1,128]{1,0:T(1,128)} %bitcast.4), custom_call_target="tpu_custom_call" | custom-call | bytes 1180160 | tf_op jit(solution)/shard_map/prep/pallas_call | solution.py:57
  6.1 1.6 %collective-permute-start.5 = (bf16[2,128,768]{2,1,0:T(8,128)(2,1)}, bf16[2,128,768]{2,1,0:T(8,128)(2,1)S(1)}, u32[]{:S(2)}, u32[]{:S(2)}) collective-permute-start(bf16[2,128,768]{2,1,0:T(8,128)(2,1)} %get-tuple-element.30.refs_1_), channel_id=1, source_target_pairs={{0,16},{1,17},{2,18},{3,19},{4,20},{5,21},{6,22},{7,23},{8,24},{9,... | collective-permute-start | bytes 1179656 | tf_op jit(solution)/shard_map/ppermute | solution.py:47
  7.6 1.5 %collective-permute-start.7 = (bf16[2,128,768]{2,1,0:T(8,128)(2,1)}, bf16[2,128,768]{2,1,0:T(8,128)(2,1)S(1)}, u32[]{:S(2)}, u32[]{:S(2)}) collective-permute-start(bf16[2,128,768]{2,1,0:T(8,128)(2,1)} %get-tuple-element.30.refs_1_), channel_id=1, source_target_pairs={{0,1},{1,0},{2,3},{3,2},{4,5},{5,4},{6,7},{7,6},{8,9},{9,8},{10,11... | collective-permute-start | bytes 1179656 | tf_op jit(solution)/shard_map/ppermute | solution.py:47
  9.6 1.6 %collective-permute-start.3 = (bf16[3,48,768]{2,1,0:T(8,128)(2,1)}, bf16[3,48,768]{2,1,0:T(8,128)(2,1)S(1)}, u32[]{:S(2)}, u32[]{:S(2)}) collective-permute-start(bf16[3,48,768]{2,1,0:T(8,128)(2,1)} %refs_0_), channel_id=1, source_target_pairs={{0,2},{1,3},{2,0},{3,1},{4,6},{5,7},{6,4},{7,5},{8,10},{9,11},{10,... | collective-permute-start | bytes 663560 | tf_op jit(solution)/shard_map/ppermute | solution.py:47
  11.2 3.3 %collective-permute-done.2.refs_8_.refs_4_ = bf16[3,48,768]{2,1,0:T(8,128)(2,1)S(1)} collective-permute-done((bf16[3,48,768]{2,1,0:T(8,128)(2,1)}, bf16[3,48,768]{2,1,0:T(8,128)(2,1)S(1)}, u32[]{:S(2)}, u32[]{:S(2)}) %collective-permute-start.2) | collective-permute-done | bytes 221216 | tf_op jit(solution)/shard_map/ppermute | solution.py:47
  18.4 8.2 %collective-permute-done.7.refs_2_ = bf16[2,128,768]{2,1,0:T(8,128)(2,1)S(1)} collective-permute-done((bf16[2,128,768]{2,1,0:T(8,128)(2,1)}, bf16[2,128,768]{2,1,0:T(8,128)(2,1)S(1)}, u32[]{:S(2)}, u32[]{:S(2)}) %collective-permute-start.7) | collective-permute-done | bytes 393248 | tf_op jit(solution)/shard_map/ppermute | solution.py:47
  28.9 2.2 %gradient_part.1.refs_6_ = f32[576,768]{1,0:T(8,128)S(1)} custom-call(bf16[2,128,768]{2,1,0:T(8,128)(2,1)S(1)} %get-tuple-element.34.refs_0_, bf16[2,128,768]{2,1,0:T(8,128)(2,1)S(1)} %collective-permute-done.6.refs_1_, bf16[2,128,768]{2,1,0:T(8,128)(2,1)S(1)} %collective-permute-done.7.refs_2_, bf16[2,128,768]{2,1,0:T(8,128)(2,1)S(1)} %collective-permute-done.5.refs_3_, ...), custom_call_target="tpu_custom_call" | custom-call | flops 1358954496 | bytes 5013504 | tf_op jit(solution)/shard_map/gradient_part/pallas_call | solution.py:57
  32.0 1.6 %collective-permute-start.13 = (bf16[2,80,768]{2,1,0:T(8,128)(2,1)S(1)}, bf16[2,80,768]{2,1,0:T(8,128)(2,1)S(1)}, u32[]{:S(2)}, u32[]{:S(2)}) collective-permute-start(bf16[2,80,768]{2,1,0:T(8,128)(2,1)S(1)} %get-tuple-element.35), channel_id=1, source_target_pairs={{0,2},{1,3},{2,0},{3,1},{4,6},{5,7},{6,4},{7,5},{8,10},{9,11},{10,... | collective-permute-start | bytes 737288 | tf_op jit(solution)/shard_map/ppermute | solution.py:47
  33.7 2.1 %collective-permute-start.11 = (bf16[128,768]{1,0:T(8,128)(2,1)S(1)}, bf16[128,768]{1,0:T(8,128)(2,1)S(1)}, u32[]{:S(2)}, u32[]{:S(2)}) collective-permute-start(bf16[128,768]{1,0:T(8,128)(2,1)S(1)} %copy-done.5), channel_id=1, source_target_pairs={{0,1},{1,0},{2,3},{3,2},{4,5},{5,4},{6,7},{7,6},{8,9},{9,8},{10,11... | collective-permute-start | bytes 589832 | tf_op jit(solution)/shard_map/ppermute | solution.py:47
  36.2 4.7 %collective-permute-done.13.arrived_ref = bf16[2,80,768]{2,1,0:T(8,128)(2,1)S(1)} collective-permute-done((bf16[2,80,768]{2,1,0:T(8,128)(2,1)S(1)}, bf16[2,80,768]{2,1,0:T(8,128)(2,1)S(1)}, u32[]{:S(2)}, u32[]{:S(2)}) %collective-permute-start.13) | collective-permute-done | bytes 245792 | tf_op jit(solution)/shard_map/ppermute | solution.py:47
  41.4 4.1 %collective-permute-done.15.arrived_ref = bf16[2,64,768]{2,1,0:T(8,128)(2,1)S(1)} collective-permute-done((bf16[2,64,768]{2,1,0:T(8,128)(2,1)S(1)}, bf16[2,64,768]{2,1,0:T(8,128)(2,1)S(1)}, u32[]{:S(2)}, u32[]{:S(2)}) %collective-permute-start.15) | collective-permute-done | bytes 196640 | tf_op jit(solution)/shard_map/ppermute | solution.py:47
  45.6 1.5 %collective-permute-start.12 = (bf16[128,768]{1,0:T(8,128)(2,1)S(1)}, bf16[128,768]{1,0:T(8,128)(2,1)S(1)}, u32[]{:S(2)}, u32[]{:S(2)}) collective-permute-start(bf16[128,768]{1,0:T(8,128)(2,1)S(1)} %copy-done.5), channel_id=1, source_target_pairs={{0,17},{1,16},{2,19},{3,18},{4,21},{5,20},{6,23},{7,22},{8,25},{9,... | collective-permute-start | bytes 589832 | tf_op jit(solution)/shard_map/ppermute | solution.py:47
  47.1 2.4 %collective-permute-done.14.arrived_ref = bf16[1,80,768]{2,1,0:T(8,128)(2,1)S(1)} collective-permute-done((bf16[1,80,768]{2,1,0:T(8,128)(2,1)S(1)}, bf16[1,80,768]{2,1,0:T(8,128)(2,1)S(1)}, u32[]{:S(2)}, u32[]{:S(2)}) %collective-permute-start.14) | collective-permute-done | bytes 122912 | tf_op jit(solution)/shard_map/ppermute | solution.py:47
  50.4 3.6 %collective-permute-start.19 = (bf16[80,768]{1,0:T(8,128)(2,1)S(1)}, bf16[80,768]{1,0:T(8,128)(2,1)S(1)}, u32[]{:S(2)}, u32[]{:S(2)}) collective-permute-start(bf16[80,768]{1,0:T(8,128)(2,1)S(1)} %step.2.refs_4_), channel_id=1, source_target_pairs={{0,4},{1,5},{2,6},{3,7},{4,0},{5,1},{6,2},{7,3},{8,12},{9,13},{10,... | collective-permute-start | bytes 368648 | tf_op jit(solution)/shard_map/ppermute | solution.py:47
  54.8 3.2 %collective-permute-start.18 = (bf16[64,768]{1,0:T(8,128)(2,1)S(1)}, bf16[64,768]{1,0:T(8,128)(2,1)S(1)}, u32[]{:S(2)}, u32[]{:S(2)}) collective-permute-start(bf16[64,768]{1,0:T(8,128)(2,1)S(1)} %step.3.refs_5_), channel_id=1, source_target_pairs={{0,2},{1,3},{2,0},{3,1},{4,6},{5,7},{6,4},{7,5},{8,10},{9,11},{10,... | collective-permute-start | bytes 294920 | tf_op jit(solution)/shard_map/ppermute | solution.py:47
  57.9 3.1 %collective-permute-done.19.refs_8_ = bf16[80,768]{1,0:T(8,128)(2,1)S(1)} collective-permute-done((bf16[80,768]{1,0:T(8,128)(2,1)S(1)}, bf16[80,768]{1,0:T(8,128)(2,1)S(1)}, u32[]{:S(2)}, u32[]{:S(2)}) %collective-permute-start.19) | collective-permute-done | bytes 122912 | tf_op jit(solution)/shard_map/ppermute | solution.py:47
  63.6 3.3 %collective-permute-done.21.refs_10_ = bf16[80,768]{1,0:T(8,128)(2,1)S(1)} collective-permute-done((bf16[80,768]{1,0:T(8,128)(2,1)S(1)}, bf16[80,768]{1,0:T(8,128)(2,1)S(1)}, u32[]{:S(2)}, u32[]{:S(2)}) %collective-permute-start.21) | collective-permute-done | bytes 122912 | tf_op jit(solution)/shard_map/ppermute | solution.py:47
  69.7 1.5 %apply.1 = (bf16[128,768]{1,0:T(8,128)(2,1)S(1)}, bf16[128,768]{1,0:T(8,128)(2,1)S(1)}, bf16[128,768]{1,0:T(8,128)(2,1)S(1)}, f32[128,768]{1,0:T(8,128)S(1)}) custom-call(bf16[128,768]{1,0:T(8,128)(2,1)S(1)} %collective-permute-done.10.refs_0_, bf16[128,768]{1,0:T(8,128)(2,1)S(1)} %collective-permute-done.11.refs_1_, ...), custom_call_target="tpu_custom_call" | custom-call | flops 905969664 | bytes 3538944 | tf_op jit(solution)/shard_map/apply/pallas_call | solution.py:57
  71.7 1.8 %collective-permute-start.32 = (bf16[128,768]{1,0:T(8,128)(2,1)S(1)}, bf16[128,768]{1,0:T(8,128)(2,1)S(1)}, u32[]{:S(2)}, u32[]{:S(2)}) collective-permute-start(bf16[128,768]{1,0:T(8,128)(2,1)S(1)} %get-tuple-element.51), channel_id=1, source_target_pairs={{0,1},{1,0},{2,3},{3,2},{4,5},{5,4},{6,7},{7,6},{8,9},{9,8},{10,11... | collective-permute-start | bytes 589832 | tf_op jit(solution)/shard_map/ppermute | solution.py:47
  74.8 2.1 %attention.1.refs_1_ = f32[128,768]{1,0:T(8,128)S(1)} custom-call(bf16[128,768]{1,0:T(8,128)(2,1)S(1)} %copy-done.2, bf16[128,768]{1,0:T(8,128)(2,1)S(1)} %copy-done, bf16[128,768]{1,0:T(8,128)(2,1)S(1)} %copy-done.1), custom_call_target="tpu_custom_call" | custom-call | flops 50331648 | bytes 983040 | tf_op jit(solution)/shard_map/attention/pallas_call | solution.py:57
  76.9 2.2 %collective-permute-done.31.refs_2_ = bf16[128,768]{1,0:T(8,128)(2,1)S(1)} collective-permute-done((bf16[128,768]{1,0:T(8,128)(2,1)S(1)}, bf16[128,768]{1,0:T(8,128)(2,1)S(1)}, u32[]{:S(2)}, u32[]{:S(2)}) %collective-permute-start.31) | collective-permute-done | bytes 196640 | tf_op jit(solution)/shard_map/ppermute | solution.py:47
  79.1 2.9 %collective-permute-done.32.refs_3_ = bf16[128,768]{1,0:T(8,128)(2,1)S(1)} collective-permute-done((bf16[128,768]{1,0:T(8,128)(2,1)S(1)}, bf16[128,768]{1,0:T(8,128)(2,1)S(1)}, u32[]{:S(2)}, u32[]{:S(2)}) %collective-permute-start.32) | collective-permute-done | bytes 196640 | tf_op jit(solution)/shard_map/ppermute | solution.py:47
  82.0 1.6 %collective-permute-done.33.refs_4_ = bf16[128,768]{1,0:T(8,128)(2,1)S(1)} collective-permute-done((bf16[128,768]{1,0:T(8,128)(2,1)S(1)}, bf16[128,768]{1,0:T(8,128)(2,1)S(1)}, u32[]{:S(2)}, u32[]{:S(2)}) %collective-permute-start.33) | collective-permute-done | bytes 196640 | tf_op jit(solution)/shard_map/ppermute | solution.py:47
  (69 shorter events, 18.1 us)
Async XLA Ops:
  0.0 14.5 %collective-permute-start.2 = (bf16[3,48,768]{2,1,0:T(8,128)(2,1)}, bf16[3,48,768]{2,1,0:T(8,128)(2,1)S(1)}, u32[]{:S(2)}, u32[]{:S(2)}) collective-permute-start(bf16[3,48,768]{2,1,0:T(8,128)(2,1)} %refs_0_), channel_id=1, source_target_pairs={{0,4},{1,5},{2,6},{3,7},{4,0},{5,1},{6,2},{7,3},{8,12},{9,13},{10,... | collective-permute-start | bytes 663560 | tf_op jit(solution)/shard_map/ppermute | solution.py:47
  6.1 12.3 %collective-permute-start.5 = (bf16[2,128,768]{2,1,0:T(8,128)(2,1)}, bf16[2,128,768]{2,1,0:T(8,128)(2,1)S(1)}, u32[]{:S(2)}, u32[]{:S(2)}) collective-permute-start(bf16[2,128,768]{2,1,0:T(8,128)(2,1)} %get-tuple-element.30.refs_1_), channel_id=1, source_target_pairs={{0,16},{1,17},{2,18},{3,19},{4,20},{5,21},{6,22},{7,23},{8,24},{9,... | collective-permute-start | bytes 1179656 | tf_op jit(solution)/shard_map/ppermute | solution.py:47
  7.6 18.9 %collective-permute-start.7 = (bf16[2,128,768]{2,1,0:T(8,128)(2,1)}, bf16[2,128,768]{2,1,0:T(8,128)(2,1)S(1)}, u32[]{:S(2)}, u32[]{:S(2)}) collective-permute-start(bf16[2,128,768]{2,1,0:T(8,128)(2,1)} %get-tuple-element.30.refs_1_), channel_id=1, source_target_pairs={{0,1},{1,0},{2,3},{3,2},{4,5},{5,4},{6,7},{7,6},{8,9},{9,8},{10,11... | collective-permute-start | bytes 1179656 | tf_op jit(solution)/shard_map/ppermute | solution.py:47
  9.2 17.9 %collective-permute-start = (bf16[2,128,768]{2,1,0:T(8,128)(2,1)}, bf16[2,128,768]{2,1,0:T(8,128)(2,1)S(1)}, u32[]{:S(2)}, u32[]{:S(2)}) collective-permute-start(bf16[2,128,768]{2,1,0:T(8,128)(2,1)} %get-tuple-element.30.refs_1_), channel_id=1, source_target_pairs={{0,17},{1,16},{2,19},{3,18},{4,21},{5,20},{6,23},{7,22},{8,25},{9,... | collective-permute-start | bytes 1179656 | tf_op jit(solution)/shard_map/ppermute | solution.py:47
  9.6 16.9 %collective-permute-start.3 = (bf16[3,48,768]{2,1,0:T(8,128)(2,1)}, bf16[3,48,768]{2,1,0:T(8,128)(2,1)S(1)}, u32[]{:S(2)}, u32[]{:S(2)}) collective-permute-start(bf16[3,48,768]{2,1,0:T(8,128)(2,1)} %refs_0_), channel_id=1, source_target_pairs={{0,2},{1,3},{2,0},{3,1},{4,6},{5,7},{6,4},{7,5},{8,10},{9,11},{10,... | collective-permute-start | bytes 663560 | tf_op jit(solution)/shard_map/ppermute | solution.py:47
  14.5 12.1 %collective-permute-start.4 = (bf16[3,48,768]{2,1,0:T(8,128)(2,1)S(1)}, bf16[3,48,768]{2,1,0:T(8,128)(2,1)S(1)}, u32[]{:S(2)}, u32[]{:S(2)}) collective-permute-start(bf16[3,48,768]{2,1,0:T(8,128)(2,1)S(1)} %collective-permute-done.2.refs_8_.refs_4_), channel_id=1, source_target_pairs={{0,2},{1,3},{2,0},{3,1},{4,6},{5,7},{6,4},{7,5},{8,10},{9,11},{10,... | collective-permute-start | bytes 663560 | tf_op jit(solution)/shard_map/ppermute | solution.py:47
  18.4 8.8 %collective-permute-start.9 = (bf16[2,128,768]{2,1,0:T(8,128)(2,1)S(1)}, bf16[2,128,768]{2,1,0:T(8,128)(2,1)S(1)}, u32[]{:S(2)}, u32[]{:S(2)}) collective-permute-start(bf16[2,128,768]{2,1,0:T(8,128)(2,1)S(1)} %collective-permute-done.5.refs_3_), channel_id=1, source_target_pairs={{0,8},{1,9},{2,10},{3,11},{4,12},{5,13},{6,14},{7,15},{8,0},{9,1},... | collective-permute-start | bytes 1179656 | tf_op jit(solution)/shard_map/ppermute | solution.py:47
  32.0 8.9 %collective-permute-start.13 = (bf16[2,80,768]{2,1,0:T(8,128)(2,1)S(1)}, bf16[2,80,768]{2,1,0:T(8,128)(2,1)S(1)}, u32[]{:S(2)}, u32[]{:S(2)}) collective-permute-start(bf16[2,80,768]{2,1,0:T(8,128)(2,1)S(1)} %get-tuple-element.35), channel_id=1, source_target_pairs={{0,2},{1,3},{2,0},{3,1},{4,6},{5,7},{6,4},{7,5},{8,10},{9,11},{10,... | collective-permute-start | bytes 737288 | tf_op jit(solution)/shard_map/ppermute | solution.py:47
  33.7 7.7 %collective-permute-start.10 = (bf16[128,768]{1,0:T(8,128)(2,1)S(1)}, bf16[128,768]{1,0:T(8,128)(2,1)S(1)}, u32[]{:S(2)}, u32[]{:S(2)}) collective-permute-start(bf16[128,768]{1,0:T(8,128)(2,1)S(1)} %copy-done.5), channel_id=1, source_target_pairs={{0,16},{1,17},{2,18},{3,19},{4,20},{5,21},{6,22},{7,23},{8,24},{9,... | collective-permute-start | bytes 589832 | tf_op jit(solution)/shard_map/ppermute | solution.py:47
  33.7 7.7 %collective-permute-start.11 = (bf16[128,768]{1,0:T(8,128)(2,1)S(1)}, bf16[128,768]{1,0:T(8,128)(2,1)S(1)}, u32[]{:S(2)}, u32[]{:S(2)}) collective-permute-start(bf16[128,768]{1,0:T(8,128)(2,1)S(1)} %copy-done.5), channel_id=1, source_target_pairs={{0,1},{1,0},{2,3},{3,2},{4,5},{5,4},{6,7},{7,6},{8,9},{9,8},{10,11... | collective-permute-start | bytes 589832 | tf_op jit(solution)/shard_map/ppermute | solution.py:47
  35.7 9.7 %collective-permute-start.15 = (bf16[2,64,768]{2,1,0:T(8,128)(2,1)S(1)}, bf16[2,64,768]{2,1,0:T(8,128)(2,1)S(1)}, u32[]{:S(2)}, u32[]{:S(2)}) collective-permute-start(bf16[2,64,768]{2,1,0:T(8,128)(2,1)S(1)} %get-tuple-element.43), channel_id=1, source_target_pairs={{0,2},{1,3},{2,0},{3,1},{4,6},{5,7},{6,4},{7,5},{8,10},{9,11},{10,... | collective-permute-start | bytes 589832 | tf_op jit(solution)/shard_map/ppermute | solution.py:47
  41.0 8.5 %collective-permute-start.14 = (bf16[1,80,768]{2,1,0:T(8,128)(2,1)S(1)}, bf16[1,80,768]{2,1,0:T(8,128)(2,1)S(1)}, u32[]{:S(2)}, u32[]{:S(2)}) collective-permute-start(bf16[1,80,768]{2,1,0:T(8,128)(2,1)S(1)} %get-tuple-element.40), channel_id=1, source_target_pairs={{0,4},{1,5},{2,6},{3,7},{4,0},{5,1},{6,2},{7,3},{8,12},{9,13},{10,... | collective-permute-start | bytes 368648 | tf_op jit(solution)/shard_map/ppermute | solution.py:47
  45.5 9.0 %collective-permute-start.16 = (bf16[1,64,768]{2,1,0:T(8,128)(2,1)S(1)}, bf16[1,64,768]{2,1,0:T(8,128)(2,1)S(1)}, u32[]{:S(2)}, u32[]{:S(2)}) collective-permute-start(bf16[1,64,768]{2,1,0:T(8,128)(2,1)S(1)} %get-tuple-element.45), channel_id=1, source_target_pairs={{0,4},{1,5},{2,6},{3,7},{4,0},{5,1},{6,2},{7,3},{8,12},{9,13},{10,... | collective-permute-start | bytes 294920 | tf_op jit(solution)/shard_map/ppermute | solution.py:47
  45.6 15.5 %collective-permute-start.12 = (bf16[128,768]{1,0:T(8,128)(2,1)S(1)}, bf16[128,768]{1,0:T(8,128)(2,1)S(1)}, u32[]{:S(2)}, u32[]{:S(2)}) collective-permute-start(bf16[128,768]{1,0:T(8,128)(2,1)S(1)} %copy-done.5), channel_id=1, source_target_pairs={{0,17},{1,16},{2,19},{3,18},{4,21},{5,20},{6,23},{7,22},{8,25},{9,... | collective-permute-start | bytes 589832 | tf_op jit(solution)/shard_map/ppermute | solution.py:47
  49.7 8.3 %collective-permute-start.17 = (bf16[80,768]{1,0:T(8,128)(2,1)S(1)}, bf16[80,768]{1,0:T(8,128)(2,1)S(1)}, u32[]{:S(2)}, u32[]{:S(2)}) collective-permute-start(bf16[80,768]{1,0:T(8,128)(2,1)S(1)} %step.2.refs_4_), channel_id=1, source_target_pairs={{0,2},{1,3},{2,0},{3,1},{4,6},{5,7},{6,4},{7,5},{8,10},{9,11},{10,... | collective-permute-start | bytes 368648 | tf_op jit(solution)/shard_map/ppermute | solution.py:47
  50.4 10.6 %collective-permute-start.19 = (bf16[80,768]{1,0:T(8,128)(2,1)S(1)}, bf16[80,768]{1,0:T(8,128)(2,1)S(1)}, u32[]{:S(2)}, u32[]{:S(2)}) collective-permute-start(bf16[80,768]{1,0:T(8,128)(2,1)S(1)} %step.2.refs_4_), channel_id=1, source_target_pairs={{0,4},{1,5},{2,6},{3,7},{4,0},{5,1},{6,2},{7,3},{8,12},{9,13},{10,... | collective-permute-start | bytes 368648 | tf_op jit(solution)/shard_map/ppermute | solution.py:47
  54.7 7.5 %collective-permute-start.20 = (bf16[64,768]{1,0:T(8,128)(2,1)S(1)}, bf16[64,768]{1,0:T(8,128)(2,1)S(1)}, u32[]{:S(2)}, u32[]{:S(2)}) collective-permute-start(bf16[64,768]{1,0:T(8,128)(2,1)S(1)} %step.3.refs_5_), channel_id=1, source_target_pairs={{0,4},{1,5},{2,6},{3,7},{4,0},{5,1},{6,2},{7,3},{8,12},{9,13},{10,... | collective-permute-start | bytes 294920 | tf_op jit(solution)/shard_map/ppermute | solution.py:47
  54.8 8.8 %collective-permute-start.18 = (bf16[64,768]{1,0:T(8,128)(2,1)S(1)}, bf16[64,768]{1,0:T(8,128)(2,1)S(1)}, u32[]{:S(2)}, u32[]{:S(2)}) collective-permute-start(bf16[64,768]{1,0:T(8,128)(2,1)S(1)} %step.3.refs_5_), channel_id=1, source_target_pairs={{0,2},{1,3},{2,0},{3,1},{4,6},{5,7},{6,4},{7,5},{8,10},{9,11},{10,... | collective-permute-start | bytes 294920 | tf_op jit(solution)/shard_map/ppermute | solution.py:47
  61.0 5.8 %collective-permute-start.21 = (bf16[80,768]{1,0:T(8,128)(2,1)S(1)}, bf16[80,768]{1,0:T(8,128)(2,1)S(1)}, u32[]{:S(2)}, u32[]{:S(2)}) collective-permute-start(bf16[80,768]{1,0:T(8,128)(2,1)S(1)} %collective-permute-done.19.refs_8_), channel_id=1, source_target_pairs={{0,2},{1,3},{2,0},{3,1},{4,6},{5,7},{6,4},{7,5},{8,10},{9,11},{10,... | collective-permute-start | bytes 368648 | tf_op jit(solution)/shard_map/ppermute | solution.py:47
  61.0 6.9 %collective-permute-start.23 = (bf16[80,768]{1,0:T(8,128)(2,1)S(1)}, bf16[80,768]{1,0:T(8,128)(2,1)S(1)}, u32[]{:S(2)}, u32[]{:S(2)}) collective-permute-start(bf16[80,768]{1,0:T(8,128)(2,1)S(1)} %step.2.refs_4_), channel_id=1, source_target_pairs={{0,8},{1,9},{2,10},{3,11},{4,12},{5,13},{6,14},{7,15},{8,0},{9,1},... | collective-permute-start | bytes 368648 | tf_op jit(solution)/shard_map/ppermute | solution.py:47
  61.0 5.8 %collective-permute-start.24 = (bf16[64,768]{1,0:T(8,128)(2,1)S(1)}, bf16[64,768]{1,0:T(8,128)(2,1)S(1)}, u32[]{:S(2)}, u32[]{:S(2)}) collective-permute-start(bf16[64,768]{1,0:T(8,128)(2,1)S(1)} %step.3.refs_5_), channel_id=1, source_target_pairs={{0,8},{1,9},{2,10},{3,11},{4,12},{5,13},{6,14},{7,15},{8,0},{9,1},... | collective-permute-start | bytes 294920 | tf_op jit(solution)/shard_map/ppermute | solution.py:47
  71.3 7.8 %collective-permute-start.31 = (bf16[128,768]{1,0:T(8,128)(2,1)S(1)}, bf16[128,768]{1,0:T(8,128)(2,1)S(1)}, u32[]{:S(2)}, u32[]{:S(2)}) collective-permute-start(bf16[128,768]{1,0:T(8,128)(2,1)S(1)} %get-tuple-element.50), channel_id=1, source_target_pairs={{0,16},{1,17},{2,18},{3,19},{4,20},{5,21},{6,22},{7,23},{8,24},{9,... | collective-permute-start | bytes 589832 | tf_op jit(solution)/shard_map/ppermute | solution.py:47
  71.7 10.3 %collective-permute-start.32 = (bf16[128,768]{1,0:T(8,128)(2,1)S(1)}, bf16[128,768]{1,0:T(8,128)(2,1)S(1)}, u32[]{:S(2)}, u32[]{:S(2)}) collective-permute-start(bf16[128,768]{1,0:T(8,128)(2,1)S(1)} %get-tuple-element.51), channel_id=1, source_target_pairs={{0,1},{1,0},{2,3},{3,2},{4,5},{5,4},{6,7},{7,6},{8,9},{9,8},{10,11... | collective-permute-start | bytes 589832 | tf_op jit(solution)/shard_map/ppermute | solution.py:47
  73.5 10.1 %collective-permute-start.33 = (bf16[128,768]{1,0:T(8,128)(2,1)S(1)}, bf16[128,768]{1,0:T(8,128)(2,1)S(1)}, u32[]{:S(2)}, u32[]{:S(2)}) collective-permute-start(bf16[128,768]{1,0:T(8,128)(2,1)S(1)} %get-tuple-element.52), channel_id=1, source_target_pairs={{0,17},{1,16},{2,19},{3,18},{4,21},{5,20},{6,23},{7,22},{8,25},{9,... | collective-permute-start | bytes 589832 | tf_op jit(solution)/shard_map/ppermute | solution.py:47
  (16 other events, 93.9 us)
where the time goes:
time: 84.5 us; the launch traced here: 84.4 us
  waiting for transfers between devices  41.4 us (49%)
  starting transfers between devices  30.9 us (37%)
  Pallas kernels  9.98 us (12%)
  local copies, waits for them, and re-layouts  1.97 us (2%)
    ppermute x34, waiting for transfers between devices, send(): return lax.ppermute(array, AXES, pairs)  41.4 us
    ppermute x34, starting transfers between devices, send(): return lax.ppermute(array, AXES, pairs)  30.9 us
    pallas_call x11, Pallas kernels, call(): pl.pallas_call(kernel, out_shape=list(outs), in_specs=[pl.BlockSpec(memor...  9.98 us
    unnamed x12, local copies, waits for them, and re-layouts  1.96 us
  transfers between devices with their start and end apart: 34, of which 18 were waited for; matrix products, arithmetic and copies ran while one was open for 0% of the time, Pallas kernels for 8%

commit v1 on v0

--- a/solution.py
+++ b/solution.py
@@ -350,19 +350,17 @@
         for old, (part, keep) in zip(olds, chunks):
             for bit in bits[:-1]:
                 arrived = send(part, along(bit))
-                if stepped:
-                    keep = after(keep, *all_queries)
                 part, keep = fold(keep, arrived)
             updated = step(old, keep, send(part, along(bits[-1])))
             stepped.append(line_gather(updated, near_first=not stepped))
-        corner_query = send(after(query_normed, all_queries[0]), layer(1, 1))
+        corner_query = send(after(query_normed, *all_queries), layer(1, 1))
         blocks = [[chunk[k] for chunk in stepped] for k in range(n_far)]
         there = [[send(array, swap) for array in block] for block in blocks[:-1]]
         there.append([send(after(array, corner_query), swap) for array in blocks[-1]])
         blocks += there
 
-        outs = apply_rows(all_queries + [corner_query, query_normed], blocks, rows)
-        back = [send(part, layer(*o)) for part, o in zip(outs[:-1], ((1, 0), (0, 1), (1, 1)))]
+        outs = apply_rows([corner_query, *all_queries, query_normed], blocks, rows)
+        back = [send(part, layer(*o)) for part, o in zip(outs[:-1], ((1, 1), (1, 0), (0, 1)))]
         return call(total_kernel, [struct(queries.shape, BF)], outs[-1], mixed, *back, name="total")[0]
 
     in_specs = (

time: 84.5 us -> 84.6 us (level)
  transfers between devices with their start and end apart: 34 -> 34, of which waited for: 18 -> 16; matrix products, arithmetic and copies ran while one was open for 0% -> 0% of each run, Pallas kernels for 8% -> 8%
where the time goes in v1:
time: 84.6 us; the launch traced here: 84.4 us
  waiting for transfers between devices  41 us (48%)
  starting transfers between devices  31.3 us (37%)
  Pallas kernels  9.99 us (12%)
  local copies, waits for them, and re-layouts  1.97 us (2%)
    ppermute x34, waiting for transfers between devices, send(): return lax.ppermute(array, AXES, pairs)  41 us
    ppermute x34, starting transfers between devices, send(): return lax.ppermute(array, AXES, pairs)  31.3 us
    pallas_call x11, Pallas kernels, call(): pl.pallas_call(kernel, out_shape=list(outs), in_specs=[pl.BlockSpec(memor...  9.99 us
    unnamed x12, local copies, waits for them, and re-layouts  1.96 us
  transfers between devices with their start and end apart: 34, of which 16 were waited for; matrix products, arithmetic and copies ran while one was open for 0% of the time, Pallas kernels for 8%

profile of v1, /device:TPU:0, one launch (start us, length us, event | category | flops | bytes accessed | tf_op | source)
XLA Modules:
  0.0 84.4 jit_solution(786470075081411082)
XLA Ops:
  0.0 4.0 %collective-permute-start.2 = (bf16[3,48,768]{2,1,0:T(8,128)(2,1)}, bf16[3,48,768]{2,1,0:T(8,128)(2,1)S(1)}, u32[]{:S(2)}, u32[]{:S(2)}) collective-permute-start(bf16[3,48,768]{2,1,0:T(8,128)(2,1)} %refs_0_), channel_id=1, source_target_pairs={{0,4},{1,5},{2,6},{3,7},{4,0},{5,1},{6,2},{7,3},{8,12},{9,13},{10,... | collective-permute-start | bytes 663560 | tf_op jit(solution)/shard_map/ppermute | solution.py:47
  4.0 2.0 %prep.1 = (bf16[2,128,768]{2,1,0:T(8,128)(2,1)}, bf16[128,768]{1,0:T(8,128)(2,1)}) custom-call(bf16[128,768]{1,0:T(8,128)(2,1)} %key_ref.1, bf16[128,768]{1,0:T(8,128)(2,1)} %value_ref.1, bf16[128,768]{1,0:T(8,128)(2,1)} %query_ref.1, f32[1,128]{1,0:T(1,128)} %bitcast.4), custom_call_target="tpu_custom_call" | custom-call | bytes 1180160 | tf_op jit(solution)/shard_map/prep/pallas_call | solution.py:57
  6.1 1.6 %collective-permute-start.5 = (bf16[2,128,768]{2,1,0:T(8,128)(2,1)}, bf16[2,128,768]{2,1,0:T(8,128)(2,1)S(1)}, u32[]{:S(2)}, u32[]{:S(2)}) collective-permute-start(bf16[2,128,768]{2,1,0:T(8,128)(2,1)} %get-tuple-element.29.refs_1_), channel_id=1, source_target_pairs={{0,16},{1,17},{2,18},{3,19},{4,20},{5,21},{6,22},{7,23},{8,24},{9,... | collective-permute-start | bytes 1179656 | tf_op jit(solution)/shard_map/ppermute | solution.py:47
  7.6 1.5 %collective-permute-start.7 = (bf16[2,128,768]{2,1,0:T(8,128)(2,1)}, bf16[2,128,768]{2,1,0:T(8,128)(2,1)S(1)}, u32[]{:S(2)}, u32[]{:S(2)}) collective-permute-start(bf16[2,128,768]{2,1,0:T(8,128)(2,1)} %get-tuple-element.29.refs_1_), channel_id=1, source_target_pairs={{0,1},{1,0},{2,3},{3,2},{4,5},{5,4},{6,7},{7,6},{8,9},{9,8},{10,11... | collective-permute-start | bytes 1179656 | tf_op jit(solution)/shard_map/ppermute | solution.py:47
  9.6 1.6 %collective-permute-start.3 = (bf16[3,48,768]{2,1,0:T(8,128)(2,1)}, bf16[3,48,768]{2,1,0:T(8,128)(2,1)S(1)}, u32[]{:S(2)}, u32[]{:S(2)}) collective-permute-start(bf16[3,48,768]{2,1,0:T(8,128)(2,1)} %refs_0_), channel_id=1, source_target_pairs={{0,2},{1,3},{2,0},{3,1},{4,6},{5,7},{6,4},{7,5},{8,10},{9,11},{10,... | collective-permute-start | bytes 663560 | tf_op jit(solution)/shard_map/ppermute | solution.py:47
  11.2 3.3 %collective-permute-done.2.refs_8_.refs_4_ = bf16[3,48,768]{2,1,0:T(8,128)(2,1)S(1)} collective-permute-done((bf16[3,48,768]{2,1,0:T(8,128)(2,1)}, bf16[3,48,768]{2,1,0:T(8,128)(2,1)S(1)}, u32[]{:S(2)}, u32[]{:S(2)}) %collective-permute-start.2) | collective-permute-done | bytes 221216 | tf_op jit(solution)/shard_map/ppermute | solution.py:47
  18.4 8.2 %collective-permute-done.7.refs_2_ = bf16[2,128,768]{2,1,0:T(8,128)(2,1)S(1)} collective-permute-done((bf16[2,128,768]{2,1,0:T(8,128)(2,1)}, bf16[2,128,768]{2,1,0:T(8,128)(2,1)S(1)}, u32[]{:S(2)}, u32[]{:S(2)}) %collective-permute-start.7) | collective-permute-done | bytes 393248 | tf_op jit(solution)/shard_map/ppermute | solution.py:47
  28.9 2.2 %gradient_part.1.refs_6_ = f32[576,768]{1,0:T(8,128)S(1)} custom-call(bf16[2,128,768]{2,1,0:T(8,128)(2,1)S(1)} %get-tuple-element.33.refs_0_, bf16[2,128,768]{2,1,0:T(8,128)(2,1)S(1)} %collective-permute-done.6.refs_1_, bf16[2,128,768]{2,1,0:T(8,128)(2,1)S(1)} %collective-permute-done.7.refs_2_, bf16[2,128,768]{2,1,0:T(8,128)(2,1)S(1)} %collective-permute-done.5.refs_3_, ...), custom_call_target="tpu_custom_call" | custom-call | flops 1358954496 | bytes 5013504 | tf_op jit(solution)/shard_map/gradient_part/pallas_call | solution.py:57
  32.0 1.6 %collective-permute-start.13 = (bf16[2,80,768]{2,1,0:T(8,128)(2,1)S(1)}, bf16[2,80,768]{2,1,0:T(8,128)(2,1)S(1)}, u32[]{:S(2)}, u32[]{:S(2)}) collective-permute-start(bf16[2,80,768]{2,1,0:T(8,128)(2,1)S(1)} %get-tuple-element.34), channel_id=1, source_target_pairs={{0,2},{1,3},{2,0},{3,1},{4,6},{5,7},{6,4},{7,5},{8,10},{9,11},{10,... | collective-permute-start | bytes 737288 | tf_op jit(solution)/shard_map/ppermute | solution.py:47
  34.1 2.0 %collective-permute-start.11 = (bf16[128,768]{1,0:T(8,128)(2,1)S(1)}, bf16[128,768]{1,0:T(8,128)(2,1)S(1)}, u32[]{:S(2)}, u32[]{:S(2)}) collective-permute-start(bf16[128,768]{1,0:T(8,128)(2,1)S(1)} %copy-done.5), channel_id=1, source_target_pairs={{0,1},{1,0},{2,3},{3,2},{4,5},{5,4},{6,7},{7,6},{8,9},{9,8},{10,11... | collective-permute-start | bytes 589832 | tf_op jit(solution)/shard_map/ppermute | solution.py:47
  36.2 4.7 %collective-permute-done.13.arrived_ref = bf16[2,80,768]{2,1,0:T(8,128)(2,1)S(1)} collective-permute-done((bf16[2,80,768]{2,1,0:T(8,128)(2,1)S(1)}, bf16[2,80,768]{2,1,0:T(8,128)(2,1)S(1)}, u32[]{:S(2)}, u32[]{:S(2)}) %collective-permute-start.13) | collective-permute-done | bytes 245792 | tf_op jit(solution)/shard_map/ppermute | solution.py:47
  41.4 4.1 %collective-permute-done.15.arrived_ref = bf16[2,64,768]{2,1,0:T(8,128)(2,1)S(1)} collective-permute-done((bf16[2,64,768]{2,1,0:T(8,128)(2,1)S(1)}, bf16[2,64,768]{2,1,0:T(8,128)(2,1)S(1)}, u32[]{:S(2)}, u32[]{:S(2)}) %collective-permute-start.15) | collective-permute-done | bytes 196640 | tf_op jit(solution)/shard_map/ppermute | solution.py:47
  45.6 1.5 %collective-permute-start.12 = (bf16[128,768]{1,0:T(8,128)(2,1)S(1)}, bf16[128,768]{1,0:T(8,128)(2,1)S(1)}, u32[]{:S(2)}, u32[]{:S(2)}) collective-permute-start(bf16[128,768]{1,0:T(8,128)(2,1)S(1)} %copy-done.5), channel_id=1, source_target_pairs={{0,17},{1,16},{2,19},{3,18},{4,21},{5,20},{6,23},{7,22},{8,25},{9,... | collective-permute-start | bytes 589832 | tf_op jit(solution)/shard_map/ppermute | solution.py:47
  47.1 2.4 %collective-permute-done.14.arrived_ref = bf16[1,80,768]{2,1,0:T(8,128)(2,1)S(1)} collective-permute-done((bf16[1,80,768]{2,1,0:T(8,128)(2,1)S(1)}, bf16[1,80,768]{2,1,0:T(8,128)(2,1)S(1)}, u32[]{:S(2)}, u32[]{:S(2)}) %collective-permute-start.14) | collective-permute-done | bytes 122912 | tf_op jit(solution)/shard_map/ppermute | solution.py:47
  50.4 3.6 %collective-permute-start.19 = (bf16[80,768]{1,0:T(8,128)(2,1)S(1)}, bf16[80,768]{1,0:T(8,128)(2,1)S(1)}, u32[]{:S(2)}, u32[]{:S(2)}) collective-permute-start(bf16[80,768]{1,0:T(8,128)(2,1)S(1)} %step.2.refs_4_), channel_id=1, source_target_pairs={{0,4},{1,5},{2,6},{3,7},{4,0},{5,1},{6,2},{7,3},{8,12},{9,13},{10,... | collective-permute-start | bytes 368648 | tf_op jit(solution)/shard_map/ppermute | solution.py:47
  54.4 3.6 %collective-permute-start.18 = (bf16[64,768]{1,0:T(8,128)(2,1)S(1)}, bf16[64,768]{1,0:T(8,128)(2,1)S(1)}, u32[]{:S(2)}, u32[]{:S(2)}) collective-permute-start(bf16[64,768]{1,0:T(8,128)(2,1)S(1)} %step.3.refs_5_), channel_id=1, source_target_pairs={{0,2},{1,3},{2,0},{3,1},{4,6},{5,7},{6,4},{7,5},{8,10},{9,11},{10,... | collective-permute-start | bytes 294920 | tf_op jit(solution)/shard_map/ppermute | solution.py:47
  57.9 3.1 %collective-permute-done.19.refs_8_ = bf16[80,768]{1,0:T(8,128)(2,1)S(1)} collective-permute-done((bf16[80,768]{1,0:T(8,128)(2,1)S(1)}, bf16[80,768]{1,0:T(8,128)(2,1)S(1)}, u32[]{:S(2)}, u32[]{:S(2)}) %collective-permute-start.19) | collective-permute-done | bytes 122912 | tf_op jit(solution)/shard_map/ppermute | solution.py:47
  63.6 3.3 %collective-permute-done.21.refs_10_ = bf16[80,768]{1,0:T(8,128)(2,1)S(1)} collective-permute-done((bf16[80,768]{1,0:T(8,128)(2,1)S(1)}, bf16[80,768]{1,0:T(8,128)(2,1)S(1)}, u32[]{:S(2)}, u32[]{:S(2)}) %collective-permute-start.21) | collective-permute-done | bytes 122912 | tf_op jit(solution)/shard_map/ppermute | solution.py:47
  69.8 1.5 %apply.1 = (bf16[128,768]{1,0:T(8,128)(2,1)S(1)}, bf16[128,768]{1,0:T(8,128)(2,1)S(1)}, bf16[128,768]{1,0:T(8,128)(2,1)S(1)}, f32[128,768]{1,0:T(8,128)S(1)}) custom-call(bf16[128,768]{1,0:T(8,128)(2,1)S(1)} %collective-permute-done.12.refs_0_, bf16[128,768]{1,0:T(8,128)(2,1)S(1)} %collective-permute-done.10.refs_1_, ...), custom_call_target="tpu_custom_call" | custom-call | flops 905969664 | bytes 3538944 | tf_op jit(solution)/shard_map/apply/pallas_call | solution.py:57
  71.3 1.7 %collective-permute-start.31 = (bf16[128,768]{1,0:T(8,128)(2,1)S(1)}, bf16[128,768]{1,0:T(8,128)(2,1)S(1)}, u32[]{:S(2)}, u32[]{:S(2)}) collective-permute-start(bf16[128,768]{1,0:T(8,128)(2,1)S(1)} %get-tuple-element.48), channel_id=1, source_target_pairs={{0,17},{1,16},{2,19},{3,18},{4,21},{5,20},{6,23},{7,22},{8,25},{9,... | collective-permute-start | bytes 589832 | tf_op jit(solution)/shard_map/ppermute | solution.py:47
  72.9 1.5 %collective-permute-start.32 = (bf16[128,768]{1,0:T(8,128)(2,1)S(1)}, bf16[128,768]{1,0:T(8,128)(2,1)S(1)}, u32[]{:S(2)}, u32[]{:S(2)}) collective-permute-start(bf16[128,768]{1,0:T(8,128)(2,1)S(1)} %get-tuple-element.49), channel_id=1, source_target_pairs={{0,16},{1,17},{2,18},{3,19},{4,20},{5,21},{6,22},{7,23},{8,24},{9,... | collective-permute-start | bytes 589832 | tf_op jit(solution)/shard_map/ppermute | solution.py:47
  74.8 2.1 %attention.1.refs_1_ = f32[128,768]{1,0:T(8,128)S(1)} custom-call(bf16[128,768]{1,0:T(8,128)(2,1)S(1)} %copy-done.2, bf16[128,768]{1,0:T(8,128)(2,1)S(1)} %copy-done, bf16[128,768]{1,0:T(8,128)(2,1)S(1)} %copy-done.1), custom_call_target="tpu_custom_call" | custom-call | flops 50331648 | bytes 983040 | tf_op jit(solution)/shard_map/attention/pallas_call | solution.py:57
  76.9 3.1 %collective-permute-done.31.refs_2_ = bf16[128,768]{1,0:T(8,128)(2,1)S(1)} collective-permute-done((bf16[128,768]{1,0:T(8,128)(2,1)S(1)}, bf16[128,768]{1,0:T(8,128)(2,1)S(1)}, u32[]{:S(2)}, u32[]{:S(2)}) %collective-permute-start.31) | collective-permute-done | bytes 196640 | tf_op jit(solution)/shard_map/ppermute | solution.py:47
  80.0 3.6 %collective-permute-done.32.refs_3_ = bf16[128,768]{1,0:T(8,128)(2,1)S(1)} collective-permute-done((bf16[128,768]{1,0:T(8,128)(2,1)S(1)}, bf16[128,768]{1,0:T(8,128)(2,1)S(1)}, u32[]{:S(2)}, u32[]{:S(2)}) %collective-permute-start.32) | collective-permute-done | bytes 196640 | tf_op jit(solution)/shard_map/ppermute | solution.py:47
  (69 shorter events, 16.4 us)
Async XLA Ops:
  0.0 14.5 %collective-permute-start.2 = (bf16[3,48,768]{2,1,0:T(8,128)(2,1)}, bf16[3,48,768]{2,1,0:T(8,128)(2,1)S(1)}, u32[]{:S(2)}, u32[]{:S(2)}) collective-permute-start(bf16[3,48,768]{2,1,0:T(8,128)(2,1)} %refs_0_), channel_id=1, source_target_pairs={{0,4},{1,5},{2,6},{3,7},{4,0},{5,1},{6,2},{7,3},{8,12},{9,13},{10,... | collective-permute-start | bytes 663560 | tf_op jit(solution)/shard_map/ppermute | solution.py:47
  6.1 12.3 %collective-permute-start.5 = (bf16[2,128,768]{2,1,0:T(8,128)(2,1)}, bf16[2,128,768]{2,1,0:T(8,128)(2,1)S(1)}, u32[]{:S(2)}, u32[]{:S(2)}) collective-permute-start(bf16[2,128,768]{2,1,0:T(8,128)(2,1)} %get-tuple-element.29.refs_1_), channel_id=1, source_target_pairs={{0,16},{1,17},{2,18},{3,19},{4,20},{5,21},{6,22},{7,23},{8,24},{9,... | collective-permute-start | bytes 1179656 | tf_op jit(solution)/shard_map/ppermute | solution.py:47
  7.6 18.9 %collective-permute-start.7 = (bf16[2,128,768]{2,1,0:T(8,128)(2,1)}, bf16[2,128,768]{2,1,0:T(8,128)(2,1)S(1)}, u32[]{:S(2)}, u32[]{:S(2)}) collective-permute-start(bf16[2,128,768]{2,1,0:T(8,128)(2,1)} %get-tuple-element.29.refs_1_), channel_id=1, source_target_pairs={{0,1},{1,0},{2,3},{3,2},{4,5},{5,4},{6,7},{7,6},{8,9},{9,8},{10,11... | collective-permute-start | bytes 1179656 | tf_op jit(solution)/shard_map/ppermute | solution.py:47
  9.2 17.9 %collective-permute-start = (bf16[2,128,768]{2,1,0:T(8,128)(2,1)}, bf16[2,128,768]{2,1,0:T(8,128)(2,1)S(1)}, u32[]{:S(2)}, u32[]{:S(2)}) collective-permute-start(bf16[2,128,768]{2,1,0:T(8,128)(2,1)} %get-tuple-element.29.refs_1_), channel_id=1, source_target_pairs={{0,17},{1,16},{2,19},{3,18},{4,21},{5,20},{6,23},{7,22},{8,25},{9,... | collective-permute-start | bytes 1179656 | tf_op jit(solution)/shard_map/ppermute | solution.py:47
  9.6 16.9 %collective-permute-start.3 = (bf16[3,48,768]{2,1,0:T(8,128)(2,1)}, bf16[3,48,768]{2,1,0:T(8,128)(2,1)S(1)}, u32[]{:S(2)}, u32[]{:S(2)}) collective-permute-start(bf16[3,48,768]{2,1,0:T(8,128)(2,1)} %refs_0_), channel_id=1, source_target_pairs={{0,2},{1,3},{2,0},{3,1},{4,6},{5,7},{6,4},{7,5},{8,10},{9,11},{10,... | collective-permute-start | bytes 663560 | tf_op jit(solution)/shard_map/ppermute | solution.py:47
  14.5 12.1 %collective-permute-start.4 = (bf16[3,48,768]{2,1,0:T(8,128)(2,1)S(1)}, bf16[3,48,768]{2,1,0:T(8,128)(2,1)S(1)}, u32[]{:S(2)}, u32[]{:S(2)}) collective-permute-start(bf16[3,48,768]{2,1,0:T(8,128)(2,1)S(1)} %collective-permute-done.2.refs_8_.refs_4_), channel_id=1, source_target_pairs={{0,2},{1,3},{2,0},{3,1},{4,6},{5,7},{6,4},{7,5},{8,10},{9,11},{10,... | collective-permute-start | bytes 663560 | tf_op jit(solution)/shard_map/ppermute | solution.py:47
  18.4 8.8 %collective-permute-start.9 = (bf16[2,128,768]{2,1,0:T(8,128)(2,1)S(1)}, bf16[2,128,768]{2,1,0:T(8,128)(2,1)S(1)}, u32[]{:S(2)}, u32[]{:S(2)}) collective-permute-start(bf16[2,128,768]{2,1,0:T(8,128)(2,1)S(1)} %collective-permute-done.5.refs_3_), channel_id=1, source_target_pairs={{0,8},{1,9},{2,10},{3,11},{4,12},{5,13},{6,14},{7,15},{8,0},{9,1},... | collective-permute-start | bytes 1179656 | tf_op jit(solution)/shard_map/ppermute | solution.py:47
  32.0 8.9 %collective-permute-start.13 = (bf16[2,80,768]{2,1,0:T(8,128)(2,1)S(1)}, bf16[2,80,768]{2,1,0:T(8,128)(2,1)S(1)}, u32[]{:S(2)}, u32[]{:S(2)}) collective-permute-start(bf16[2,80,768]{2,1,0:T(8,128)(2,1)S(1)} %get-tuple-element.34), channel_id=1, source_target_pairs={{0,2},{1,3},{2,0},{3,1},{4,6},{5,7},{6,4},{7,5},{8,10},{9,11},{10,... | collective-permute-start | bytes 737288 | tf_op jit(solution)/shard_map/ppermute | solution.py:47
  33.7 11.8 %collective-permute-start.15 = (bf16[2,64,768]{2,1,0:T(8,128)(2,1)S(1)}, bf16[2,64,768]{2,1,0:T(8,128)(2,1)S(1)}, u32[]{:S(2)}, u32[]{:S(2)}) collective-permute-start(bf16[2,64,768]{2,1,0:T(8,128)(2,1)S(1)} %get-tuple-element.41), channel_id=1, source_target_pairs={{0,2},{1,3},{2,0},{3,1},{4,6},{5,7},{6,4},{7,5},{8,10},{9,11},{10,... | collective-permute-start | bytes 589832 | tf_op jit(solution)/shard_map/ppermute | solution.py:47
  34.1 11.4 %collective-permute-start.10 = (bf16[128,768]{1,0:T(8,128)(2,1)S(1)}, bf16[128,768]{1,0:T(8,128)(2,1)S(1)}, u32[]{:S(2)}, u32[]{:S(2)}) collective-permute-start(bf16[128,768]{1,0:T(8,128)(2,1)S(1)} %copy-done.5), channel_id=1, source_target_pairs={{0,16},{1,17},{2,18},{3,19},{4,20},{5,21},{6,22},{7,23},{8,24},{9,... | collective-permute-start | bytes 589832 | tf_op jit(solution)/shard_map/ppermute | solution.py:47
  34.1 11.4 %collective-permute-start.11 = (bf16[128,768]{1,0:T(8,128)(2,1)S(1)}, bf16[128,768]{1,0:T(8,128)(2,1)S(1)}, u32[]{:S(2)}, u32[]{:S(2)}) collective-permute-start(bf16[128,768]{1,0:T(8,128)(2,1)S(1)} %copy-done.5), channel_id=1, source_target_pairs={{0,1},{1,0},{2,3},{3,2},{4,5},{5,4},{6,7},{7,6},{8,9},{9,8},{10,11... | collective-permute-start | bytes 589832 | tf_op jit(solution)/shard_map/ppermute | solution.py:47
  41.0 8.5 %collective-permute-start.14 = (bf16[1,80,768]{2,1,0:T(8,128)(2,1)S(1)}, bf16[1,80,768]{2,1,0:T(8,128)(2,1)S(1)}, u32[]{:S(2)}, u32[]{:S(2)}) collective-permute-start(bf16[1,80,768]{2,1,0:T(8,128)(2,1)S(1)} %get-tuple-element.39), channel_id=1, source_target_pairs={{0,4},{1,5},{2,6},{3,7},{4,0},{5,1},{6,2},{7,3},{8,12},{9,13},{10,... | collective-permute-start | bytes 368648 | tf_op jit(solution)/shard_map/ppermute | solution.py:47
  45.5 8.6 %collective-permute-start.16 = (bf16[1,64,768]{2,1,0:T(8,128)(2,1)S(1)}, bf16[1,64,768]{2,1,0:T(8,128)(2,1)S(1)}, u32[]{:S(2)}, u32[]{:S(2)}) collective-permute-start(bf16[1,64,768]{2,1,0:T(8,128)(2,1)S(1)} %get-tuple-element.43), channel_id=1, source_target_pairs={{0,4},{1,5},{2,6},{3,7},{4,0},{5,1},{6,2},{7,3},{8,12},{9,13},{10,... | collective-permute-start | bytes 294920 | tf_op jit(solution)/shard_map/ppermute | solution.py:47
  45.6 15.5 %collective-permute-start.12 = (bf16[128,768]{1,0:T(8,128)(2,1)S(1)}, bf16[128,768]{1,0:T(8,128)(2,1)S(1)}, u32[]{:S(2)}, u32[]{:S(2)}) collective-permute-start(bf16[128,768]{1,0:T(8,128)(2,1)S(1)} %copy-done.5), channel_id=1, source_target_pairs={{0,17},{1,16},{2,19},{3,18},{4,21},{5,20},{6,23},{7,22},{8,25},{9,... | collective-permute-start | bytes 589832 | tf_op jit(solution)/shard_map/ppermute | solution.py:47
  49.7 8.3 %collective-permute-start.17 = (bf16[80,768]{1,0:T(8,128)(2,1)S(1)}, bf16[80,768]{1,0:T(8,128)(2,1)S(1)}, u32[]{:S(2)}, u32[]{:S(2)}) collective-permute-start(bf16[80,768]{1,0:T(8,128)(2,1)S(1)} %step.2.refs_4_), channel_id=1, source_target_pairs={{0,2},{1,3},{2,0},{3,1},{4,6},{5,7},{6,4},{7,5},{8,10},{9,11},{10,... | collective-permute-start | bytes 368648 | tf_op jit(solution)/shard_map/ppermute | solution.py:47
  50.4 10.6 %collective-permute-start.19 = (bf16[80,768]{1,0:T(8,128)(2,1)S(1)}, bf16[80,768]{1,0:T(8,128)(2,1)S(1)}, u32[]{:S(2)}, u32[]{:S(2)}) collective-permute-start(bf16[80,768]{1,0:T(8,128)(2,1)S(1)} %step.2.refs_4_), channel_id=1, source_target_pairs={{0,4},{1,5},{2,6},{3,7},{4,0},{5,1},{6,2},{7,3},{8,12},{9,13},{10,... | collective-permute-start | bytes 368648 | tf_op jit(solution)/shard_map/ppermute | solution.py:47
  54.3 7.9 %collective-permute-start.20 = (bf16[64,768]{1,0:T(8,128)(2,1)S(1)}, bf16[64,768]{1,0:T(8,128)(2,1)S(1)}, u32[]{:S(2)}, u32[]{:S(2)}) collective-permute-start(bf16[64,768]{1,0:T(8,128)(2,1)S(1)} %step.3.refs_5_), channel_id=1, source_target_pairs={{0,4},{1,5},{2,6},{3,7},{4,0},{5,1},{6,2},{7,3},{8,12},{9,13},{10,... | collective-permute-start | bytes 294920 | tf_op jit(solution)/shard_map/ppermute | solution.py:47
  54.4 9.2 %collective-permute-start.18 = (bf16[64,768]{1,0:T(8,128)(2,1)S(1)}, bf16[64,768]{1,0:T(8,128)(2,1)S(1)}, u32[]{:S(2)}, u32[]{:S(2)}) collective-permute-start(bf16[64,768]{1,0:T(8,128)(2,1)S(1)} %step.3.refs_5_), channel_id=1, source_target_pairs={{0,2},{1,3},{2,0},{3,1},{4,6},{5,7},{6,4},{7,5},{8,10},{9,11},{10,... | collective-permute-start | bytes 294920 | tf_op jit(solution)/shard_map/ppermute | solution.py:47
  61.0 5.8 %collective-permute-start.21 = (bf16[80,768]{1,0:T(8,128)(2,1)S(1)}, bf16[80,768]{1,0:T(8,128)(2,1)S(1)}, u32[]{:S(2)}, u32[]{:S(2)}) collective-permute-start(bf16[80,768]{1,0:T(8,128)(2,1)S(1)} %collective-permute-done.19.refs_8_), channel_id=1, source_target_pairs={{0,2},{1,3},{2,0},{3,1},{4,6},{5,7},{6,4},{7,5},{8,10},{9,11},{10,... | collective-permute-start | bytes 368648 | tf_op jit(solution)/shard_map/ppermute | solution.py:47
  61.0 6.9 %collective-permute-start.23 = (bf16[80,768]{1,0:T(8,128)(2,1)S(1)}, bf16[80,768]{1,0:T(8,128)(2,1)S(1)}, u32[]{:S(2)}, u32[]{:S(2)}) collective-permute-start(bf16[80,768]{1,0:T(8,128)(2,1)S(1)} %step.2.refs_4_), channel_id=1, source_target_pairs={{0,8},{1,9},{2,10},{3,11},{4,12},{5,13},{6,14},{7,15},{8,0},{9,1},... | collective-permute-start | bytes 368648 | tf_op jit(solution)/shard_map/ppermute | solution.py:47
  61.0 5.8 %collective-permute-start.24 = (bf16[64,768]{1,0:T(8,128)(2,1)S(1)}, bf16[64,768]{1,0:T(8,128)(2,1)S(1)}, u32[]{:S(2)}, u32[]{:S(2)}) collective-permute-start(bf16[64,768]{1,0:T(8,128)(2,1)S(1)} %step.3.refs_5_), channel_id=1, source_target_pairs={{0,8},{1,9},{2,10},{3,11},{4,12},{5,13},{6,14},{7,15},{8,0},{9,1},... | collective-permute-start | bytes 294920 | tf_op jit(solution)/shard_map/ppermute | solution.py:47
  71.3 8.7 %collective-permute-start.31 = (bf16[128,768]{1,0:T(8,128)(2,1)S(1)}, bf16[128,768]{1,0:T(8,128)(2,1)S(1)}, u32[]{:S(2)}, u32[]{:S(2)}) collective-permute-start(bf16[128,768]{1,0:T(8,128)(2,1)S(1)} %get-tuple-element.48), channel_id=1, source_target_pairs={{0,17},{1,16},{2,19},{3,18},{4,21},{5,20},{6,23},{7,22},{8,25},{9,... | collective-permute-start | bytes 589832 | tf_op jit(solution)/shard_map/ppermute | solution.py:47
  72.9 10.7 %collective-permute-start.32 = (bf16[128,768]{1,0:T(8,128)(2,1)S(1)}, bf16[128,768]{1,0:T(8,128)(2,1)S(1)}, u32[]{:S(2)}, u32[]{:S(2)}) collective-permute-start(bf16[128,768]{1,0:T(8,128)(2,1)S(1)} %get-tuple-element.49), channel_id=1, source_target_pairs={{0,16},{1,17},{2,18},{3,19},{4,20},{5,21},{6,22},{7,23},{8,24},{9,... | collective-permute-start | bytes 589832 | tf_op jit(solution)/shard_map/ppermute | solution.py:47
  74.4 9.2 %collective-permute-start.33 = (bf16[128,768]{1,0:T(8,128)(2,1)S(1)}, bf16[128,768]{1,0:T(8,128)(2,1)S(1)}, u32[]{:S(2)}, u32[]{:S(2)}) collective-permute-start(bf16[128,768]{1,0:T(8,128)(2,1)S(1)} %get-tuple-element.50), channel_id=1, source_target_pairs={{0,1},{1,0},{2,3},{3,2},{4,5},{5,4},{6,7},{7,6},{8,9},{9,8},{10,11... | collective-permute-start | bytes 589832 | tf_op jit(solution)/shard_map/ppermute | solution.py:47
  (16 other events, 95.6 us)

commit v2 on v1

--- a/solution.py
+++ b/solution.py
@@ -83,10 +83,10 @@
     return matrix / jnp.sqrt(jnp.mean(matrix * matrix, axis=-1, keepdims=True) + epsilon)
 
 
-def prep_kernel(key_hbm, value_hbm, query_hbm, rate_hbm, pair_ref, query_out, key_ref, value_ref, query_ref, rate_ref, sems):
+def prep_kernel(key_hbm, value_hbm, rate_hbm, pair_ref, key_ref, value_ref, rate_ref, sems):
     count = key_ref.shape[0]
-    sources = (key_hbm, rate_hbm, value_hbm, query_hbm)
-    targets = (key_ref, rate_ref, value_ref, query_ref)
+    sources = (key_hbm, rate_hbm, value_hbm)
+    targets = (key_ref, rate_ref, value_ref)
     copies = [pltpu.make_async_copy(a, b, sems.at[i]) for i, (a, b) in enumerate(zip(sources, targets))]
     for copy in copies:
         copy.start()
@@ -99,21 +99,19 @@
     col = lax.broadcasted_iota(jnp.int32, (count, count), 1)
     rate = jnp.sum(jnp.where(row == col, spread, 0.0), axis=1, keepdims=True)
     pair_ref[1] = (-(rate * value_ref[...].astype(F32))).astype(BF)
-    copies[3].wait()
-    query_out[...] = rms(query_ref[...].astype(F32)).astype(BF)
-
-
-def prep(key_tokens, value_tokens, queries, token_rate):
+
+
+def prep(key_tokens, value_tokens, token_rate):
     count = key_tokens.shape[0]
     return call(
         prep_kernel,
-        [struct((2, count, D), BF), struct((count, D), BF)],
-        key_tokens, value_tokens, queries, token_rate.reshape(1, count),
-        scratch=[pltpu.VMEM((count, D), BF)] * 3 + [pltpu.VMEM((1, count), F32), pltpu.SemaphoreType.DMA((4,))],
-        in_hbm=(0, 1, 2, 3),
+        [struct((2, count, D), BF)],
+        key_tokens, value_tokens, token_rate.reshape(1, count),
+        scratch=[pltpu.VMEM((count, D), BF)] * 2 + [pltpu.VMEM((1, count), F32), pltpu.SemaphoreType.DMA((3,))],
+        in_hbm=(0, 1, 2),
         limit=62 * 1024 * 1024,
         name="prep",
-    )
+    )[0]
 
 
 def cut(rows):
@@ -131,12 +129,13 @@
     return found
 
 
-def stage(*arrays):
-    def kernel(*refs):
-        for source, target in zip(refs[:len(arrays)], refs[len(arrays):]):
-            target[...] = source[...]
-
-    return call(kernel, [struct(a.shape, a.dtype) for a in arrays], *arrays, name="stage")
+def stage(weights, pair, queries):
+    def kernel(weights_ref, pair_ref, query_ref, weights_out, pair_out, query_out):
+        weights_out[...] = weights_ref[...]
+        pair_out[...] = pair_ref[...]
+        query_out[...] = rms(query_ref[...].astype(F32)).astype(BF)
+
+    return call(kernel, [struct(a.shape, BF) for a in (weights, pair, queries)], weights, pair, queries, name="stage")
 
 
 def gradient(tokens, blocks, before=None):
@@ -266,7 +265,7 @@
     )[0]
 
 
-def apply_rows(queries, blocks, rows):
+def apply_rows(queries, blocks, rows, last):
     count = queries[0].shape[0]
     number = len(blocks)
     aligned = rows % 16 == 0
@@ -300,7 +299,7 @@
         for i, out in enumerate(out_refs):
             out[...] = result[i * count:(i + 1) * count].astype(out.dtype)
 
-    outs = [struct((count, D), BF) for _ in queries[:-1]] + [struct((count, D), F32)]
+    outs = [struct((count, D), BF) for _ in queries[:-1]] + [struct((count, D), last)]
     return call(
         kernel, outs, *queries, *chunks,
         flops=6 * count * len(queries) * units * D,
@@ -330,10 +329,10 @@
 
     def body(key_tokens, value_tokens, queries, token_rate, fast_weights):
         rows = fast_weights.shape[1]
-        pair, query_normed = prep(key_tokens, value_tokens, queries, token_rate)
+        pair = prep(key_tokens, value_tokens, token_rate)
         at_x, at_y, corner = [send(pair, layer(*o)) for o in ((1, 0), (0, 1), (1, 1))]
         line = line_gather(fast_weights)
-        own_weights, own_pair = stage(after(fast_weights, line[bits[-1]]), pair)
+        own_weights, own_pair, query_normed = stage(after(fast_weights, line[bits[-1]]), pair, queries)
         own_there = send(after(own_pair, at_x, *[line[k] for k in range(1, n_far)]), swap)
         blocks = [own_weights] + [line[k] for k in range(1, n_far)]
         tokens = [own_pair, own_there, at_y, at_x, send(at_y, swap), send(at_x, swap)]
@@ -359,7 +358,8 @@
         there.append([send(after(array, corner_query), swap) for array in blocks[-1]])
         blocks += there
 
-        outs = apply_rows([corner_query, *all_queries, query_normed], blocks, rows)
+        outs = apply_rows([corner_query, all_queries[0]], blocks, rows, BF)
+        outs += apply_rows([all_queries[1], query_normed], blocks, rows, F32)
         back = [send(part, layer(*o)) for part, o in zip(outs[:-1], ((1, 1), (1, 0), (0, 1)))]
         return call(total_kernel, [struct(queries.shape, BF)], outs[-1], mixed, *back, name="total")[0]
 

time: 84.6 us -> 83.9 us (level)
  waiting for transfers between devices: 41 us -> 39.5 us
  local copies, waits for them, and re-layouts: 1.97 us -> 2.89 us
    ppermute x34, waiting for transfers between devices: 41 us -> 39.5 us  [send(): return lax.ppermute(array, AXES, pairs)]
    unnamed x12, local copies, waits for them, and re-layouts: 1.96 us -> 2.88 us
    pallas_call x11 -> x12, Pallas kernels: 9.99 us -> 10.3 us  [call(): pl.pallas_call(kernel, out_shape=list(outs), in_specs=[pl.BlockSpec(memor...]
  transfers between devices with their start and end apart: 34 -> 34, of which waited for: 16 -> 17; matrix products, arithmetic and copies ran while one was open for 0% -> 0% of each run, Pallas kernels for 8% -> 9%
where the time goes in v2:
time: 83.9 us; the launch traced here: 83.7 us
  waiting for transfers between devices  39.5 us (47%)
  starting transfers between devices  30.8 us (37%)
  Pallas kernels  10.3 us (12%)
  local copies, waits for them, and re-layouts  2.89 us (3%)
    ppermute x34, waiting for transfers between devices, send(): return lax.ppermute(array, AXES, pairs)  39.5 us
    ppermute x34, starting transfers between devices, send(): return lax.ppermute(array, AXES, pairs)  30.8 us
    pallas_call x12, Pallas kernels, call(): pl.pallas_call(kernel, out_shape=list(outs), in_specs=[pl.BlockSpec(memor...  10.3 us
    unnamed x12, local copies, waits for them, and re-layouts  2.88 us
  transfers between devices with their start and end apart: 34, of which 17 were waited for; matrix products, arithmetic and copies ran while one was open for 0% of the time, Pallas kernels for 9%

profile of v2, /device:TPU:0, one launch (start us, length us, event | category | flops | bytes accessed | tf_op | source)
XLA Modules:
  0.0 83.7 jit_solution(2310954740888534291)
XLA Ops:
  0.0 4.0 %collective-permute-start = (bf16[3,48,768]{2,1,0:T(8,128)(2,1)}, bf16[3,48,768]{2,1,0:T(8,128)(2,1)S(1)}, u32[]{:S(2)}, u32[]{:S(2)}) collective-permute-start(bf16[3,48,768]{2,1,0:T(8,128)(2,1)} %weights_ref), channel_id=1, source_target_pairs={{0,4},{1,5},{2,6},{3,7},{4,0},{5,1},{6,2},{7,3},{8,12},{9,13},{10,... | collective-permute-start | bytes 663560 | tf_op jit(solution)/shard_map/ppermute | solution.py:47
  4.0 1.9 %prep.1.pair_ref = bf16[2,128,768]{2,1,0:T(8,128)(2,1)} custom-call(bf16[128,768]{1,0:T(8,128)(2,1)} %key_ref.1, bf16[128,768]{1,0:T(8,128)(2,1)} %value_ref.1, f32[1,128]{1,0:T(1,128)} %bitcast.4), custom_call_target="tpu_custom_call" | custom-call | bytes 786944 | tf_op jit(solution)/shard_map/prep/pallas_call | solution.py:57
  6.0 1.6 %collective-permute-start.5 = (bf16[2,128,768]{2,1,0:T(8,128)(2,1)}, bf16[2,128,768]{2,1,0:T(8,128)(2,1)S(1)}, u32[]{:S(2)}, u32[]{:S(2)}) collective-permute-start(bf16[2,128,768]{2,1,0:T(8,128)(2,1)} %prep.1.pair_ref), channel_id=1, source_target_pairs={{0,16},{1,17},{2,18},{3,19},{4,20},{5,21},{6,22},{7,23},{8,24},{9,... | collective-permute-start | bytes 1179656 | tf_op jit(solution)/shard_map/ppermute | solution.py:47
  7.5 1.5 %collective-permute-start.7 = (bf16[2,128,768]{2,1,0:T(8,128)(2,1)}, bf16[2,128,768]{2,1,0:T(8,128)(2,1)S(1)}, u32[]{:S(2)}, u32[]{:S(2)}) collective-permute-start(bf16[2,128,768]{2,1,0:T(8,128)(2,1)} %prep.1.pair_ref), channel_id=1, source_target_pairs={{0,1},{1,0},{2,3},{3,2},{4,5},{5,4},{6,7},{7,6},{8,9},{9,8},{10,11... | collective-permute-start | bytes 1179656 | tf_op jit(solution)/shard_map/ppermute | solution.py:47
  9.5 1.6 %collective-permute-start.3 = (bf16[3,48,768]{2,1,0:T(8,128)(2,1)}, bf16[3,48,768]{2,1,0:T(8,128)(2,1)S(1)}, u32[]{:S(2)}, u32[]{:S(2)}) collective-permute-start(bf16[3,48,768]{2,1,0:T(8,128)(2,1)} %weights_ref), channel_id=1, source_target_pairs={{0,2},{1,3},{2,0},{3,1},{4,6},{5,7},{6,4},{7,5},{8,10},{9,11},{10,... | collective-permute-start | bytes 663560 | tf_op jit(solution)/shard_map/ppermute | solution.py:47
  11.1 3.4 %collective-permute-done.refs_8_.refs_4_ = bf16[3,48,768]{2,1,0:T(8,128)(2,1)S(1)} collective-permute-done((bf16[3,48,768]{2,1,0:T(8,128)(2,1)}, bf16[3,48,768]{2,1,0:T(8,128)(2,1)S(1)}, u32[]{:S(2)}, u32[]{:S(2)}) %collective-permute-start) | collective-permute-done | bytes 221216 | tf_op jit(solution)/shard_map/ppermute | solution.py:47
  18.4 8.1 %collective-permute-done.7.refs_2_ = bf16[2,128,768]{2,1,0:T(8,128)(2,1)S(1)} collective-permute-done((bf16[2,128,768]{2,1,0:T(8,128)(2,1)}, bf16[2,128,768]{2,1,0:T(8,128)(2,1)S(1)}, u32[]{:S(2)}, u32[]{:S(2)}) %collective-permute-start.7) | collective-permute-done | bytes 393248 | tf_op jit(solution)/shard_map/ppermute | solution.py:47
  27.1 1.1 %collective-permute-done.8.refs_4_ = bf16[2,128,768]{2,1,0:T(8,128)(2,1)S(1)} collective-permute-done((bf16[2,128,768]{2,1,0:T(8,128)(2,1)S(1)}, bf16[2,128,768]{2,1,0:T(8,128)(2,1)S(1)}, u32[]{:S(2)}, u32[]{:S(2)}) %collective-permute-start.8) | collective-permute-done | bytes 393248 | tf_op jit(solution)/shard_map/ppermute | solution.py:47
  28.8 2.2 %gradient_part.1.refs_6_ = f32[576,768]{1,0:T(8,128)S(1)} custom-call(bf16[2,128,768]{2,1,0:T(8,128)(2,1)S(1)} %get-tuple-element.31.refs_0_, bf16[2,128,768]{2,1,0:T(8,128)(2,1)S(1)} %collective-permute-done.6.refs_1_, bf16[2,128,768]{2,1,0:T(8,128)(2,1)S(1)} %collective-permute-done.7.refs_2_, bf16[2,128,768]{2,1,0:T(8,128)(2,1)S(1)} %collective-permute-done.5.refs_3_, ...), custom_call_target="tpu_custom_call" | custom-call | flops 1358954496 | bytes 5013504 | tf_op jit(solution)/shard_map/gradient_part/pallas_call | solution.py:57
  31.9 1.7 %collective-permute-start.11 = (bf16[2,80,768]{2,1,0:T(8,128)(2,1)S(1)}, bf16[2,80,768]{2,1,0:T(8,128)(2,1)S(1)}, u32[]{:S(2)}, u32[]{:S(2)}) collective-permute-start(bf16[2,80,768]{2,1,0:T(8,128)(2,1)S(1)} %get-tuple-element.32), channel_id=1, source_target_pairs={{0,2},{1,3},{2,0},{3,1},{4,6},{5,7},{6,4},{7,5},{8,10},{9,11},{10,... | collective-permute-start | bytes 737288 | tf_op jit(solution)/shard_map/ppermute | solution.py:47
  33.6 1.5 %collective-permute-start.10 = (bf16[128,768]{1,0:T(8,128)(2,1)S(1)}, bf16[128,768]{1,0:T(8,128)(2,1)S(1)}, u32[]{:S(2)}, u32[]{:S(2)}) collective-permute-start(bf16[128,768]{1,0:T(8,128)(2,1)S(1)} %get-tuple-element.42.refs_1_), channel_id=1, source_target_pairs={{0,1},{1,0},{2,3},{3,2},{4,5},{5,4},{6,7},{7,6},{8,9},{9,8},{10,11... | collective-permute-start | bytes 589832 | tf_op jit(solution)/shard_map/ppermute | solution.py:47
  36.1 4.7 %collective-permute-done.11.arrived_ref = bf16[2,80,768]{2,1,0:T(8,128)(2,1)S(1)} collective-permute-done((bf16[2,80,768]{2,1,0:T(8,128)(2,1)S(1)}, bf16[2,80,768]{2,1,0:T(8,128)(2,1)S(1)}, u32[]{:S(2)}, u32[]{:S(2)}) %collective-permute-start.11) | collective-permute-done | bytes 245792 | tf_op jit(solution)/shard_map/ppermute | solution.py:47
  41.5 3.9 %collective-permute-done.13.arrived_ref = bf16[2,64,768]{2,1,0:T(8,128)(2,1)S(1)} collective-permute-done((bf16[2,64,768]{2,1,0:T(8,128)(2,1)S(1)}, bf16[2,64,768]{2,1,0:T(8,128)(2,1)S(1)}, u32[]{:S(2)}, u32[]{:S(2)}) %collective-permute-start.13) | collective-permute-done | bytes 196640 | tf_op jit(solution)/shard_map/ppermute | solution.py:47
  45.4 1.6 %collective-permute-start.28 = (bf16[128,768]{1,0:T(8,128)(2,1)S(1)}, bf16[128,768]{1,0:T(8,128)(2,1)S(1)}, u32[]{:S(2)}, u32[]{:S(2)}) collective-permute-start(bf16[128,768]{1,0:T(8,128)(2,1)S(1)} %get-tuple-element.42.refs_1_), channel_id=1, source_target_pairs={{0,17},{1,16},{2,19},{3,18},{4,21},{5,20},{6,23},{7,22},{8,25},{9,... | collective-permute-start | bytes 589832 | tf_op jit(solution)/shard_map/ppermute | solution.py:47
  47.0 2.4 %collective-permute-done.12.arrived_ref = bf16[1,80,768]{2,1,0:T(8,128)(2,1)S(1)} collective-permute-done((bf16[1,80,768]{2,1,0:T(8,128)(2,1)S(1)}, bf16[1,80,768]{2,1,0:T(8,128)(2,1)S(1)}, u32[]{:S(2)}, u32[]{:S(2)}) %collective-permute-start.12) | collective-permute-done | bytes 122912 | tf_op jit(solution)/shard_map/ppermute | solution.py:47
  50.3 3.6 %collective-permute-start.17 = (bf16[80,768]{1,0:T(8,128)(2,1)S(1)}, bf16[80,768]{1,0:T(8,128)(2,1)S(1)}, u32[]{:S(2)}, u32[]{:S(2)}) collective-permute-start(bf16[80,768]{1,0:T(8,128)(2,1)S(1)} %step.2.refs_2_), channel_id=1, source_target_pairs={{0,4},{1,5},{2,6},{3,7},{4,0},{5,1},{6,2},{7,3},{8,12},{9,13},{10,... | collective-permute-start | bytes 368648 | tf_op jit(solution)/shard_map/ppermute | solution.py:47
  54.8 3.0 %collective-permute-start.16 = (bf16[64,768]{1,0:T(8,128)(2,1)S(1)}, bf16[64,768]{1,0:T(8,128)(2,1)S(1)}, u32[]{:S(2)}, u32[]{:S(2)}) collective-permute-start(bf16[64,768]{1,0:T(8,128)(2,1)S(1)} %step.3.refs_3_), channel_id=1, source_target_pairs={{0,2},{1,3},{2,0},{3,1},{4,6},{5,7},{6,4},{7,5},{8,10},{9,11},{10,... | collective-permute-start | bytes 294920 | tf_op jit(solution)/shard_map/ppermute | solution.py:47
  57.8 3.2 %collective-permute-done.17.refs_6_ = bf16[80,768]{1,0:T(8,128)(2,1)S(1)} collective-permute-done((bf16[80,768]{1,0:T(8,128)(2,1)S(1)}, bf16[80,768]{1,0:T(8,128)(2,1)S(1)}, u32[]{:S(2)}, u32[]{:S(2)}) %collective-permute-start.17) | collective-permute-done | bytes 122912 | tf_op jit(solution)/shard_map/ppermute | solution.py:47
  62.1 1.4 %collective-permute-start.20 = (bf16[64,768]{1,0:T(8,128)(2,1)S(1)}, bf16[64,768]{1,0:T(8,128)(2,1)S(1)}, u32[]{:S(2)}, u32[]{:S(2)}) collective-permute-start(bf16[64,768]{1,0:T(8,128)(2,1)S(1)} %collective-permute-done.18.refs_7_), channel_id=1, source_target_pairs={{0,2},{1,3},{2,0},{3,1},{4,6},{5,7},{6,4},{7,5},{8,10},{9,11},{10,... | collective-permute-start | bytes 294920 | tf_op jit(solution)/shard_map/ppermute | solution.py:47
  63.5 3.3 %collective-permute-done.19.refs_8_ = bf16[80,768]{1,0:T(8,128)(2,1)S(1)} collective-permute-done((bf16[80,768]{1,0:T(8,128)(2,1)S(1)}, bf16[80,768]{1,0:T(8,128)(2,1)S(1)}, u32[]{:S(2)}, u32[]{:S(2)}) %collective-permute-start.19) | collective-permute-done | bytes 122912 | tf_op jit(solution)/shard_map/ppermute | solution.py:47
  71.6 2.1 %collective-permute-start.32 = (bf16[128,768]{1,0:T(8,128)(2,1)S(1)}, bf16[128,768]{1,0:T(8,128)(2,1)S(1)}, u32[]{:S(2)}, u32[]{:S(2)}) collective-permute-start(bf16[128,768]{1,0:T(8,128)(2,1)S(1)} %get-tuple-element.47), channel_id=1, source_target_pairs={{0,16},{1,17},{2,18},{3,19},{4,20},{5,21},{6,22},{7,23},{8,24},{9,... | collective-permute-start | bytes 589832 | tf_op jit(solution)/shard_map/ppermute | solution.py:47
  75.1 2.1 %attention.1.refs_1_ = f32[128,768]{1,0:T(8,128)S(1)} custom-call(bf16[128,768]{1,0:T(8,128)(2,1)S(1)} %copy-done.4, bf16[128,768]{1,0:T(8,128)(2,1)S(1)} %copy-done.1, bf16[128,768]{1,0:T(8,128)(2,1)S(1)} %copy-done.2), custom_call_target="tpu_custom_call" | custom-call | flops 50331648 | bytes 983040 | tf_op jit(solution)/shard_map/attention/pallas_call | solution.py:57
  77.2 2.1 %collective-permute-done.31.refs_2_ = bf16[128,768]{1,0:T(8,128)(2,1)S(1)} collective-permute-done((bf16[128,768]{1,0:T(8,128)(2,1)S(1)}, bf16[128,768]{1,0:T(8,128)(2,1)S(1)}, u32[]{:S(2)}, u32[]{:S(2)}) %collective-permute-start.31) | collective-permute-done | bytes 196640 | tf_op jit(solution)/shard_map/ppermute | solution.py:47
  79.3 3.6 %collective-permute-done.32.refs_3_ = bf16[128,768]{1,0:T(8,128)(2,1)S(1)} collective-permute-done((bf16[128,768]{1,0:T(8,128)(2,1)S(1)}, bf16[128,768]{1,0:T(8,128)(2,1)S(1)}, u32[]{:S(2)}, u32[]{:S(2)}) %collective-permute-start.32) | collective-permute-done | bytes 196640 | tf_op jit(solution)/shard_map/ppermute | solution.py:47
  (70 shorter events, 18.0 us)
Async XLA Ops:
  0.0 14.5 %collective-permute-start = (bf16[3,48,768]{2,1,0:T(8,128)(2,1)}, bf16[3,48,768]{2,1,0:T(8,128)(2,1)S(1)}, u32[]{:S(2)}, u32[]{:S(2)}) collective-permute-start(bf16[3,48,768]{2,1,0:T(8,128)(2,1)} %weights_ref), channel_id=1, source_target_pairs={{0,4},{1,5},{2,6},{3,7},{4,0},{5,1},{6,2},{7,3},{8,12},{9,13},{10,... | collective-permute-start | bytes 663560 | tf_op jit(solution)/shard_map/ppermute | solution.py:47
  6.0 12.3 %collective-permute-start.5 = (bf16[2,128,768]{2,1,0:T(8,128)(2,1)}, bf16[2,128,768]{2,1,0:T(8,128)(2,1)S(1)}, u32[]{:S(2)}, u32[]{:S(2)}) collective-permute-start(bf16[2,128,768]{2,1,0:T(8,128)(2,1)} %prep.1.pair_ref), channel_id=1, source_target_pairs={{0,16},{1,17},{2,18},{3,19},{4,20},{5,21},{6,22},{7,23},{8,24},{9,... | collective-permute-start | bytes 1179656 | tf_op jit(solution)/shard_map/ppermute | solution.py:47
  7.5 18.9 %collective-permute-start.7 = (bf16[2,128,768]{2,1,0:T(8,128)(2,1)}, bf16[2,128,768]{2,1,0:T(8,128)(2,1)S(1)}, u32[]{:S(2)}, u32[]{:S(2)}) collective-permute-start(bf16[2,128,768]{2,1,0:T(8,128)(2,1)} %prep.1.pair_ref), channel_id=1, source_target_pairs={{0,1},{1,0},{2,3},{3,2},{4,5},{5,4},{6,7},{7,6},{8,9},{9,8},{10,11... | collective-permute-start | bytes 1179656 | tf_op jit(solution)/shard_map/ppermute | solution.py:47
  9.1 17.9 %collective-permute-start.1 = (bf16[2,128,768]{2,1,0:T(8,128)(2,1)}, bf16[2,128,768]{2,1,0:T(8,128)(2,1)S(1)}, u32[]{:S(2)}, u32[]{:S(2)}) collective-permute-start(bf16[2,128,768]{2,1,0:T(8,128)(2,1)} %prep.1.pair_ref), channel_id=1, source_target_pairs={{0,17},{1,16},{2,19},{3,18},{4,21},{5,20},{6,23},{7,22},{8,25},{9,... | collective-permute-start | bytes 1179656 | tf_op jit(solution)/shard_map/ppermute | solution.py:47
  9.5 16.9 %collective-permute-start.3 = (bf16[3,48,768]{2,1,0:T(8,128)(2,1)}, bf16[3,48,768]{2,1,0:T(8,128)(2,1)S(1)}, u32[]{:S(2)}, u32[]{:S(2)}) collective-permute-start(bf16[3,48,768]{2,1,0:T(8,128)(2,1)} %weights_ref), channel_id=1, source_target_pairs={{0,2},{1,3},{2,0},{3,1},{4,6},{5,7},{6,4},{7,5},{8,10},{9,11},{10,... | collective-permute-start | bytes 663560 | tf_op jit(solution)/shard_map/ppermute | solution.py:47
  14.5 12.0 %collective-permute-start.4 = (bf16[3,48,768]{2,1,0:T(8,128)(2,1)S(1)}, bf16[3,48,768]{2,1,0:T(8,128)(2,1)S(1)}, u32[]{:S(2)}, u32[]{:S(2)}) collective-permute-start(bf16[3,48,768]{2,1,0:T(8,128)(2,1)S(1)} %collective-permute-done.refs_8_.refs_4_), channel_id=1, source_target_pairs={{0,2},{1,3},{2,0},{3,1},{4,6},{5,7},{6,4},{7,5},{8,10},{9,11},{10,... | collective-permute-start | bytes 663560 | tf_op jit(solution)/shard_map/ppermute | solution.py:47
  18.3 8.8 %collective-permute-start.9 = (bf16[2,128,768]{2,1,0:T(8,128)(2,1)S(1)}, bf16[2,128,768]{2,1,0:T(8,128)(2,1)S(1)}, u32[]{:S(2)}, u32[]{:S(2)}) collective-permute-start(bf16[2,128,768]{2,1,0:T(8,128)(2,1)S(1)} %collective-permute-done.5.refs_3_), channel_id=1, source_target_pairs={{0,8},{1,9},{2,10},{3,11},{4,12},{5,13},{6,14},{7,15},{8,0},{9,1},... | collective-permute-start | bytes 1179656 | tf_op jit(solution)/shard_map/ppermute | solution.py:47
  31.9 8.9 %collective-permute-start.11 = (bf16[2,80,768]{2,1,0:T(8,128)(2,1)S(1)}, bf16[2,80,768]{2,1,0:T(8,128)(2,1)S(1)}, u32[]{:S(2)}, u32[]{:S(2)}) collective-permute-start(bf16[2,80,768]{2,1,0:T(8,128)(2,1)S(1)} %get-tuple-element.32), channel_id=1, source_target_pairs={{0,2},{1,3},{2,0},{3,1},{4,6},{5,7},{6,4},{7,5},{8,10},{9,11},{10,... | collective-permute-start | bytes 737288 | tf_op jit(solution)/shard_map/ppermute | solution.py:47
  33.6 7.7 %collective-permute-start.10 = (bf16[128,768]{1,0:T(8,128)(2,1)S(1)}, bf16[128,768]{1,0:T(8,128)(2,1)S(1)}, u32[]{:S(2)}, u32[]{:S(2)}) collective-permute-start(bf16[128,768]{1,0:T(8,128)(2,1)S(1)} %get-tuple-element.42.refs_1_), channel_id=1, source_target_pairs={{0,1},{1,0},{2,3},{3,2},{4,5},{5,4},{6,7},{7,6},{8,9},{9,8},{10,11... | collective-permute-start | bytes 589832 | tf_op jit(solution)/shard_map/ppermute | solution.py:47
  35.1 6.4 %collective-permute-start.27 = (bf16[128,768]{1,0:T(8,128)(2,1)S(1)}, bf16[128,768]{1,0:T(8,128)(2,1)S(1)}, u32[]{:S(2)}, u32[]{:S(2)}) collective-permute-start(bf16[128,768]{1,0:T(8,128)(2,1)S(1)} %get-tuple-element.42.refs_1_), channel_id=1, source_target_pairs={{0,16},{1,17},{2,18},{3,19},{4,20},{5,21},{6,22},{7,23},{8,24},{9,... | collective-permute-start | bytes 589832 | tf_op jit(solution)/shard_map/ppermute | solution.py:47
  35.6 9.7 %collective-permute-start.13 = (bf16[2,64,768]{2,1,0:T(8,128)(2,1)S(1)}, bf16[2,64,768]{2,1,0:T(8,128)(2,1)S(1)}, u32[]{:S(2)}, u32[]{:S(2)}) collective-permute-start(bf16[2,64,768]{2,1,0:T(8,128)(2,1)S(1)} %get-tuple-element.38), channel_id=1, source_target_pairs={{0,2},{1,3},{2,0},{3,1},{4,6},{5,7},{6,4},{7,5},{8,10},{9,11},{10,... | collective-permute-start | bytes 589832 | tf_op jit(solution)/shard_map/ppermute | solution.py:47
  40.8 8.6 %collective-permute-start.12 = (bf16[1,80,768]{2,1,0:T(8,128)(2,1)S(1)}, bf16[1,80,768]{2,1,0:T(8,128)(2,1)S(1)}, u32[]{:S(2)}, u32[]{:S(2)}) collective-permute-start(bf16[1,80,768]{2,1,0:T(8,128)(2,1)S(1)} %get-tuple-element.36), channel_id=1, source_target_pairs={{0,4},{1,5},{2,6},{3,7},{4,0},{5,1},{6,2},{7,3},{8,12},{9,13},{10,... | collective-permute-start | bytes 368648 | tf_op jit(solution)/shard_map/ppermute | solution.py:47
  45.4 9.1 %collective-permute-start.14 = (bf16[1,64,768]{2,1,0:T(8,128)(2,1)S(1)}, bf16[1,64,768]{2,1,0:T(8,128)(2,1)S(1)}, u32[]{:S(2)}, u32[]{:S(2)}) collective-permute-start(bf16[1,64,768]{2,1,0:T(8,128)(2,1)S(1)} %get-tuple-element.40), channel_id=1, source_target_pairs={{0,4},{1,5},{2,6},{3,7},{4,0},{5,1},{6,2},{7,3},{8,12},{9,13},{10,... | collective-permute-start | bytes 294920 | tf_op jit(solution)/shard_map/ppermute | solution.py:47
  45.4 15.5 %collective-permute-start.28 = (bf16[128,768]{1,0:T(8,128)(2,1)S(1)}, bf16[128,768]{1,0:T(8,128)(2,1)S(1)}, u32[]{:S(2)}, u32[]{:S(2)}) collective-permute-start(bf16[128,768]{1,0:T(8,128)(2,1)S(1)} %get-tuple-element.42.refs_1_), channel_id=1, source_target_pairs={{0,17},{1,16},{2,19},{3,18},{4,21},{5,20},{6,23},{7,22},{8,25},{9,... | collective-permute-start | bytes 589832 | tf_op jit(solution)/shard_map/ppermute | solution.py:47
  49.6 8.2 %collective-permute-start.15 = (bf16[80,768]{1,0:T(8,128)(2,1)S(1)}, bf16[80,768]{1,0:T(8,128)(2,1)S(1)}, u32[]{:S(2)}, u32[]{:S(2)}) collective-permute-start(bf16[80,768]{1,0:T(8,128)(2,1)S(1)} %step.2.refs_2_), channel_id=1, source_target_pairs={{0,2},{1,3},{2,0},{3,1},{4,6},{5,7},{6,4},{7,5},{8,10},{9,11},{10,... | collective-permute-start | bytes 368648 | tf_op jit(solution)/shard_map/ppermute | solution.py:47
  50.3 10.6 %collective-permute-start.17 = (bf16[80,768]{1,0:T(8,128)(2,1)S(1)}, bf16[80,768]{1,0:T(8,128)(2,1)S(1)}, u32[]{:S(2)}, u32[]{:S(2)}) collective-permute-start(bf16[80,768]{1,0:T(8,128)(2,1)S(1)} %step.2.refs_2_), channel_id=1, source_target_pairs={{0,4},{1,5},{2,6},{3,7},{4,0},{5,1},{6,2},{7,3},{8,12},{9,13},{10,... | collective-permute-start | bytes 368648 | tf_op jit(solution)/shard_map/ppermute | solution.py:47
  54.7 7.4 %collective-permute-start.18 = (bf16[64,768]{1,0:T(8,128)(2,1)S(1)}, bf16[64,768]{1,0:T(8,128)(2,1)S(1)}, u32[]{:S(2)}, u32[]{:S(2)}) collective-permute-start(bf16[64,768]{1,0:T(8,128)(2,1)S(1)} %step.3.refs_3_), channel_id=1, source_target_pairs={{0,4},{1,5},{2,6},{3,7},{4,0},{5,1},{6,2},{7,3},{8,12},{9,13},{10,... | collective-permute-start | bytes 294920 | tf_op jit(solution)/shard_map/ppermute | solution.py:47
  54.8 8.7 %collective-permute-start.16 = (bf16[64,768]{1,0:T(8,128)(2,1)S(1)}, bf16[64,768]{1,0:T(8,128)(2,1)S(1)}, u32[]{:S(2)}, u32[]{:S(2)}) collective-permute-start(bf16[64,768]{1,0:T(8,128)(2,1)S(1)} %step.3.refs_3_), channel_id=1, source_target_pairs={{0,2},{1,3},{2,0},{3,1},{4,6},{5,7},{6,4},{7,5},{8,10},{9,11},{10,... | collective-permute-start | bytes 294920 | tf_op jit(solution)/shard_map/ppermute | solution.py:47
  60.9 5.8 %collective-permute-start.19 = (bf16[80,768]{1,0:T(8,128)(2,1)S(1)}, bf16[80,768]{1,0:T(8,128)(2,1)S(1)}, u32[]{:S(2)}, u32[]{:S(2)}) collective-permute-start(bf16[80,768]{1,0:T(8,128)(2,1)S(1)} %collective-permute-done.17.refs_6_), channel_id=1, source_target_pairs={{0,2},{1,3},{2,0},{3,1},{4,6},{5,7},{6,4},{7,5},{8,10},{9,11},{10,... | collective-permute-start | bytes 368648 | tf_op jit(solution)/shard_map/ppermute | solution.py:47
  60.9 6.9 %collective-permute-start.21 = (bf16[80,768]{1,0:T(8,128)(2,1)S(1)}, bf16[80,768]{1,0:T(8,128)(2,1)S(1)}, u32[]{:S(2)}, u32[]{:S(2)}) collective-permute-start(bf16[80,768]{1,0:T(8,128)(2,1)S(1)} %step.2.refs_2_), channel_id=1, source_target_pairs={{0,8},{1,9},{2,10},{3,11},{4,12},{5,13},{6,14},{7,15},{8,0},{9,1},... | collective-permute-start | bytes 368648 | tf_op jit(solution)/shard_map/ppermute | solution.py:47
  61.0 5.8 %collective-permute-start.22 = (bf16[64,768]{1,0:T(8,128)(2,1)S(1)}, bf16[64,768]{1,0:T(8,128)(2,1)S(1)}, u32[]{:S(2)}, u32[]{:S(2)}) collective-permute-start(bf16[64,768]{1,0:T(8,128)(2,1)S(1)} %step.3.refs_3_), channel_id=1, source_target_pairs={{0,8},{1,9},{2,10},{3,11},{4,12},{5,13},{6,14},{7,15},{8,0},{9,1},... | collective-permute-start | bytes 294920 | tf_op jit(solution)/shard_map/ppermute | solution.py:47
  70.6 8.7 %collective-permute-start.31 = (bf16[128,768]{1,0:T(8,128)(2,1)S(1)}, bf16[128,768]{1,0:T(8,128)(2,1)S(1)}, u32[]{:S(2)}, u32[]{:S(2)}) collective-permute-start(bf16[128,768]{1,0:T(8,128)(2,1)S(1)} %get-tuple-element.46), channel_id=1, source_target_pairs={{0,17},{1,16},{2,19},{3,18},{4,21},{5,20},{6,23},{7,22},{8,25},{9,... | collective-permute-start | bytes 589832 | tf_op jit(solution)/shard_map/ppermute | solution.py:47
  71.6 11.3 %collective-permute-start.32 = (bf16[128,768]{1,0:T(8,128)(2,1)S(1)}, bf16[128,768]{1,0:T(8,128)(2,1)S(1)}, u32[]{:S(2)}, u32[]{:S(2)}) collective-permute-start(bf16[128,768]{1,0:T(8,128)(2,1)S(1)} %get-tuple-element.47), channel_id=1, source_target_pairs={{0,16},{1,17},{2,18},{3,19},{4,20},{5,21},{6,22},{7,23},{8,24},{9,... | collective-permute-start | bytes 589832 | tf_op jit(solution)/shard_map/ppermute | solution.py:47
  74.6 8.3 %collective-permute-start.33 = (bf16[128,768]{1,0:T(8,128)(2,1)S(1)}, bf16[128,768]{1,0:T(8,128)(2,1)S(1)}, u32[]{:S(2)}, u32[]{:S(2)}) collective-permute-start(bf16[128,768]{1,0:T(8,128)(2,1)S(1)} %get-tuple-element.48), channel_id=1, source_target_pairs={{0,1},{1,0},{2,3},{3,2},{4,5},{5,4},{6,7},{7,6},{8,9},{9,8},{10,11... | collective-permute-start | bytes 589832 | tf_op jit(solution)/shard_map/ppermute | solution.py:47
  (16 other events, 93.1 us)

commit v3 on v2

--- a/solution.py
+++ b/solution.py
@@ -335,9 +335,9 @@
         own_weights, own_pair, query_normed = stage(after(fast_weights, line[bits[-1]]), pair, queries)
         own_there = send(after(own_pair, at_x, *[line[k] for k in range(1, n_far)]), swap)
         blocks = [own_weights] + [line[k] for k in range(1, n_far)]
-        tokens = [own_pair, own_there, at_y, at_x, send(at_y, swap), send(at_x, swap)]
-        part = gradient([(token,) for token in tokens], blocks)
-        chunks = gradient([(corner,), (send(corner, swap),)], blocks, part)
+        part = gradient([(token,) for token in (own_pair, own_there, at_x, send(at_x, swap))], blocks)
+        late = [at_y, corner, send(at_y, swap), send(corner, swap)]
+        chunks = gradient([(token,) for token in late], blocks, part)
 
         query_normed = after(query_normed, chunks[0][0])
         all_queries = [send(query_normed, layer(*o)) for o in ((1, 0), (0, 1))]

time: 83.9 us -> 82.3 us (0.981)
  waiting for transfers between devices: 39.5 us -> 36.8 us
  starting transfers between devices: 30.8 us -> 32 us
    ppermute x34, waiting for transfers between devices: 39.5 us -> 36.8 us  [send(): return lax.ppermute(array, AXES, pairs)]
    ppermute x34, starting transfers between devices: 30.8 us -> 32 us  [send(): return lax.ppermute(array, AXES, pairs)]
  transfers between devices with their start and end apart: 34 -> 34, of which waited for: 17 -> 18; matrix products, arithmetic and copies ran while one was open for 0% -> 0% of each run, Pallas kernels for 9% -> 9%
where the time goes in v3:
time: 82.3 us; the launch traced here: 82.1 us
  waiting for transfers between devices  36.8 us (45%)
  starting transfers between devices  32 us (39%)
  Pallas kernels  10.2 us (12%)
  local copies, waits for them, and re-layouts  2.89 us (4%)
    ppermute x34, waiting for transfers between devices, send(): return lax.ppermute(array, AXES, pairs)  36.8 us
    ppermute x34, starting transfers between devices, send(): return lax.ppermute(array, AXES, pairs)  32 us
    pallas_call x12, Pallas kernels, call(): pl.pallas_call(kernel, out_shape=list(outs), in_specs=[pl.BlockSpec(memor...  10.2 us
    unnamed x12, local copies, waits for them, and re-layouts  2.88 us
  transfers between devices with their start and end apart: 34, of which 18 were waited for; matrix products, arithmetic and copies ran while one was open for 0% of the time, Pallas kernels for 9%

profile of v3, /device:TPU:0, one launch (start us, length us, event | category | flops | bytes accessed | tf_op | source)
XLA Modules:
  0.0 82.1 jit_solution(6199855626345781290)
XLA Ops:
  0.0 4.0 %collective-permute-start = (bf16[3,48,768]{2,1,0:T(8,128)(2,1)}, bf16[3,48,768]{2,1,0:T(8,128)(2,1)S(1)}, u32[]{:S(2)}, u32[]{:S(2)}) collective-permute-start(bf16[3,48,768]{2,1,0:T(8,128)(2,1)} %weights_ref), channel_id=1, source_target_pairs={{0,4},{1,5},{2,6},{3,7},{4,0},{5,1},{6,2},{7,3},{8,12},{9,13},{10,... | collective-permute-start | bytes 663560 | tf_op jit(solution)/shard_map/ppermute | solution.py:47
  4.0 1.9 %prep.1.pair_ref = bf16[2,128,768]{2,1,0:T(8,128)(2,1)} custom-call(bf16[128,768]{1,0:T(8,128)(2,1)} %key_ref.1, bf16[128,768]{1,0:T(8,128)(2,1)} %value_ref.1, f32[1,128]{1,0:T(1,128)} %bitcast.4), custom_call_target="tpu_custom_call" | custom-call | bytes 786944 | tf_op jit(solution)/shard_map/prep/pallas_call | solution.py:57
  6.0 1.6 %collective-permute-start.7 = (bf16[2,128,768]{2,1,0:T(8,128)(2,1)}, bf16[2,128,768]{2,1,0:T(8,128)(2,1)S(1)}, u32[]{:S(2)}, u32[]{:S(2)}) collective-permute-start(bf16[2,128,768]{2,1,0:T(8,128)(2,1)} %prep.1.pair_ref), channel_id=1, source_target_pairs={{0,16},{1,17},{2,18},{3,19},{4,20},{5,21},{6,22},{7,23},{8,24},{9,... | collective-permute-start | bytes 1179656 | tf_op jit(solution)/shard_map/ppermute | solution.py:47
  7.5 1.5 %collective-permute-start.1 = (bf16[2,128,768]{2,1,0:T(8,128)(2,1)}, bf16[2,128,768]{2,1,0:T(8,128)(2,1)S(1)}, u32[]{:S(2)}, u32[]{:S(2)}) collective-permute-start(bf16[2,128,768]{2,1,0:T(8,128)(2,1)} %prep.1.pair_ref), channel_id=1, source_target_pairs={{0,1},{1,0},{2,3},{3,2},{4,5},{5,4},{6,7},{7,6},{8,9},{9,8},{10,11... | collective-permute-start | bytes 1179656 | tf_op jit(solution)/shard_map/ppermute | solution.py:47
  9.5 1.6 %collective-permute-start.5 = (bf16[3,48,768]{2,1,0:T(8,128)(2,1)}, bf16[3,48,768]{2,1,0:T(8,128)(2,1)S(1)}, u32[]{:S(2)}, u32[]{:S(2)}) collective-permute-start(bf16[3,48,768]{2,1,0:T(8,128)(2,1)} %weights_ref), channel_id=1, source_target_pairs={{0,2},{1,3},{2,0},{3,1},{4,6},{5,7},{6,4},{7,5},{8,10},{9,11},{10,... | collective-permute-start | bytes 663560 | tf_op jit(solution)/shard_map/ppermute | solution.py:47
  11.1 3.4 %collective-permute-done.refs_6_ = bf16[3,48,768]{2,1,0:T(8,128)(2,1)S(1)} collective-permute-done((bf16[3,48,768]{2,1,0:T(8,128)(2,1)}, bf16[3,48,768]{2,1,0:T(8,128)(2,1)S(1)}, u32[]{:S(2)}, u32[]{:S(2)}) %collective-permute-start) | collective-permute-done | bytes 221216 | tf_op jit(solution)/shard_map/ppermute | solution.py:47
  19.2 4.6 %collective-permute-done.6.refs_7_ = bf16[3,48,768]{2,1,0:T(8,128)(2,1)S(1)} collective-permute-done((bf16[3,48,768]{2,1,0:T(8,128)(2,1)S(1)}, bf16[3,48,768]{2,1,0:T(8,128)(2,1)S(1)}, u32[]{:S(2)}, u32[]{:S(2)}) %collective-permute-start.6) | collective-permute-done | bytes 221216 | tf_op jit(solution)/shard_map/ppermute | solution.py:47
  23.9 2.6 %collective-permute-done.1.refs_0_ = bf16[2,128,768]{2,1,0:T(8,128)(2,1)S(1)} collective-permute-done((bf16[2,128,768]{2,1,0:T(8,128)(2,1)}, bf16[2,128,768]{2,1,0:T(8,128)(2,1)S(1)}, u32[]{:S(2)}, u32[]{:S(2)}) %collective-permute-start.1) | collective-permute-done | bytes 393248 | tf_op jit(solution)/shard_map/ppermute | solution.py:47
  27.0 1.5 %gradient_part.1.refs_8_ = f32[576,768]{1,0:T(8,128)S(1)} custom-call(bf16[2,128,768]{2,1,0:T(8,128)(2,1)S(1)} %get-tuple-element.31.refs_0_, bf16[2,128,768]{2,1,0:T(8,128)(2,1)S(1)} %collective-permute-done.8.refs_1_, bf16[2,128,768]{2,1,0:T(8,128)(2,1)S(1)} %collective-permute-done.7.refs_2_, bf16[2,128,768]{2,1,0:T(8,128)(2,1)S(1)} %collective-permute-done.9.refs_3_, ...), custom_call_target="tpu_custom_call" | custom-call | flops 905969664 | bytes 4227072 | tf_op jit(solution)/shard_map/gradient_part/pallas_call | solution.py:57
  28.8 1.5 %gradient.1 = (bf16[2,80,768]{2,1,0:T(8,128)(2,1)S(1)}, f32[2,80,768]{2,1,0:T(8,128)S(1)}, bf16[2,64,768]{2,1,0:T(8,128)(2,1)S(1)}, f32[2,64,768]{2,1,0:T(8,128)S(1)}) custom-call(bf16[2,128,768]{2,1,0:T(8,128)(2,1)S(1)} %collective-permute-done.1.refs_0_, bf16[2,128,768]{2,1,0:T(8,128)(2,1)S(1)} %collective-permute-done.2.refs_1_, ...), custom_call_target="tpu_custom_call" | custom-call | flops 905969664 | bytes 5554176 | tf_op jit(solution)/shard_map/gradient/pallas_call | solution.py:57
  30.3 1.6 %collective-permute-start.11 = (bf16[2,80,768]{2,1,0:T(8,128)(2,1)S(1)}, bf16[2,80,768]{2,1,0:T(8,128)(2,1)S(1)}, u32[]{:S(2)}, u32[]{:S(2)}) collective-permute-start(bf16[2,80,768]{2,1,0:T(8,128)(2,1)S(1)} %get-tuple-element.32), channel_id=1, source_target_pairs={{0,2},{1,3},{2,0},{3,1},{4,6},{5,7},{6,4},{7,5},{8,10},{9,11},{10,... | collective-permute-start | bytes 737288 | tf_op jit(solution)/shard_map/ppermute | solution.py:47
  34.5 4.7 %collective-permute-done.11.arrived_ref = bf16[2,80,768]{2,1,0:T(8,128)(2,1)S(1)} collective-permute-done((bf16[2,80,768]{2,1,0:T(8,128)(2,1)S(1)}, bf16[2,80,768]{2,1,0:T(8,128)(2,1)S(1)}, u32[]{:S(2)}, u32[]{:S(2)}) %collective-permute-start.11) | collective-permute-done | bytes 245792 | tf_op jit(solution)/shard_map/ppermute | solution.py:47
  39.9 3.9 %collective-permute-done.13.arrived_ref = bf16[2,64,768]{2,1,0:T(8,128)(2,1)S(1)} collective-permute-done((bf16[2,64,768]{2,1,0:T(8,128)(2,1)S(1)}, bf16[2,64,768]{2,1,0:T(8,128)(2,1)S(1)}, u32[]{:S(2)}, u32[]{:S(2)}) %collective-permute-start.13) | collective-permute-done | bytes 196640 | tf_op jit(solution)/shard_map/ppermute | solution.py:47
  43.8 1.8 %collective-permute-start.28 = (bf16[128,768]{1,0:T(8,128)(2,1)S(1)}, bf16[128,768]{1,0:T(8,128)(2,1)S(1)}, u32[]{:S(2)}, u32[]{:S(2)}) collective-permute-start(bf16[128,768]{1,0:T(8,128)(2,1)S(1)} %get-tuple-element.42.refs_1_), channel_id=1, source_target_pairs={{0,17},{1,16},{2,19},{3,18},{4,21},{5,20},{6,23},{7,22},{8,25},{9,... | collective-permute-start | bytes 589832 | tf_op jit(solution)/shard_map/ppermute | solution.py:47
  45.7 2.0 %collective-permute-done.12.arrived_ref = bf16[1,80,768]{2,1,0:T(8,128)(2,1)S(1)} collective-permute-done((bf16[1,80,768]{2,1,0:T(8,128)(2,1)S(1)}, bf16[1,80,768]{2,1,0:T(8,128)(2,1)S(1)}, u32[]{:S(2)}, u32[]{:S(2)}) %collective-permute-start.12) | collective-permute-done | bytes 122912 | tf_op jit(solution)/shard_map/ppermute | solution.py:47
  48.7 3.6 %collective-permute-start.17 = (bf16[80,768]{1,0:T(8,128)(2,1)S(1)}, bf16[80,768]{1,0:T(8,128)(2,1)S(1)}, u32[]{:S(2)}, u32[]{:S(2)}) collective-permute-start(bf16[80,768]{1,0:T(8,128)(2,1)S(1)} %step.2.refs_2_), channel_id=1, source_target_pairs={{0,4},{1,5},{2,6},{3,7},{4,0},{5,1},{6,2},{7,3},{8,12},{9,13},{10,... | collective-permute-start | bytes 368648 | tf_op jit(solution)/shard_map/ppermute | solution.py:47
  52.6 3.8 %collective-permute-start.16 = (bf16[64,768]{1,0:T(8,128)(2,1)S(1)}, bf16[64,768]{1,0:T(8,128)(2,1)S(1)}, u32[]{:S(2)}, u32[]{:S(2)}) collective-permute-start(bf16[64,768]{1,0:T(8,128)(2,1)S(1)} %step.3.refs_3_), channel_id=1, source_target_pairs={{0,2},{1,3},{2,0},{3,1},{4,6},{5,7},{6,4},{7,5},{8,10},{9,11},{10,... | collective-permute-start | bytes 294920 | tf_op jit(solution)/shard_map/ppermute | solution.py:47
  56.5 2.5 %collective-permute-done.17.refs_6_ = bf16[80,768]{1,0:T(8,128)(2,1)S(1)} collective-permute-done((bf16[80,768]{1,0:T(8,128)(2,1)S(1)}, bf16[80,768]{1,0:T(8,128)(2,1)S(1)}, u32[]{:S(2)}, u32[]{:S(2)}) %collective-permute-start.17) | collective-permute-done | bytes 122912 | tf_op jit(solution)/shard_map/ppermute | solution.py:47
  61.6 3.1 %collective-permute-done.19.refs_8_ = bf16[80,768]{1,0:T(8,128)(2,1)S(1)} collective-permute-done((bf16[80,768]{1,0:T(8,128)(2,1)S(1)}, bf16[80,768]{1,0:T(8,128)(2,1)S(1)}, u32[]{:S(2)}, u32[]{:S(2)}) %collective-permute-start.19) | collective-permute-done | bytes 122912 | tf_op jit(solution)/shard_map/ppermute | solution.py:47
  68.6 1.9 %collective-permute-start.31 = (bf16[128,768]{1,0:T(8,128)(2,1)S(1)}, bf16[128,768]{1,0:T(8,128)(2,1)S(1)}, u32[]{:S(2)}, u32[]{:S(2)}) collective-permute-start(bf16[128,768]{1,0:T(8,128)(2,1)S(1)} %get-tuple-element.46), channel_id=1, source_target_pairs={{0,17},{1,16},{2,19},{3,18},{4,21},{5,20},{6,23},{7,22},{8,25},{9,... | collective-permute-start | bytes 589832 | tf_op jit(solution)/shard_map/ppermute | solution.py:47
  70.5 1.6 %collective-permute-start.32 = (bf16[128,768]{1,0:T(8,128)(2,1)S(1)}, bf16[128,768]{1,0:T(8,128)(2,1)S(1)}, u32[]{:S(2)}, u32[]{:S(2)}) collective-permute-start(bf16[128,768]{1,0:T(8,128)(2,1)S(1)} %get-tuple-element.47), channel_id=1, source_target_pairs={{0,16},{1,17},{2,18},{3,19},{4,20},{5,21},{6,22},{7,23},{8,24},{9,... | collective-permute-start | bytes 589832 | tf_op jit(solution)/shard_map/ppermute | solution.py:47
  73.4 2.1 %attention.1.refs_1_ = f32[128,768]{1,0:T(8,128)S(1)} custom-call(bf16[128,768]{1,0:T(8,128)(2,1)S(1)} %copy-done.4, bf16[128,768]{1,0:T(8,128)(2,1)S(1)} %copy-done.1, bf16[128,768]{1,0:T(8,128)(2,1)S(1)} %copy-done.2), custom_call_target="tpu_custom_call" | custom-call | flops 50331648 | bytes 983040 | tf_op jit(solution)/shard_map/attention/pallas_call | solution.py:57
  75.5 1.8 %collective-permute-done.31.refs_2_ = bf16[128,768]{1,0:T(8,128)(2,1)S(1)} collective-permute-done((bf16[128,768]{1,0:T(8,128)(2,1)S(1)}, bf16[128,768]{1,0:T(8,128)(2,1)S(1)}, u32[]{:S(2)}, u32[]{:S(2)}) %collective-permute-start.31) | collective-permute-done | bytes 196640 | tf_op jit(solution)/shard_map/ppermute | solution.py:47
  77.3 4.0 %collective-permute-done.32.refs_3_ = bf16[128,768]{1,0:T(8,128)(2,1)S(1)} collective-permute-done((bf16[128,768]{1,0:T(8,128)(2,1)S(1)}, bf16[128,768]{1,0:T(8,128)(2,1)S(1)}, u32[]{:S(2)}, u32[]{:S(2)}) %collective-permute-start.32) | collective-permute-done | bytes 196640 | tf_op jit(solution)/shard_map/ppermute | solution.py:47
  (70 shorter events, 19.1 us)
Async XLA Ops:
  0.0 14.5 %collective-permute-start = (bf16[3,48,768]{2,1,0:T(8,128)(2,1)}, bf16[3,48,768]{2,1,0:T(8,128)(2,1)S(1)}, u32[]{:S(2)}, u32[]{:S(2)}) collective-permute-start(bf16[3,48,768]{2,1,0:T(8,128)(2,1)} %weights_ref), channel_id=1, source_target_pairs={{0,4},{1,5},{2,6},{3,7},{4,0},{5,1},{6,2},{7,3},{8,12},{9,13},{10,... | collective-permute-start | bytes 663560 | tf_op jit(solution)/shard_map/ppermute | solution.py:47
  6.0 12.3 %collective-permute-start.7 = (bf16[2,128,768]{2,1,0:T(8,128)(2,1)}, bf16[2,128,768]{2,1,0:T(8,128)(2,1)S(1)}, u32[]{:S(2)}, u32[]{:S(2)}) collective-permute-start(bf16[2,128,768]{2,1,0:T(8,128)(2,1)} %prep.1.pair_ref), channel_id=1, source_target_pairs={{0,16},{1,17},{2,18},{3,19},{4,20},{5,21},{6,22},{7,23},{8,24},{9,... | collective-permute-start | bytes 1179656 | tf_op jit(solution)/shard_map/ppermute | solution.py:47
  7.5 18.9 %collective-permute-start.1 = (bf16[2,128,768]{2,1,0:T(8,128)(2,1)}, bf16[2,128,768]{2,1,0:T(8,128)(2,1)S(1)}, u32[]{:S(2)}, u32[]{:S(2)}) collective-permute-start(bf16[2,128,768]{2,1,0:T(8,128)(2,1)} %prep.1.pair_ref), channel_id=1, source_target_pairs={{0,1},{1,0},{2,3},{3,2},{4,5},{5,4},{6,7},{7,6},{8,9},{9,8},{10,11... | collective-permute-start | bytes 1179656 | tf_op jit(solution)/shard_map/ppermute | solution.py:47
  9.1 17.4 %collective-permute-start.2 = (bf16[2,128,768]{2,1,0:T(8,128)(2,1)}, bf16[2,128,768]{2,1,0:T(8,128)(2,1)S(1)}, u32[]{:S(2)}, u32[]{:S(2)}) collective-permute-start(bf16[2,128,768]{2,1,0:T(8,128)(2,1)} %prep.1.pair_ref), channel_id=1, source_target_pairs={{0,17},{1,16},{2,19},{3,18},{4,21},{5,20},{6,23},{7,22},{8,25},{9,... | collective-permute-start | bytes 1179656 | tf_op jit(solution)/shard_map/ppermute | solution.py:47
  9.5 9.7 %collective-permute-start.5 = (bf16[3,48,768]{2,1,0:T(8,128)(2,1)}, bf16[3,48,768]{2,1,0:T(8,128)(2,1)S(1)}, u32[]{:S(2)}, u32[]{:S(2)}) collective-permute-start(bf16[3,48,768]{2,1,0:T(8,128)(2,1)} %weights_ref), channel_id=1, source_target_pairs={{0,2},{1,3},{2,0},{3,1},{4,6},{5,7},{6,4},{7,5},{8,10},{9,11},{10,... | collective-permute-start | bytes 663560 | tf_op jit(solution)/shard_map/ppermute | solution.py:47
  14.5 9.4 %collective-permute-start.6 = (bf16[3,48,768]{2,1,0:T(8,128)(2,1)S(1)}, bf16[3,48,768]{2,1,0:T(8,128)(2,1)S(1)}, u32[]{:S(2)}, u32[]{:S(2)}) collective-permute-start(bf16[3,48,768]{2,1,0:T(8,128)(2,1)S(1)} %collective-permute-done.refs_6_), channel_id=1, source_target_pairs={{0,2},{1,3},{2,0},{3,1},{4,6},{5,7},{6,4},{7,5},{8,10},{9,11},{10,... | collective-permute-start | bytes 663560 | tf_op jit(solution)/shard_map/ppermute | solution.py:47
  18.3 8.7 %collective-permute-start.9 = (bf16[2,128,768]{2,1,0:T(8,128)(2,1)S(1)}, bf16[2,128,768]{2,1,0:T(8,128)(2,1)S(1)}, u32[]{:S(2)}, u32[]{:S(2)}) collective-permute-start(bf16[2,128,768]{2,1,0:T(8,128)(2,1)S(1)} %collective-permute-done.7.refs_2_), channel_id=1, source_target_pairs={{0,8},{1,9},{2,10},{3,11},{4,12},{5,13},{6,14},{7,15},{8,0},{9,1},... | collective-permute-start | bytes 1179656 | tf_op jit(solution)/shard_map/ppermute | solution.py:47
  30.3 8.9 %collective-permute-start.11 = (bf16[2,80,768]{2,1,0:T(8,128)(2,1)S(1)}, bf16[2,80,768]{2,1,0:T(8,128)(2,1)S(1)}, u32[]{:S(2)}, u32[]{:S(2)}) collective-permute-start(bf16[2,80,768]{2,1,0:T(8,128)(2,1)S(1)} %get-tuple-element.32), channel_id=1, source_target_pairs={{0,2},{1,3},{2,0},{3,1},{4,6},{5,7},{6,4},{7,5},{8,10},{9,11},{10,... | collective-permute-start | bytes 737288 | tf_op jit(solution)/shard_map/ppermute | solution.py:47
  31.9 7.7 %collective-permute-start.10 = (bf16[128,768]{1,0:T(8,128)(2,1)S(1)}, bf16[128,768]{1,0:T(8,128)(2,1)S(1)}, u32[]{:S(2)}, u32[]{:S(2)}) collective-permute-start(bf16[128,768]{1,0:T(8,128)(2,1)S(1)} %get-tuple-element.42.refs_1_), channel_id=1, source_target_pairs={{0,1},{1,0},{2,3},{3,2},{4,5},{5,4},{6,7},{7,6},{8,9},{9,8},{10,11... | collective-permute-start | bytes 589832 | tf_op jit(solution)/shard_map/ppermute | solution.py:47
  33.5 6.4 %collective-permute-start.27 = (bf16[128,768]{1,0:T(8,128)(2,1)S(1)}, bf16[128,768]{1,0:T(8,128)(2,1)S(1)}, u32[]{:S(2)}, u32[]{:S(2)}) collective-permute-start(bf16[128,768]{1,0:T(8,128)(2,1)S(1)} %get-tuple-element.42.refs_1_), channel_id=1, source_target_pairs={{0,16},{1,17},{2,18},{3,19},{4,20},{5,21},{6,22},{7,23},{8,24},{9,... | collective-permute-start | bytes 589832 | tf_op jit(solution)/shard_map/ppermute | solution.py:47
  34.0 9.7 %collective-permute-start.13 = (bf16[2,64,768]{2,1,0:T(8,128)(2,1)S(1)}, bf16[2,64,768]{2,1,0:T(8,128)(2,1)S(1)}, u32[]{:S(2)}, u32[]{:S(2)}) collective-permute-start(bf16[2,64,768]{2,1,0:T(8,128)(2,1)S(1)} %get-tuple-element.38), channel_id=1, source_target_pairs={{0,2},{1,3},{2,0},{3,1},{4,6},{5,7},{6,4},{7,5},{8,10},{9,11},{10,... | collective-permute-start | bytes 589832 | tf_op jit(solution)/shard_map/ppermute | solution.py:47
  39.2 8.4 %collective-permute-start.12 = (bf16[1,80,768]{2,1,0:T(8,128)(2,1)S(1)}, bf16[1,80,768]{2,1,0:T(8,128)(2,1)S(1)}, u32[]{:S(2)}, u32[]{:S(2)}) collective-permute-start(bf16[1,80,768]{2,1,0:T(8,128)(2,1)S(1)} %get-tuple-element.36), channel_id=1, source_target_pairs={{0,4},{1,5},{2,6},{3,7},{4,0},{5,1},{6,2},{7,3},{8,12},{9,13},{10,... | collective-permute-start | bytes 368648 | tf_op jit(solution)/shard_map/ppermute | solution.py:47
  43.7 8.6 %collective-permute-start.14 = (bf16[1,64,768]{2,1,0:T(8,128)(2,1)S(1)}, bf16[1,64,768]{2,1,0:T(8,128)(2,1)S(1)}, u32[]{:S(2)}, u32[]{:S(2)}) collective-permute-start(bf16[1,64,768]{2,1,0:T(8,128)(2,1)S(1)} %get-tuple-element.40), channel_id=1, source_target_pairs={{0,4},{1,5},{2,6},{3,7},{4,0},{5,1},{6,2},{7,3},{8,12},{9,13},{10,... | collective-permute-start | bytes 294920 | tf_op jit(solution)/shard_map/ppermute | solution.py:47
  43.8 15.1 %collective-permute-start.28 = (bf16[128,768]{1,0:T(8,128)(2,1)S(1)}, bf16[128,768]{1,0:T(8,128)(2,1)S(1)}, u32[]{:S(2)}, u32[]{:S(2)}) collective-permute-start(bf16[128,768]{1,0:T(8,128)(2,1)S(1)} %get-tuple-element.42.refs_1_), channel_id=1, source_target_pairs={{0,17},{1,16},{2,19},{3,18},{4,21},{5,20},{6,23},{7,22},{8,25},{9,... | collective-permute-start | bytes 589832 | tf_op jit(solution)/shard_map/ppermute | solution.py:47
  47.8 8.6 %collective-permute-start.15 = (bf16[80,768]{1,0:T(8,128)(2,1)S(1)}, bf16[80,768]{1,0:T(8,128)(2,1)S(1)}, u32[]{:S(2)}, u32[]{:S(2)}) collective-permute-start(bf16[80,768]{1,0:T(8,128)(2,1)S(1)} %step.2.refs_2_), channel_id=1, source_target_pairs={{0,2},{1,3},{2,0},{3,1},{4,6},{5,7},{6,4},{7,5},{8,10},{9,11},{10,... | collective-permute-start | bytes 368648 | tf_op jit(solution)/shard_map/ppermute | solution.py:47
  48.7 10.2 %collective-permute-start.17 = (bf16[80,768]{1,0:T(8,128)(2,1)S(1)}, bf16[80,768]{1,0:T(8,128)(2,1)S(1)}, u32[]{:S(2)}, u32[]{:S(2)}) collective-permute-start(bf16[80,768]{1,0:T(8,128)(2,1)S(1)} %step.2.refs_2_), channel_id=1, source_target_pairs={{0,4},{1,5},{2,6},{3,7},{4,0},{5,1},{6,2},{7,3},{8,12},{9,13},{10,... | collective-permute-start | bytes 368648 | tf_op jit(solution)/shard_map/ppermute | solution.py:47
  52.5 7.8 %collective-permute-start.18 = (bf16[64,768]{1,0:T(8,128)(2,1)S(1)}, bf16[64,768]{1,0:T(8,128)(2,1)S(1)}, u32[]{:S(2)}, u32[]{:S(2)}) collective-permute-start(bf16[64,768]{1,0:T(8,128)(2,1)S(1)} %step.3.refs_3_), channel_id=1, source_target_pairs={{0,4},{1,5},{2,6},{3,7},{4,0},{5,1},{6,2},{7,3},{8,12},{9,13},{10,... | collective-permute-start | bytes 294920 | tf_op jit(solution)/shard_map/ppermute | solution.py:47
  52.6 9.0 %collective-permute-start.16 = (bf16[64,768]{1,0:T(8,128)(2,1)S(1)}, bf16[64,768]{1,0:T(8,128)(2,1)S(1)}, u32[]{:S(2)}, u32[]{:S(2)}) collective-permute-start(bf16[64,768]{1,0:T(8,128)(2,1)S(1)} %step.3.refs_3_), channel_id=1, source_target_pairs={{0,2},{1,3},{2,0},{3,1},{4,6},{5,7},{6,4},{7,5},{8,10},{9,11},{10,... | collective-permute-start | bytes 294920 | tf_op jit(solution)/shard_map/ppermute | solution.py:47
  58.9 5.8 %collective-permute-start.19 = (bf16[80,768]{1,0:T(8,128)(2,1)S(1)}, bf16[80,768]{1,0:T(8,128)(2,1)S(1)}, u32[]{:S(2)}, u32[]{:S(2)}) collective-permute-start(bf16[80,768]{1,0:T(8,128)(2,1)S(1)} %collective-permute-done.17.refs_6_), channel_id=1, source_target_pairs={{0,2},{1,3},{2,0},{3,1},{4,6},{5,7},{6,4},{7,5},{8,10},{9,11},{10,... | collective-permute-start | bytes 368648 | tf_op jit(solution)/shard_map/ppermute | solution.py:47
  58.9 6.9 %collective-permute-start.21 = (bf16[80,768]{1,0:T(8,128)(2,1)S(1)}, bf16[80,768]{1,0:T(8,128)(2,1)S(1)}, u32[]{:S(2)}, u32[]{:S(2)}) collective-permute-start(bf16[80,768]{1,0:T(8,128)(2,1)S(1)} %step.2.refs_2_), channel_id=1, source_target_pairs={{0,8},{1,9},{2,10},{3,11},{4,12},{5,13},{6,14},{7,15},{8,0},{9,1},... | collective-permute-start | bytes 368648 | tf_op jit(solution)/shard_map/ppermute | solution.py:47
  58.9 5.8 %collective-permute-start.22 = (bf16[64,768]{1,0:T(8,128)(2,1)S(1)}, bf16[64,768]{1,0:T(8,128)(2,1)S(1)}, u32[]{:S(2)}, u32[]{:S(2)}) collective-permute-start(bf16[64,768]{1,0:T(8,128)(2,1)S(1)} %step.3.refs_3_), channel_id=1, source_target_pairs={{0,8},{1,9},{2,10},{3,11},{4,12},{5,13},{6,14},{7,15},{8,0},{9,1},... | collective-permute-start | bytes 294920 | tf_op jit(solution)/shard_map/ppermute | solution.py:47
  68.6 8.7 %collective-permute-start.31 = (bf16[128,768]{1,0:T(8,128)(2,1)S(1)}, bf16[128,768]{1,0:T(8,128)(2,1)S(1)}, u32[]{:S(2)}, u32[]{:S(2)}) collective-permute-start(bf16[128,768]{1,0:T(8,128)(2,1)S(1)} %get-tuple-element.46), channel_id=1, source_target_pairs={{0,17},{1,16},{2,19},{3,18},{4,21},{5,20},{6,23},{7,22},{8,25},{9,... | collective-permute-start | bytes 589832 | tf_op jit(solution)/shard_map/ppermute | solution.py:47
  70.5 10.8 %collective-permute-start.32 = (bf16[128,768]{1,0:T(8,128)(2,1)S(1)}, bf16[128,768]{1,0:T(8,128)(2,1)S(1)}, u32[]{:S(2)}, u32[]{:S(2)}) collective-permute-start(bf16[128,768]{1,0:T(8,128)(2,1)S(1)} %get-tuple-element.47), channel_id=1, source_target_pairs={{0,16},{1,17},{2,18},{3,19},{4,20},{5,21},{6,22},{7,23},{8,24},{9,... | collective-permute-start | bytes 589832 | tf_op jit(solution)/shard_map/ppermute | solution.py:47
  73.0 8.3 %collective-permute-start.33 = (bf16[128,768]{1,0:T(8,128)(2,1)S(1)}, bf16[128,768]{1,0:T(8,128)(2,1)S(1)}, u32[]{:S(2)}, u32[]{:S(2)}) collective-permute-start(bf16[128,768]{1,0:T(8,128)(2,1)S(1)} %get-tuple-element.48), channel_id=1, source_target_pairs={{0,1},{1,0},{2,3},{3,2},{4,5},{5,4},{6,7},{7,6},{8,9},{9,8},{10,11... | collective-permute-start | bytes 589832 | tf_op jit(solution)/shard_map/ppermute | solution.py:47
  (16 other events, 93.5 us)

commit v4 on v3

--- a/solution.py
+++ b/solution.py
@@ -319,11 +319,11 @@
     n_far, along, layer, swap = moves(mesh)
     bits = [1 << i for i in range(n_far.bit_length() - 1)]
 
-    def line_gather(block, near_first=False):
+    def line_gather(block, *first):
         blocks = {0: block}
         for bit in reversed(bits):
             for k in list(blocks):
-                source = after(blocks[k], blocks[1]) if near_first and k and bit == 1 else blocks[k]
+                source = after(blocks[k], *first) if first and k and bit == 1 else blocks[k]
                 blocks[k ^ bit] = send(source, along(bit))
         return blocks
 
@@ -351,7 +351,7 @@
                 arrived = send(part, along(bit))
                 part, keep = fold(keep, arrived)
             updated = step(old, keep, send(part, along(bits[-1])))
-            stepped.append(line_gather(updated, near_first=not stepped))
+            stepped.append(line_gather(updated, *[chunk[1] for chunk in stepped]))
         corner_query = send(after(query_normed, *all_queries), layer(1, 1))
         blocks = [[chunk[k] for chunk in stepped] for k in range(n_far)]
         there = [[send(array, swap) for array in block] for block in blocks[:-1]]

time: 82.3 us -> 81.7 us (level)
  transfers between devices with their start and end apart: 34 -> 34, of which waited for: 18 -> 17; matrix products, arithmetic and copies ran while one was open for 0% -> 0% of each run, Pallas kernels for 9% -> 9%
where the time goes in v4:
time: 81.7 us; the launch traced here: 81.5 us
  waiting for transfers between devices  36.2 us (44%)
  starting transfers between devices  32 us (39%)
  Pallas kernels  10.2 us (12%)
  local copies, waits for them, and re-layouts  2.89 us (4%)
    ppermute x34, waiting for transfers between devices, send(): return lax.ppermute(array, AXES, pairs)  36.2 us
    ppermute x34, starting transfers between devices, send(): return lax.ppermute(array, AXES, pairs)  32 us
    pallas_call x12, Pallas kernels, call(): pl.pallas_call(kernel, out_shape=list(outs), in_specs=[pl.BlockSpec(memor...  10.2 us
    unnamed x12, local copies, waits for them, and re-layouts  2.88 us
  transfers between devices with their start and end apart: 34, of which 17 were waited for; matrix products, arithmetic and copies ran while one was open for 0% of the time, Pallas kernels for 9%

profile of v4, /device:TPU:0, one launch (start us, length us, event | category | flops | bytes accessed | tf_op | source)
XLA Modules:
  0.0 81.5 jit_solution(8569681089733292795)
XLA Ops:
  0.0 4.0 %collective-permute-start = (bf16[3,48,768]{2,1,0:T(8,128)(2,1)}, bf16[3,48,768]{2,1,0:T(8,128)(2,1)S(1)}, u32[]{:S(2)}, u32[]{:S(2)}) collective-permute-start(bf16[3,48,768]{2,1,0:T(8,128)(2,1)} %weights_ref), channel_id=1, source_target_pairs={{0,4},{1,5},{2,6},{3,7},{4,0},{5,1},{6,2},{7,3},{8,12},{9,13},{10,... | collective-permute-start | bytes 663560 | tf_op jit(solution)/shard_map/ppermute | solution.py:47
  4.0 1.9 %prep.1.pair_ref = bf16[2,128,768]{2,1,0:T(8,128)(2,1)} custom-call(bf16[128,768]{1,0:T(8,128)(2,1)} %key_ref.1, bf16[128,768]{1,0:T(8,128)(2,1)} %value_ref.1, f32[1,128]{1,0:T(1,128)} %bitcast.4), custom_call_target="tpu_custom_call" | custom-call | bytes 786944 | tf_op jit(solution)/shard_map/prep/pallas_call | solution.py:57
  6.0 1.6 %collective-permute-start.7 = (bf16[2,128,768]{2,1,0:T(8,128)(2,1)}, bf16[2,128,768]{2,1,0:T(8,128)(2,1)S(1)}, u32[]{:S(2)}, u32[]{:S(2)}) collective-permute-start(bf16[2,128,768]{2,1,0:T(8,128)(2,1)} %prep.1.pair_ref), channel_id=1, source_target_pairs={{0,16},{1,17},{2,18},{3,19},{4,20},{5,21},{6,22},{7,23},{8,24},{9,... | collective-permute-start | bytes 1179656 | tf_op jit(solution)/shard_map/ppermute | solution.py:47
  7.5 1.5 %collective-permute-start.1 = (bf16[2,128,768]{2,1,0:T(8,128)(2,1)}, bf16[2,128,768]{2,1,0:T(8,128)(2,1)S(1)}, u32[]{:S(2)}, u32[]{:S(2)}) collective-permute-start(bf16[2,128,768]{2,1,0:T(8,128)(2,1)} %prep.1.pair_ref), channel_id=1, source_target_pairs={{0,1},{1,0},{2,3},{3,2},{4,5},{5,4},{6,7},{7,6},{8,9},{9,8},{10,11... | collective-permute-start | bytes 1179656 | tf_op jit(solution)/shard_map/ppermute | solution.py:47
  9.5 1.6 %collective-permute-start.5 = (bf16[3,48,768]{2,1,0:T(8,128)(2,1)}, bf16[3,48,768]{2,1,0:T(8,128)(2,1)S(1)}, u32[]{:S(2)}, u32[]{:S(2)}) collective-permute-start(bf16[3,48,768]{2,1,0:T(8,128)(2,1)} %weights_ref), channel_id=1, source_target_pairs={{0,2},{1,3},{2,0},{3,1},{4,6},{5,7},{6,4},{7,5},{8,10},{9,11},{10,... | collective-permute-start | bytes 663560 | tf_op jit(solution)/shard_map/ppermute | solution.py:47
  11.1 3.4 %collective-permute-done.refs_6_ = bf16[3,48,768]{2,1,0:T(8,128)(2,1)S(1)} collective-permute-done((bf16[3,48,768]{2,1,0:T(8,128)(2,1)}, bf16[3,48,768]{2,1,0:T(8,128)(2,1)S(1)}, u32[]{:S(2)}, u32[]{:S(2)}) %collective-permute-start) | collective-permute-done | bytes 221216 | tf_op jit(solution)/shard_map/ppermute | solution.py:47
  19.2 4.6 %collective-permute-done.6.refs_7_ = bf16[3,48,768]{2,1,0:T(8,128)(2,1)S(1)} collective-permute-done((bf16[3,48,768]{2,1,0:T(8,128)(2,1)S(1)}, bf16[3,48,768]{2,1,0:T(8,128)(2,1)S(1)}, u32[]{:S(2)}, u32[]{:S(2)}) %collective-permute-start.6) | collective-permute-done | bytes 221216 | tf_op jit(solution)/shard_map/ppermute | solution.py:47
  23.9 2.6 %collective-permute-done.1.refs_0_ = bf16[2,128,768]{2,1,0:T(8,128)(2,1)S(1)} collective-permute-done((bf16[2,128,768]{2,1,0:T(8,128)(2,1)}, bf16[2,128,768]{2,1,0:T(8,128)(2,1)S(1)}, u32[]{:S(2)}, u32[]{:S(2)}) %collective-permute-start.1) | collective-permute-done | bytes 393248 | tf_op jit(solution)/shard_map/ppermute | solution.py:47
  27.0 1.5 %gradient_part.1.refs_8_ = f32[576,768]{1,0:T(8,128)S(1)} custom-call(bf16[2,128,768]{2,1,0:T(8,128)(2,1)S(1)} %get-tuple-element.31.refs_0_, bf16[2,128,768]{2,1,0:T(8,128)(2,1)S(1)} %collective-permute-done.8.refs_1_, bf16[2,128,768]{2,1,0:T(8,128)(2,1)S(1)} %collective-permute-done.7.refs_2_, bf16[2,128,768]{2,1,0:T(8,128)(2,1)S(1)} %collective-permute-done.9.refs_3_, ...), custom_call_target="tpu_custom_call" | custom-call | flops 905969664 | bytes 4227072 | tf_op jit(solution)/shard_map/gradient_part/pallas_call | solution.py:57
  28.8 1.5 %gradient.1 = (bf16[2,80,768]{2,1,0:T(8,128)(2,1)S(1)}, f32[2,80,768]{2,1,0:T(8,128)S(1)}, bf16[2,64,768]{2,1,0:T(8,128)(2,1)S(1)}, f32[2,64,768]{2,1,0:T(8,128)S(1)}) custom-call(bf16[2,128,768]{2,1,0:T(8,128)(2,1)S(1)} %collective-permute-done.1.refs_0_, bf16[2,128,768]{2,1,0:T(8,128)(2,1)S(1)} %collective-permute-done.2.refs_1_, ...), custom_call_target="tpu_custom_call" | custom-call | flops 905969664 | bytes 5554176 | tf_op jit(solution)/shard_map/gradient/pallas_call | solution.py:57
  30.3 1.6 %collective-permute-start.11 = (bf16[2,80,768]{2,1,0:T(8,128)(2,1)S(1)}, bf16[2,80,768]{2,1,0:T(8,128)(2,1)S(1)}, u32[]{:S(2)}, u32[]{:S(2)}) collective-permute-start(bf16[2,80,768]{2,1,0:T(8,128)(2,1)S(1)} %get-tuple-element.32), channel_id=1, source_target_pairs={{0,2},{1,3},{2,0},{3,1},{4,6},{5,7},{6,4},{7,5},{8,10},{9,11},{10,... | collective-permute-start | bytes 737288 | tf_op jit(solution)/shard_map/ppermute | solution.py:47
  32.4 1.5 %collective-permute-start.10 = (bf16[128,768]{1,0:T(8,128)(2,1)S(1)}, bf16[128,768]{1,0:T(8,128)(2,1)S(1)}, u32[]{:S(2)}, u32[]{:S(2)}) collective-permute-start(bf16[128,768]{1,0:T(8,128)(2,1)S(1)} %get-tuple-element.42.refs_1_), channel_id=1, source_target_pairs={{0,1},{1,0},{2,3},{3,2},{4,5},{5,4},{6,7},{7,6},{8,9},{9,8},{10,11... | collective-permute-start | bytes 589832 | tf_op jit(solution)/shard_map/ppermute | solution.py:47
  34.5 4.7 %collective-permute-done.11.arrived_ref = bf16[2,80,768]{2,1,0:T(8,128)(2,1)S(1)} collective-permute-done((bf16[2,80,768]{2,1,0:T(8,128)(2,1)S(1)}, bf16[2,80,768]{2,1,0:T(8,128)(2,1)S(1)}, u32[]{:S(2)}, u32[]{:S(2)}) %collective-permute-start.11) | collective-permute-done | bytes 245792 | tf_op jit(solution)/shard_map/ppermute | solution.py:47
  39.6 4.1 %collective-permute-done.13.arrived_ref = bf16[2,64,768]{2,1,0:T(8,128)(2,1)S(1)} collective-permute-done((bf16[2,64,768]{2,1,0:T(8,128)(2,1)S(1)}, bf16[2,64,768]{2,1,0:T(8,128)(2,1)S(1)}, u32[]{:S(2)}, u32[]{:S(2)}) %collective-permute-start.13) | collective-permute-done | bytes 196640 | tf_op jit(solution)/shard_map/ppermute | solution.py:47
  43.8 1.8 %collective-permute-start.28 = (bf16[128,768]{1,0:T(8,128)(2,1)S(1)}, bf16[128,768]{1,0:T(8,128)(2,1)S(1)}, u32[]{:S(2)}, u32[]{:S(2)}) collective-permute-start(bf16[128,768]{1,0:T(8,128)(2,1)S(1)} %get-tuple-element.42.refs_1_), channel_id=1, source_target_pairs={{0,17},{1,16},{2,19},{3,18},{4,21},{5,20},{6,23},{7,22},{8,25},{9,... | collective-permute-start | bytes 589832 | tf_op jit(solution)/shard_map/ppermute | solution.py:47
  45.7 2.0 %collective-permute-done.12.arrived_ref = bf16[1,80,768]{2,1,0:T(8,128)(2,1)S(1)} collective-permute-done((bf16[1,80,768]{2,1,0:T(8,128)(2,1)S(1)}, bf16[1,80,768]{2,1,0:T(8,128)(2,1)S(1)}, u32[]{:S(2)}, u32[]{:S(2)}) %collective-permute-start.12) | collective-permute-done | bytes 122912 | tf_op jit(solution)/shard_map/ppermute | solution.py:47
  48.8 3.4 %collective-permute-start.15 = (bf16[80,768]{1,0:T(8,128)(2,1)S(1)}, bf16[80,768]{1,0:T(8,128)(2,1)S(1)}, u32[]{:S(2)}, u32[]{:S(2)}) collective-permute-start(bf16[80,768]{1,0:T(8,128)(2,1)S(1)} %step.2.refs_2_), channel_id=1, source_target_pairs={{0,2},{1,3},{2,0},{3,1},{4,6},{5,7},{6,4},{7,5},{8,10},{9,11},{10,... | collective-permute-start | bytes 368648 | tf_op jit(solution)/shard_map/ppermute | solution.py:47
  53.1 5.0 %collective-permute-start.16 = (bf16[64,768]{1,0:T(8,128)(2,1)S(1)}, bf16[64,768]{1,0:T(8,128)(2,1)S(1)}, u32[]{:S(2)}, u32[]{:S(2)}) collective-permute-start(bf16[64,768]{1,0:T(8,128)(2,1)S(1)} %step.3.refs_3_), channel_id=1, source_target_pairs={{0,2},{1,3},{2,0},{3,1},{4,6},{5,7},{6,4},{7,5},{8,10},{9,11},{10,... | collective-permute-start | bytes 294920 | tf_op jit(solution)/shard_map/ppermute | solution.py:47
  58.1 2.4 %collective-permute-done.18.refs_7_ = bf16[64,768]{1,0:T(8,128)(2,1)S(1)} collective-permute-done((bf16[64,768]{1,0:T(8,128)(2,1)S(1)}, bf16[64,768]{1,0:T(8,128)(2,1)S(1)}, u32[]{:S(2)}, u32[]{:S(2)}) %collective-permute-start.18) | collective-permute-done | bytes 98336 | tf_op jit(solution)/shard_map/ppermute | solution.py:47
  63.9 1.8 %collective-permute-done.20.refs_9_ = bf16[64,768]{1,0:T(8,128)(2,1)S(1)} collective-permute-done((bf16[64,768]{1,0:T(8,128)(2,1)S(1)}, bf16[64,768]{1,0:T(8,128)(2,1)S(1)}, u32[]{:S(2)}, u32[]{:S(2)}) %collective-permute-start.20) | collective-permute-done | bytes 98336 | tf_op jit(solution)/shard_map/ppermute | solution.py:47
  68.5 2.1 %collective-permute-start.31 = (bf16[128,768]{1,0:T(8,128)(2,1)S(1)}, bf16[128,768]{1,0:T(8,128)(2,1)S(1)}, u32[]{:S(2)}, u32[]{:S(2)}) collective-permute-start(bf16[128,768]{1,0:T(8,128)(2,1)S(1)} %get-tuple-element.46), channel_id=1, source_target_pairs={{0,17},{1,16},{2,19},{3,18},{4,21},{5,20},{6,23},{7,22},{8,25},{9,... | collective-permute-start | bytes 589832 | tf_op jit(solution)/shard_map/ppermute | solution.py:47
  73.0 2.1 %attention.1.refs_1_ = f32[128,768]{1,0:T(8,128)S(1)} custom-call(bf16[128,768]{1,0:T(8,128)(2,1)S(1)} %copy-done.4, bf16[128,768]{1,0:T(8,128)(2,1)S(1)} %copy-done.1, bf16[128,768]{1,0:T(8,128)(2,1)S(1)} %copy-done.2), custom_call_target="tpu_custom_call" | custom-call | flops 50331648 | bytes 983040 | tf_op jit(solution)/shard_map/attention/pallas_call | solution.py:57
  75.1 2.1 %collective-permute-done.31.refs_2_ = bf16[128,768]{1,0:T(8,128)(2,1)S(1)} collective-permute-done((bf16[128,768]{1,0:T(8,128)(2,1)S(1)}, bf16[128,768]{1,0:T(8,128)(2,1)S(1)}, u32[]{:S(2)}, u32[]{:S(2)}) %collective-permute-start.31) | collective-permute-done | bytes 196640 | tf_op jit(solution)/shard_map/ppermute | solution.py:47
  77.2 3.5 %collective-permute-done.32.refs_3_ = bf16[128,768]{1,0:T(8,128)(2,1)S(1)} collective-permute-done((bf16[128,768]{1,0:T(8,128)(2,1)S(1)}, bf16[128,768]{1,0:T(8,128)(2,1)S(1)}, u32[]{:S(2)}, u32[]{:S(2)}) %collective-permute-start.32) | collective-permute-done | bytes 196640 | tf_op jit(solution)/shard_map/ppermute | solution.py:47
  (70 shorter events, 18.8 us)
Async XLA Ops:
  0.0 14.5 %collective-permute-start = (bf16[3,48,768]{2,1,0:T(8,128)(2,1)}, bf16[3,48,768]{2,1,0:T(8,128)(2,1)S(1)}, u32[]{:S(2)}, u32[]{:S(2)}) collective-permute-start(bf16[3,48,768]{2,1,0:T(8,128)(2,1)} %weights_ref), channel_id=1, source_target_pairs={{0,4},{1,5},{2,6},{3,7},{4,0},{5,1},{6,2},{7,3},{8,12},{9,13},{10,... | collective-permute-start | bytes 663560 | tf_op jit(solution)/shard_map/ppermute | solution.py:47
  6.0 12.3 %collective-permute-start.7 = (bf16[2,128,768]{2,1,0:T(8,128)(2,1)}, bf16[2,128,768]{2,1,0:T(8,128)(2,1)S(1)}, u32[]{:S(2)}, u32[]{:S(2)}) collective-permute-start(bf16[2,128,768]{2,1,0:T(8,128)(2,1)} %prep.1.pair_ref), channel_id=1, source_target_pairs={{0,16},{1,17},{2,18},{3,19},{4,20},{5,21},{6,22},{7,23},{8,24},{9,... | collective-permute-start | bytes 1179656 | tf_op jit(solution)/shard_map/ppermute | solution.py:47
  7.5 18.9 %collective-permute-start.1 = (bf16[2,128,768]{2,1,0:T(8,128)(2,1)}, bf16[2,128,768]{2,1,0:T(8,128)(2,1)S(1)}, u32[]{:S(2)}, u32[]{:S(2)}) collective-permute-start(bf16[2,128,768]{2,1,0:T(8,128)(2,1)} %prep.1.pair_ref), channel_id=1, source_target_pairs={{0,1},{1,0},{2,3},{3,2},{4,5},{5,4},{6,7},{7,6},{8,9},{9,8},{10,11... | collective-permute-start | bytes 1179656 | tf_op jit(solution)/shard_map/ppermute | solution.py:47
  9.1 17.4 %collective-permute-start.2 = (bf16[2,128,768]{2,1,0:T(8,128)(2,1)}, bf16[2,128,768]{2,1,0:T(8,128)(2,1)S(1)}, u32[]{:S(2)}, u32[]{:S(2)}) collective-permute-start(bf16[2,128,768]{2,1,0:T(8,128)(2,1)} %prep.1.pair_ref), channel_id=1, source_target_pairs={{0,17},{1,16},{2,19},{3,18},{4,21},{5,20},{6,23},{7,22},{8,25},{9,... | collective-permute-start | bytes 1179656 | tf_op jit(solution)/shard_map/ppermute | solution.py:47
  9.5 9.7 %collective-permute-start.5 = (bf16[3,48,768]{2,1,0:T(8,128)(2,1)}, bf16[3,48,768]{2,1,0:T(8,128)(2,1)S(1)}, u32[]{:S(2)}, u32[]{:S(2)}) collective-permute-start(bf16[3,48,768]{2,1,0:T(8,128)(2,1)} %weights_ref), channel_id=1, source_target_pairs={{0,2},{1,3},{2,0},{3,1},{4,6},{5,7},{6,4},{7,5},{8,10},{9,11},{10,... | collective-permute-start | bytes 663560 | tf_op jit(solution)/shard_map/ppermute | solution.py:47
  14.5 9.4 %collective-permute-start.6 = (bf16[3,48,768]{2,1,0:T(8,128)(2,1)S(1)}, bf16[3,48,768]{2,1,0:T(8,128)(2,1)S(1)}, u32[]{:S(2)}, u32[]{:S(2)}) collective-permute-start(bf16[3,48,768]{2,1,0:T(8,128)(2,1)S(1)} %collective-permute-done.refs_6_), channel_id=1, source_target_pairs={{0,2},{1,3},{2,0},{3,1},{4,6},{5,7},{6,4},{7,5},{8,10},{9,11},{10,... | collective-permute-start | bytes 663560 | tf_op jit(solution)/shard_map/ppermute | solution.py:47
  18.3 8.7 %collective-permute-start.9 = (bf16[2,128,768]{2,1,0:T(8,128)(2,1)S(1)}, bf16[2,128,768]{2,1,0:T(8,128)(2,1)S(1)}, u32[]{:S(2)}, u32[]{:S(2)}) collective-permute-start(bf16[2,128,768]{2,1,0:T(8,128)(2,1)S(1)} %collective-permute-done.7.refs_2_), channel_id=1, source_target_pairs={{0,8},{1,9},{2,10},{3,11},{4,12},{5,13},{6,14},{7,15},{8,0},{9,1},... | collective-permute-start | bytes 1179656 | tf_op jit(solution)/shard_map/ppermute | solution.py:47
  30.3 8.9 %collective-permute-start.11 = (bf16[2,80,768]{2,1,0:T(8,128)(2,1)S(1)}, bf16[2,80,768]{2,1,0:T(8,128)(2,1)S(1)}, u32[]{:S(2)}, u32[]{:S(2)}) collective-permute-start(bf16[2,80,768]{2,1,0:T(8,128)(2,1)S(1)} %get-tuple-element.32), channel_id=1, source_target_pairs={{0,2},{1,3},{2,0},{3,1},{4,6},{5,7},{6,4},{7,5},{8,10},{9,11},{10,... | collective-permute-start | bytes 737288 | tf_op jit(solution)/shard_map/ppermute | solution.py:47
  31.9 11.8 %collective-permute-start.13 = (bf16[2,64,768]{2,1,0:T(8,128)(2,1)S(1)}, bf16[2,64,768]{2,1,0:T(8,128)(2,1)S(1)}, u32[]{:S(2)}, u32[]{:S(2)}) collective-permute-start(bf16[2,64,768]{2,1,0:T(8,128)(2,1)S(1)} %get-tuple-element.38), channel_id=1, source_target_pairs={{0,2},{1,3},{2,0},{3,1},{4,6},{5,7},{6,4},{7,5},{8,10},{9,11},{10,... | collective-permute-start | bytes 589832 | tf_op jit(solution)/shard_map/ppermute | solution.py:47
  32.4 11.4 %collective-permute-start.10 = (bf16[128,768]{1,0:T(8,128)(2,1)S(1)}, bf16[128,768]{1,0:T(8,128)(2,1)S(1)}, u32[]{:S(2)}, u32[]{:S(2)}) collective-permute-start(bf16[128,768]{1,0:T(8,128)(2,1)S(1)} %get-tuple-element.42.refs_1_), channel_id=1, source_target_pairs={{0,1},{1,0},{2,3},{3,2},{4,5},{5,4},{6,7},{7,6},{8,9},{9,8},{10,11... | collective-permute-start | bytes 589832 | tf_op jit(solution)/shard_map/ppermute | solution.py:47
  33.9 9.9 %collective-permute-start.27 = (bf16[128,768]{1,0:T(8,128)(2,1)S(1)}, bf16[128,768]{1,0:T(8,128)(2,1)S(1)}, u32[]{:S(2)}, u32[]{:S(2)}) collective-permute-start(bf16[128,768]{1,0:T(8,128)(2,1)S(1)} %get-tuple-element.42.refs_1_), channel_id=1, source_target_pairs={{0,16},{1,17},{2,18},{3,19},{4,20},{5,21},{6,22},{7,23},{8,24},{9,... | collective-permute-start | bytes 589832 | tf_op jit(solution)/shard_map/ppermute | solution.py:47
  39.2 8.4 %collective-permute-start.12 = (bf16[1,80,768]{2,1,0:T(8,128)(2,1)S(1)}, bf16[1,80,768]{2,1,0:T(8,128)(2,1)S(1)}, u32[]{:S(2)}, u32[]{:S(2)}) collective-permute-start(bf16[1,80,768]{2,1,0:T(8,128)(2,1)S(1)} %get-tuple-element.36), channel_id=1, source_target_pairs={{0,4},{1,5},{2,6},{3,7},{4,0},{5,1},{6,2},{7,3},{8,12},{9,13},{10,... | collective-permute-start | bytes 368648 | tf_op jit(solution)/shard_map/ppermute | solution.py:47
  43.7 9.1 %collective-permute-start.14 = (bf16[1,64,768]{2,1,0:T(8,128)(2,1)S(1)}, bf16[1,64,768]{2,1,0:T(8,128)(2,1)S(1)}, u32[]{:S(2)}, u32[]{:S(2)}) collective-permute-start(bf16[1,64,768]{2,1,0:T(8,128)(2,1)S(1)} %get-tuple-element.40), channel_id=1, source_target_pairs={{0,4},{1,5},{2,6},{3,7},{4,0},{5,1},{6,2},{7,3},{8,12},{9,13},{10,... | collective-permute-start | bytes 294920 | tf_op jit(solution)/shard_map/ppermute | solution.py:47
  43.8 17.1 %collective-permute-start.28 = (bf16[128,768]{1,0:T(8,128)(2,1)S(1)}, bf16[128,768]{1,0:T(8,128)(2,1)S(1)}, u32[]{:S(2)}, u32[]{:S(2)}) collective-permute-start(bf16[128,768]{1,0:T(8,128)(2,1)S(1)} %get-tuple-element.42.refs_1_), channel_id=1, source_target_pairs={{0,17},{1,16},{2,19},{3,18},{4,21},{5,20},{6,23},{7,22},{8,25},{9,... | collective-permute-start | bytes 589832 | tf_op jit(solution)/shard_map/ppermute | solution.py:47
  47.8 10.2 %collective-permute-start.17 = (bf16[80,768]{1,0:T(8,128)(2,1)S(1)}, bf16[80,768]{1,0:T(8,128)(2,1)S(1)}, u32[]{:S(2)}, u32[]{:S(2)}) collective-permute-start(bf16[80,768]{1,0:T(8,128)(2,1)S(1)} %step.2.refs_2_), channel_id=1, source_target_pairs={{0,4},{1,5},{2,6},{3,7},{4,0},{5,1},{6,2},{7,3},{8,12},{9,13},{10,... | collective-permute-start | bytes 368648 | tf_op jit(solution)/shard_map/ppermute | solution.py:47
  48.8 11.6 %collective-permute-start.15 = (bf16[80,768]{1,0:T(8,128)(2,1)S(1)}, bf16[80,768]{1,0:T(8,128)(2,1)S(1)}, u32[]{:S(2)}, u32[]{:S(2)}) collective-permute-start(bf16[80,768]{1,0:T(8,128)(2,1)S(1)} %step.2.refs_2_), channel_id=1, source_target_pairs={{0,2},{1,3},{2,0},{3,1},{4,6},{5,7},{6,4},{7,5},{8,10},{9,11},{10,... | collective-permute-start | bytes 368648 | tf_op jit(solution)/shard_map/ppermute | solution.py:47
  53.0 7.4 %collective-permute-start.18 = (bf16[64,768]{1,0:T(8,128)(2,1)S(1)}, bf16[64,768]{1,0:T(8,128)(2,1)S(1)}, u32[]{:S(2)}, u32[]{:S(2)}) collective-permute-start(bf16[64,768]{1,0:T(8,128)(2,1)S(1)} %step.3.refs_3_), channel_id=1, source_target_pairs={{0,4},{1,5},{2,6},{3,7},{4,0},{5,1},{6,2},{7,3},{8,12},{9,13},{10,... | collective-permute-start | bytes 294920 | tf_op jit(solution)/shard_map/ppermute | solution.py:47
  53.1 8.8 %collective-permute-start.16 = (bf16[64,768]{1,0:T(8,128)(2,1)S(1)}, bf16[64,768]{1,0:T(8,128)(2,1)S(1)}, u32[]{:S(2)}, u32[]{:S(2)}) collective-permute-start(bf16[64,768]{1,0:T(8,128)(2,1)S(1)} %step.3.refs_3_), channel_id=1, source_target_pairs={{0,2},{1,3},{2,0},{3,1},{4,6},{5,7},{6,4},{7,5},{8,10},{9,11},{10,... | collective-permute-start | bytes 294920 | tf_op jit(solution)/shard_map/ppermute | solution.py:47
  58.1 5.3 %collective-permute-start.19 = (bf16[80,768]{1,0:T(8,128)(2,1)S(1)}, bf16[80,768]{1,0:T(8,128)(2,1)S(1)}, u32[]{:S(2)}, u32[]{:S(2)}) collective-permute-start(bf16[80,768]{1,0:T(8,128)(2,1)S(1)} %collective-permute-done.17.refs_6_), channel_id=1, source_target_pairs={{0,2},{1,3},{2,0},{3,1},{4,6},{5,7},{6,4},{7,5},{8,10},{9,11},{10,... | collective-permute-start | bytes 368648 | tf_op jit(solution)/shard_map/ppermute | solution.py:47
  60.5 5.3 %collective-permute-start.21 = (bf16[80,768]{1,0:T(8,128)(2,1)S(1)}, bf16[80,768]{1,0:T(8,128)(2,1)S(1)}, u32[]{:S(2)}, u32[]{:S(2)}) collective-permute-start(bf16[80,768]{1,0:T(8,128)(2,1)S(1)} %step.2.refs_2_), channel_id=1, source_target_pairs={{0,8},{1,9},{2,10},{3,11},{4,12},{5,13},{6,14},{7,15},{8,0},{9,1},... | collective-permute-start | bytes 368648 | tf_op jit(solution)/shard_map/ppermute | solution.py:47
  61.0 4.8 %collective-permute-start.20 = (bf16[64,768]{1,0:T(8,128)(2,1)S(1)}, bf16[64,768]{1,0:T(8,128)(2,1)S(1)}, u32[]{:S(2)}, u32[]{:S(2)}) collective-permute-start(bf16[64,768]{1,0:T(8,128)(2,1)S(1)} %collective-permute-done.18.refs_7_), channel_id=1, source_target_pairs={{0,2},{1,3},{2,0},{3,1},{4,6},{5,7},{6,4},{7,5},{8,10},{9,11},{10,... | collective-permute-start | bytes 294920 | tf_op jit(solution)/shard_map/ppermute | solution.py:47
  68.5 8.7 %collective-permute-start.31 = (bf16[128,768]{1,0:T(8,128)(2,1)S(1)}, bf16[128,768]{1,0:T(8,128)(2,1)S(1)}, u32[]{:S(2)}, u32[]{:S(2)}) collective-permute-start(bf16[128,768]{1,0:T(8,128)(2,1)S(1)} %get-tuple-element.46), channel_id=1, source_target_pairs={{0,17},{1,16},{2,19},{3,18},{4,21},{5,20},{6,23},{7,22},{8,25},{9,... | collective-permute-start | bytes 589832 | tf_op jit(solution)/shard_map/ppermute | solution.py:47
  70.5 10.2 %collective-permute-start.32 = (bf16[128,768]{1,0:T(8,128)(2,1)S(1)}, bf16[128,768]{1,0:T(8,128)(2,1)S(1)}, u32[]{:S(2)}, u32[]{:S(2)}) collective-permute-start(bf16[128,768]{1,0:T(8,128)(2,1)S(1)} %get-tuple-element.47), channel_id=1, source_target_pairs={{0,16},{1,17},{2,18},{3,19},{4,20},{5,21},{6,22},{7,23},{8,24},{9,... | collective-permute-start | bytes 589832 | tf_op jit(solution)/shard_map/ppermute | solution.py:47
  72.4 8.3 %collective-permute-start.33 = (bf16[128,768]{1,0:T(8,128)(2,1)S(1)}, bf16[128,768]{1,0:T(8,128)(2,1)S(1)}, u32[]{:S(2)}, u32[]{:S(2)}) collective-permute-start(bf16[128,768]{1,0:T(8,128)(2,1)S(1)} %get-tuple-element.48), channel_id=1, source_target_pairs={{0,1},{1,0},{2,3},{3,2},{4,5},{5,4},{6,7},{7,6},{8,9},{9,8},{10,11... | collective-permute-start | bytes 589832 | tf_op jit(solution)/shard_map/ppermute | solution.py:47
  (16 other events, 89.9 us)

commit v5 on v4

--- a/solution.py
+++ b/solution.py
@@ -355,7 +355,7 @@
         corner_query = send(after(query_normed, *all_queries), layer(1, 1))
         blocks = [[chunk[k] for chunk in stepped] for k in range(n_far)]
         there = [[send(array, swap) for array in block] for block in blocks[:-1]]
-        there.append([send(after(array, corner_query), swap) for array in blocks[-1]])
+        there.append([send(after(blocks[-1][0], corner_query), swap), send(blocks[-1][1], swap)])
         blocks += there
 
         outs = apply_rows([corner_query, all_queries[0]], blocks, rows, BF)

time: 81.7 us -> 85.4 us (1.045)
  waiting for transfers between devices: 36.2 us -> 40.5 us
    ppermute x34, waiting for transfers between devices: 36.2 us -> 40.5 us  [send(): return lax.ppermute(array, AXES, pairs)]
  transfers between devices with their start and end apart: 34 -> 34, of which waited for: 17 -> 15; matrix products, arithmetic and copies ran while one was open for 0% -> 0% of each run, Pallas kernels for 9% -> 8%
where the time goes in v5:
time: 85.4 us; the launch traced here: 85.2 us
  waiting for transfers between devices  40.5 us (47%)
  starting transfers between devices  31.4 us (37%)
  Pallas kernels  10.2 us (12%)
  local copies, waits for them, and re-layouts  2.89 us (3%)
    ppermute x34, waiting for transfers between devices, send(): return lax.ppermute(array, AXES, pairs)  40.5 us
    ppermute x34, starting transfers between devices, send(): return lax.ppermute(array, AXES, pairs)  31.4 us
    pallas_call x12, Pallas kernels, call(): pl.pallas_call(kernel, out_shape=list(outs), in_specs=[pl.BlockSpec(memor...  10.2 us
    unnamed x12, local copies, waits for them, and re-layouts  2.88 us
  transfers between devices with their start and end apart: 34, of which 15 were waited for; matrix products, arithmetic and copies ran while one was open for 0% of the time, Pallas kernels for 8%

profile of v5, /device:TPU:0, one launch (start us, length us, event | category | flops | bytes accessed | tf_op | source)
XLA Modules:
  0.0 85.2 jit_solution(16627741763689569855)
XLA Ops:
  0.0 4.0 %collective-permute-start = (bf16[3,48,768]{2,1,0:T(8,128)(2,1)}, bf16[3,48,768]{2,1,0:T(8,128)(2,1)S(1)}, u32[]{:S(2)}, u32[]{:S(2)}) collective-permute-start(bf16[3,48,768]{2,1,0:T(8,128)(2,1)} %weights_ref), channel_id=1, source_target_pairs={{0,4},{1,5},{2,6},{3,7},{4,0},{5,1},{6,2},{7,3},{8,12},{9,13},{10,... | collective-permute-start | bytes 663560 | tf_op jit(solution)/shard_map/ppermute | solution.py:47
  4.0 1.9 %prep.1.pair_ref = bf16[2,128,768]{2,1,0:T(8,128)(2,1)} custom-call(bf16[128,768]{1,0:T(8,128)(2,1)} %key_ref.1, bf16[128,768]{1,0:T(8,128)(2,1)} %value_ref.1, f32[1,128]{1,0:T(1,128)} %bitcast.4), custom_call_target="tpu_custom_call" | custom-call | bytes 786944 | tf_op jit(solution)/shard_map/prep/pallas_call | solution.py:57
  6.0 1.6 %collective-permute-start.7 = (bf16[2,128,768]{2,1,0:T(8,128)(2,1)}, bf16[2,128,768]{2,1,0:T(8,128)(2,1)S(1)}, u32[]{:S(2)}, u32[]{:S(2)}) collective-permute-start(bf16[2,128,768]{2,1,0:T(8,128)(2,1)} %prep.1.pair_ref), channel_id=1, source_target_pairs={{0,16},{1,17},{2,18},{3,19},{4,20},{5,21},{6,22},{7,23},{8,24},{9,... | collective-permute-start | bytes 1179656 | tf_op jit(solution)/shard_map/ppermute | solution.py:47
  7.5 1.5 %collective-permute-start.1 = (bf16[2,128,768]{2,1,0:T(8,128)(2,1)}, bf16[2,128,768]{2,1,0:T(8,128)(2,1)S(1)}, u32[]{:S(2)}, u32[]{:S(2)}) collective-permute-start(bf16[2,128,768]{2,1,0:T(8,128)(2,1)} %prep.1.pair_ref), channel_id=1, source_target_pairs={{0,1},{1,0},{2,3},{3,2},{4,5},{5,4},{6,7},{7,6},{8,9},{9,8},{10,11... | collective-permute-start | bytes 1179656 | tf_op jit(solution)/shard_map/ppermute | solution.py:47
  9.5 1.6 %collective-permute-start.5 = (bf16[3,48,768]{2,1,0:T(8,128)(2,1)}, bf16[3,48,768]{2,1,0:T(8,128)(2,1)S(1)}, u32[]{:S(2)}, u32[]{:S(2)}) collective-permute-start(bf16[3,48,768]{2,1,0:T(8,128)(2,1)} %weights_ref), channel_id=1, source_target_pairs={{0,2},{1,3},{2,0},{3,1},{4,6},{5,7},{6,4},{7,5},{8,10},{9,11},{10,... | collective-permute-start | bytes 663560 | tf_op jit(solution)/shard_map/ppermute | solution.py:47
  11.1 3.4 %collective-permute-done.refs_6_ = bf16[3,48,768]{2,1,0:T(8,128)(2,1)S(1)} collective-permute-done((bf16[3,48,768]{2,1,0:T(8,128)(2,1)}, bf16[3,48,768]{2,1,0:T(8,128)(2,1)S(1)}, u32[]{:S(2)}, u32[]{:S(2)}) %collective-permute-start) | collective-permute-done | bytes 221216 | tf_op jit(solution)/shard_map/ppermute | solution.py:47
  19.2 4.6 %collective-permute-done.6.refs_7_ = bf16[3,48,768]{2,1,0:T(8,128)(2,1)S(1)} collective-permute-done((bf16[3,48,768]{2,1,0:T(8,128)(2,1)S(1)}, bf16[3,48,768]{2,1,0:T(8,128)(2,1)S(1)}, u32[]{:S(2)}, u32[]{:S(2)}) %collective-permute-start.6) | collective-permute-done | bytes 221216 | tf_op jit(solution)/shard_map/ppermute | solution.py:47
  23.9 2.6 %collective-permute-done.1.refs_0_ = bf16[2,128,768]{2,1,0:T(8,128)(2,1)S(1)} collective-permute-done((bf16[2,128,768]{2,1,0:T(8,128)(2,1)}, bf16[2,128,768]{2,1,0:T(8,128)(2,1)S(1)}, u32[]{:S(2)}, u32[]{:S(2)}) %collective-permute-start.1) | collective-permute-done | bytes 393248 | tf_op jit(solution)/shard_map/ppermute | solution.py:47
  27.0 1.5 %gradient_part.1.refs_8_ = f32[576,768]{1,0:T(8,128)S(1)} custom-call(bf16[2,128,768]{2,1,0:T(8,128)(2,1)S(1)} %get-tuple-element.30.refs_0_, bf16[2,128,768]{2,1,0:T(8,128)(2,1)S(1)} %collective-permute-done.8.refs_1_, bf16[2,128,768]{2,1,0:T(8,128)(2,1)S(1)} %collective-permute-done.7.refs_2_, bf16[2,128,768]{2,1,0:T(8,128)(2,1)S(1)} %collective-permute-done.9.refs_3_, ...), custom_call_target="tpu_custom_call" | custom-call | flops 905969664 | bytes 4227072 | tf_op jit(solution)/shard_map/gradient_part/pallas_call | solution.py:57
  28.8 1.5 %gradient.1 = (bf16[2,80,768]{2,1,0:T(8,128)(2,1)S(1)}, f32[2,80,768]{2,1,0:T(8,128)S(1)}, bf16[2,64,768]{2,1,0:T(8,128)(2,1)S(1)}, f32[2,64,768]{2,1,0:T(8,128)S(1)}) custom-call(bf16[2,128,768]{2,1,0:T(8,128)(2,1)S(1)} %collective-permute-done.1.refs_0_, bf16[2,128,768]{2,1,0:T(8,128)(2,1)S(1)} %collective-permute-done.2.refs_1_, ...), custom_call_target="tpu_custom_call" | custom-call | flops 905969664 | bytes 5554176 | tf_op jit(solution)/shard_map/gradient/pallas_call | solution.py:57
  30.3 1.6 %collective-permute-start.11 = (bf16[2,80,768]{2,1,0:T(8,128)(2,1)S(1)}, bf16[2,80,768]{2,1,0:T(8,128)(2,1)S(1)}, u32[]{:S(2)}, u32[]{:S(2)}) collective-permute-start(bf16[2,80,768]{2,1,0:T(8,128)(2,1)S(1)} %get-tuple-element.31), channel_id=1, source_target_pairs={{0,2},{1,3},{2,0},{3,1},{4,6},{5,7},{6,4},{7,5},{8,10},{9,11},{10,... | collective-permute-start | bytes 737288 | tf_op jit(solution)/shard_map/ppermute | solution.py:47
  34.5 4.7 %collective-permute-done.11.arrived_ref = bf16[2,80,768]{2,1,0:T(8,128)(2,1)S(1)} collective-permute-done((bf16[2,80,768]{2,1,0:T(8,128)(2,1)S(1)}, bf16[2,80,768]{2,1,0:T(8,128)(2,1)S(1)}, u32[]{:S(2)}, u32[]{:S(2)}) %collective-permute-start.11) | collective-permute-done | bytes 245792 | tf_op jit(solution)/shard_map/ppermute | solution.py:47
  39.6 4.1 %collective-permute-done.13.arrived_ref = bf16[2,64,768]{2,1,0:T(8,128)(2,1)S(1)} collective-permute-done((bf16[2,64,768]{2,1,0:T(8,128)(2,1)S(1)}, bf16[2,64,768]{2,1,0:T(8,128)(2,1)S(1)}, u32[]{:S(2)}, u32[]{:S(2)}) %collective-permute-start.13) | collective-permute-done | bytes 196640 | tf_op jit(solution)/shard_map/ppermute | solution.py:47
  43.8 1.8 %collective-permute-start.28 = (bf16[128,768]{1,0:T(8,128)(2,1)S(1)}, bf16[128,768]{1,0:T(8,128)(2,1)S(1)}, u32[]{:S(2)}, u32[]{:S(2)}) collective-permute-start(bf16[128,768]{1,0:T(8,128)(2,1)S(1)} %get-tuple-element.41.refs_1_), channel_id=1, source_target_pairs={{0,17},{1,16},{2,19},{3,18},{4,21},{5,20},{6,23},{7,22},{8,25},{9,... | collective-permute-start | bytes 589832 | tf_op jit(solution)/shard_map/ppermute | solution.py:47
  45.7 2.0 %collective-permute-done.12.arrived_ref = bf16[1,80,768]{2,1,0:T(8,128)(2,1)S(1)} collective-permute-done((bf16[1,80,768]{2,1,0:T(8,128)(2,1)S(1)}, bf16[1,80,768]{2,1,0:T(8,128)(2,1)S(1)}, u32[]{:S(2)}, u32[]{:S(2)}) %collective-permute-start.12) | collective-permute-done | bytes 122912 | tf_op jit(solution)/shard_map/ppermute | solution.py:47
  48.8 4.0 %collective-permute-done.14.arrived_ref = bf16[1,64,768]{2,1,0:T(8,128)(2,1)S(1)} collective-permute-done((bf16[1,64,768]{2,1,0:T(8,128)(2,1)S(1)}, bf16[1,64,768]{2,1,0:T(8,128)(2,1)S(1)}, u32[]{:S(2)}, u32[]{:S(2)}) %collective-permute-start.14) | collective-permute-done | bytes 98336 | tf_op jit(solution)/shard_map/ppermute | solution.py:47
  53.1 5.0 %collective-permute-start.15 = (bf16[80,768]{1,0:T(8,128)(2,1)S(1)}, bf16[80,768]{1,0:T(8,128)(2,1)S(1)}, u32[]{:S(2)}, u32[]{:S(2)}) collective-permute-start(bf16[80,768]{1,0:T(8,128)(2,1)S(1)} %step.2.refs_2_), channel_id=1, source_target_pairs={{0,2},{1,3},{2,0},{3,1},{4,6},{5,7},{6,4},{7,5},{8,10},{9,11},{10,... | collective-permute-start | bytes 368648 | tf_op jit(solution)/shard_map/ppermute | solution.py:47
  58.1 2.0 %collective-permute-start.19 = (bf16[80,768]{1,0:T(8,128)(2,1)S(1)}, bf16[80,768]{1,0:T(8,128)(2,1)S(1)}, u32[]{:S(2)}, u32[]{:S(2)}) collective-permute-start(bf16[80,768]{1,0:T(8,128)(2,1)S(1)} %collective-permute-done.17.refs_6_), channel_id=1, source_target_pairs={{0,2},{1,3},{2,0},{3,1},{4,6},{5,7},{6,4},{7,5},{8,10},{9,11},{10,... | collective-permute-start | bytes 368648 | tf_op jit(solution)/shard_map/ppermute | solution.py:47
  60.2 4.5 %collective-permute-done.16.refs_5_ = bf16[64,768]{1,0:T(8,128)(2,1)S(1)} collective-permute-done((bf16[64,768]{1,0:T(8,128)(2,1)S(1)}, bf16[64,768]{1,0:T(8,128)(2,1)S(1)}, u32[]{:S(2)}, u32[]{:S(2)}) %collective-permute-start.16) | collective-permute-done | bytes 98336 | tf_op jit(solution)/shard_map/ppermute | solution.py:47
  67.5 2.5 %collective-permute-done.20.refs_9_ = bf16[64,768]{1,0:T(8,128)(2,1)S(1)} collective-permute-done((bf16[64,768]{1,0:T(8,128)(2,1)S(1)}, bf16[64,768]{1,0:T(8,128)(2,1)S(1)}, u32[]{:S(2)}, u32[]{:S(2)}) %collective-permute-start.20) | collective-permute-done | bytes 98336 | tf_op jit(solution)/shard_map/ppermute | solution.py:47
  72.2 1.9 %collective-permute-start.31 = (bf16[128,768]{1,0:T(8,128)(2,1)S(1)}, bf16[128,768]{1,0:T(8,128)(2,1)S(1)}, u32[]{:S(2)}, u32[]{:S(2)}) collective-permute-start(bf16[128,768]{1,0:T(8,128)(2,1)S(1)} %get-tuple-element.44), channel_id=1, source_target_pairs={{0,17},{1,16},{2,19},{3,18},{4,21},{5,20},{6,23},{7,22},{8,25},{9,... | collective-permute-start | bytes 589832 | tf_op jit(solution)/shard_map/ppermute | solution.py:47
  76.7 2.1 %attention.1.refs_1_ = f32[128,768]{1,0:T(8,128)S(1)} custom-call(bf16[128,768]{1,0:T(8,128)(2,1)S(1)} %copy-done.4, bf16[128,768]{1,0:T(8,128)(2,1)S(1)} %copy-done.1, bf16[128,768]{1,0:T(8,128)(2,1)S(1)} %copy-done.2), custom_call_target="tpu_custom_call" | custom-call | flops 50331648 | bytes 983040 | tf_op jit(solution)/shard_map/attention/pallas_call | solution.py:57
  78.8 2.1 %collective-permute-done.31.refs_2_ = bf16[128,768]{1,0:T(8,128)(2,1)S(1)} collective-permute-done((bf16[128,768]{1,0:T(8,128)(2,1)S(1)}, bf16[128,768]{1,0:T(8,128)(2,1)S(1)}, u32[]{:S(2)}, u32[]{:S(2)}) %collective-permute-start.31) | collective-permute-done | bytes 196640 | tf_op jit(solution)/shard_map/ppermute | solution.py:47
  80.9 3.5 %collective-permute-done.32.refs_3_ = bf16[128,768]{1,0:T(8,128)(2,1)S(1)} collective-permute-done((bf16[128,768]{1,0:T(8,128)(2,1)S(1)}, bf16[128,768]{1,0:T(8,128)(2,1)S(1)}, u32[]{:S(2)}, u32[]{:S(2)}) %collective-permute-start.32) | collective-permute-done | bytes 196640 | tf_op jit(solution)/shard_map/ppermute | solution.py:47
  (70 shorter events, 19.0 us)
Async XLA Ops:
  0.0 14.5 %collective-permute-start = (bf16[3,48,768]{2,1,0:T(8,128)(2,1)}, bf16[3,48,768]{2,1,0:T(8,128)(2,1)S(1)}, u32[]{:S(2)}, u32[]{:S(2)}) collective-permute-start(bf16[3,48,768]{2,1,0:T(8,128)(2,1)} %weights_ref), channel_id=1, source_target_pairs={{0,4},{1,5},{2,6},{3,7},{4,0},{5,1},{6,2},{7,3},{8,12},{9,13},{10,... | collective-permute-start | bytes 663560 | tf_op jit(solution)/shard_map/ppermute | solution.py:47
  6.0 12.3 %collective-permute-start.7 = (bf16[2,128,768]{2,1,0:T(8,128)(2,1)}, bf16[2,128,768]{2,1,0:T(8,128)(2,1)S(1)}, u32[]{:S(2)}, u32[]{:S(2)}) collective-permute-start(bf16[2,128,768]{2,1,0:T(8,128)(2,1)} %prep.1.pair_ref), channel_id=1, source_target_pairs={{0,16},{1,17},{2,18},{3,19},{4,20},{5,21},{6,22},{7,23},{8,24},{9,... | collective-permute-start | bytes 1179656 | tf_op jit(solution)/shard_map/ppermute | solution.py:47
  7.5 18.9 %collective-permute-start.1 = (bf16[2,128,768]{2,1,0:T(8,128)(2,1)}, bf16[2,128,768]{2,1,0:T(8,128)(2,1)S(1)}, u32[]{:S(2)}, u32[]{:S(2)}) collective-permute-start(bf16[2,128,768]{2,1,0:T(8,128)(2,1)} %prep.1.pair_ref), channel_id=1, source_target_pairs={{0,1},{1,0},{2,3},{3,2},{4,5},{5,4},{6,7},{7,6},{8,9},{9,8},{10,11... | collective-permute-start | bytes 1179656 | tf_op jit(solution)/shard_map/ppermute | solution.py:47
  9.1 17.4 %collective-permute-start.2 = (bf16[2,128,768]{2,1,0:T(8,128)(2,1)}, bf16[2,128,768]{2,1,0:T(8,128)(2,1)S(1)}, u32[]{:S(2)}, u32[]{:S(2)}) collective-permute-start(bf16[2,128,768]{2,1,0:T(8,128)(2,1)} %prep.1.pair_ref), channel_id=1, source_target_pairs={{0,17},{1,16},{2,19},{3,18},{4,21},{5,20},{6,23},{7,22},{8,25},{9,... | collective-permute-start | bytes 1179656 | tf_op jit(solution)/shard_map/ppermute | solution.py:47
  9.5 9.7 %collective-permute-start.5 = (bf16[3,48,768]{2,1,0:T(8,128)(2,1)}, bf16[3,48,768]{2,1,0:T(8,128)(2,1)S(1)}, u32[]{:S(2)}, u32[]{:S(2)}) collective-permute-start(bf16[3,48,768]{2,1,0:T(8,128)(2,1)} %weights_ref), channel_id=1, source_target_pairs={{0,2},{1,3},{2,0},{3,1},{4,6},{5,7},{6,4},{7,5},{8,10},{9,11},{10,... | collective-permute-start | bytes 663560 | tf_op jit(solution)/shard_map/ppermute | solution.py:47
  14.5 9.4 %collective-permute-start.6 = (bf16[3,48,768]{2,1,0:T(8,128)(2,1)S(1)}, bf16[3,48,768]{2,1,0:T(8,128)(2,1)S(1)}, u32[]{:S(2)}, u32[]{:S(2)}) collective-permute-start(bf16[3,48,768]{2,1,0:T(8,128)(2,1)S(1)} %collective-permute-done.refs_6_), channel_id=1, source_target_pairs={{0,2},{1,3},{2,0},{3,1},{4,6},{5,7},{6,4},{7,5},{8,10},{9,11},{10,... | collective-permute-start | bytes 663560 | tf_op jit(solution)/shard_map/ppermute | solution.py:47
  18.3 8.7 %collective-permute-start.9 = (bf16[2,128,768]{2,1,0:T(8,128)(2,1)S(1)}, bf16[2,128,768]{2,1,0:T(8,128)(2,1)S(1)}, u32[]{:S(2)}, u32[]{:S(2)}) collective-permute-start(bf16[2,128,768]{2,1,0:T(8,128)(2,1)S(1)} %collective-permute-done.7.refs_2_), channel_id=1, source_target_pairs={{0,8},{1,9},{2,10},{3,11},{4,12},{5,13},{6,14},{7,15},{8,0},{9,1},... | collective-permute-start | bytes 1179656 | tf_op jit(solution)/shard_map/ppermute | solution.py:47
  30.3 8.9 %collective-permute-start.11 = (bf16[2,80,768]{2,1,0:T(8,128)(2,1)S(1)}, bf16[2,80,768]{2,1,0:T(8,128)(2,1)S(1)}, u32[]{:S(2)}, u32[]{:S(2)}) collective-permute-start(bf16[2,80,768]{2,1,0:T(8,128)(2,1)S(1)} %get-tuple-element.31), channel_id=1, source_target_pairs={{0,2},{1,3},{2,0},{3,1},{4,6},{5,7},{6,4},{7,5},{8,10},{9,11},{10,... | collective-permute-start | bytes 737288 | tf_op jit(solution)/shard_map/ppermute | solution.py:47
  31.9 11.8 %collective-permute-start.13 = (bf16[2,64,768]{2,1,0:T(8,128)(2,1)S(1)}, bf16[2,64,768]{2,1,0:T(8,128)(2,1)S(1)}, u32[]{:S(2)}, u32[]{:S(2)}) collective-permute-start(bf16[2,64,768]{2,1,0:T(8,128)(2,1)S(1)} %get-tuple-element.37), channel_id=1, source_target_pairs={{0,2},{1,3},{2,0},{3,1},{4,6},{5,7},{6,4},{7,5},{8,10},{9,11},{10,... | collective-permute-start | bytes 589832 | tf_op jit(solution)/shard_map/ppermute | solution.py:47
  32.4 11.4 %collective-permute-start.10 = (bf16[128,768]{1,0:T(8,128)(2,1)S(1)}, bf16[128,768]{1,0:T(8,128)(2,1)S(1)}, u32[]{:S(2)}, u32[]{:S(2)}) collective-permute-start(bf16[128,768]{1,0:T(8,128)(2,1)S(1)} %get-tuple-element.41.refs_1_), channel_id=1, source_target_pairs={{0,1},{1,0},{2,3},{3,2},{4,5},{5,4},{6,7},{7,6},{8,9},{9,8},{10,11... | collective-permute-start | bytes 589832 | tf_op jit(solution)/shard_map/ppermute | solution.py:47
  33.9 9.9 %collective-permute-start.27 = (bf16[128,768]{1,0:T(8,128)(2,1)S(1)}, bf16[128,768]{1,0:T(8,128)(2,1)S(1)}, u32[]{:S(2)}, u32[]{:S(2)}) collective-permute-start(bf16[128,768]{1,0:T(8,128)(2,1)S(1)} %get-tuple-element.41.refs_1_), channel_id=1, source_target_pairs={{0,16},{1,17},{2,18},{3,19},{4,20},{5,21},{6,22},{7,23},{8,24},{9,... | collective-permute-start | bytes 589832 | tf_op jit(solution)/shard_map/ppermute | solution.py:47
  39.2 8.4 %collective-permute-start.12 = (bf16[1,80,768]{2,1,0:T(8,128)(2,1)S(1)}, bf16[1,80,768]{2,1,0:T(8,128)(2,1)S(1)}, u32[]{:S(2)}, u32[]{:S(2)}) collective-permute-start(bf16[1,80,768]{2,1,0:T(8,128)(2,1)S(1)} %get-tuple-element.35), channel_id=1, source_target_pairs={{0,4},{1,5},{2,6},{3,7},{4,0},{5,1},{6,2},{7,3},{8,12},{9,13},{10,... | collective-permute-start | bytes 368648 | tf_op jit(solution)/shard_map/ppermute | solution.py:47
  43.7 9.1 %collective-permute-start.14 = (bf16[1,64,768]{2,1,0:T(8,128)(2,1)S(1)}, bf16[1,64,768]{2,1,0:T(8,128)(2,1)S(1)}, u32[]{:S(2)}, u32[]{:S(2)}) collective-permute-start(bf16[1,64,768]{2,1,0:T(8,128)(2,1)S(1)} %get-tuple-element.39), channel_id=1, source_target_pairs={{0,4},{1,5},{2,6},{3,7},{4,0},{5,1},{6,2},{7,3},{8,12},{9,13},{10,... | collective-permute-start | bytes 294920 | tf_op jit(solution)/shard_map/ppermute | solution.py:47
  43.8 21.4 %collective-permute-start.28 = (bf16[128,768]{1,0:T(8,128)(2,1)S(1)}, bf16[128,768]{1,0:T(8,128)(2,1)S(1)}, u32[]{:S(2)}, u32[]{:S(2)}) collective-permute-start(bf16[128,768]{1,0:T(8,128)(2,1)S(1)} %get-tuple-element.41.refs_1_), channel_id=1, source_target_pairs={{0,17},{1,16},{2,19},{3,18},{4,21},{5,20},{6,23},{7,22},{8,25},{9,... | collective-permute-start | bytes 589832 | tf_op jit(solution)/shard_map/ppermute | solution.py:47
  47.8 10.3 %collective-permute-start.17 = (bf16[80,768]{1,0:T(8,128)(2,1)S(1)}, bf16[80,768]{1,0:T(8,128)(2,1)S(1)}, u32[]{:S(2)}, u32[]{:S(2)}) collective-permute-start(bf16[80,768]{1,0:T(8,128)(2,1)S(1)} %step.2.refs_2_), channel_id=1, source_target_pairs={{0,4},{1,5},{2,6},{3,7},{4,0},{5,1},{6,2},{7,3},{8,12},{9,13},{10,... | collective-permute-start | bytes 368648 | tf_op jit(solution)/shard_map/ppermute | solution.py:47
  53.0 7.2 %collective-permute-start.18 = (bf16[64,768]{1,0:T(8,128)(2,1)S(1)}, bf16[64,768]{1,0:T(8,128)(2,1)S(1)}, u32[]{:S(2)}, u32[]{:S(2)}) collective-permute-start(bf16[64,768]{1,0:T(8,128)(2,1)S(1)} %step.3.refs_3_), channel_id=1, source_target_pairs={{0,4},{1,5},{2,6},{3,7},{4,0},{5,1},{6,2},{7,3},{8,12},{9,13},{10,... | collective-permute-start | bytes 294920 | tf_op jit(solution)/shard_map/ppermute | solution.py:47
  53.1 11.6 %collective-permute-start.15 = (bf16[80,768]{1,0:T(8,128)(2,1)S(1)}, bf16[80,768]{1,0:T(8,128)(2,1)S(1)}, u32[]{:S(2)}, u32[]{:S(2)}) collective-permute-start(bf16[80,768]{1,0:T(8,128)(2,1)S(1)} %step.2.refs_2_), channel_id=1, source_target_pairs={{0,2},{1,3},{2,0},{3,1},{4,6},{5,7},{6,4},{7,5},{8,10},{9,11},{10,... | collective-permute-start | bytes 368648 | tf_op jit(solution)/shard_map/ppermute | solution.py:47
  58.1 6.7 %collective-permute-start.16 = (bf16[64,768]{1,0:T(8,128)(2,1)S(1)}, bf16[64,768]{1,0:T(8,128)(2,1)S(1)}, u32[]{:S(2)}, u32[]{:S(2)}) collective-permute-start(bf16[64,768]{1,0:T(8,128)(2,1)S(1)} %step.3.refs_3_), channel_id=1, source_target_pairs={{0,2},{1,3},{2,0},{3,1},{4,6},{5,7},{6,4},{7,5},{8,10},{9,11},{10,... | collective-permute-start | bytes 294920 | tf_op jit(solution)/shard_map/ppermute | solution.py:47
  58.1 8.4 %collective-permute-start.19 = (bf16[80,768]{1,0:T(8,128)(2,1)S(1)}, bf16[80,768]{1,0:T(8,128)(2,1)S(1)}, u32[]{:S(2)}, u32[]{:S(2)}) collective-permute-start(bf16[80,768]{1,0:T(8,128)(2,1)S(1)} %collective-permute-done.17.refs_6_), channel_id=1, source_target_pairs={{0,2},{1,3},{2,0},{3,1},{4,6},{5,7},{6,4},{7,5},{8,10},{9,11},{10,... | collective-permute-start | bytes 368648 | tf_op jit(solution)/shard_map/ppermute | solution.py:47
  60.2 6.8 %collective-permute-start.21 = (bf16[80,768]{1,0:T(8,128)(2,1)S(1)}, bf16[80,768]{1,0:T(8,128)(2,1)S(1)}, u32[]{:S(2)}, u32[]{:S(2)}) collective-permute-start(bf16[80,768]{1,0:T(8,128)(2,1)S(1)} %step.2.refs_2_), channel_id=1, source_target_pairs={{0,8},{1,9},{2,10},{3,11},{4,12},{5,13},{6,14},{7,15},{8,0},{9,1},... | collective-permute-start | bytes 368648 | tf_op jit(solution)/shard_map/ppermute | solution.py:47
  65.2 4.8 %collective-permute-start.20 = (bf16[64,768]{1,0:T(8,128)(2,1)S(1)}, bf16[64,768]{1,0:T(8,128)(2,1)S(1)}, u32[]{:S(2)}, u32[]{:S(2)}) collective-permute-start(bf16[64,768]{1,0:T(8,128)(2,1)S(1)} %collective-permute-done.18.refs_7_), channel_id=1, source_target_pairs={{0,2},{1,3},{2,0},{3,1},{4,6},{5,7},{6,4},{7,5},{8,10},{9,11},{10,... | collective-permute-start | bytes 294920 | tf_op jit(solution)/shard_map/ppermute | solution.py:47
  72.2 8.7 %collective-permute-start.31 = (bf16[128,768]{1,0:T(8,128)(2,1)S(1)}, bf16[128,768]{1,0:T(8,128)(2,1)S(1)}, u32[]{:S(2)}, u32[]{:S(2)}) collective-permute-start(bf16[128,768]{1,0:T(8,128)(2,1)S(1)} %get-tuple-element.44), channel_id=1, source_target_pairs={{0,17},{1,16},{2,19},{3,18},{4,21},{5,20},{6,23},{7,22},{8,25},{9,... | collective-permute-start | bytes 589832 | tf_op jit(solution)/shard_map/ppermute | solution.py:47
  74.1 10.4 %collective-permute-start.32 = (bf16[128,768]{1,0:T(8,128)(2,1)S(1)}, bf16[128,768]{1,0:T(8,128)(2,1)S(1)}, u32[]{:S(2)}, u32[]{:S(2)}) collective-permute-start(bf16[128,768]{1,0:T(8,128)(2,1)S(1)} %get-tuple-element.45), channel_id=1, source_target_pairs={{0,16},{1,17},{2,18},{3,19},{4,20},{5,21},{6,22},{7,23},{8,24},{9,... | collective-permute-start | bytes 589832 | tf_op jit(solution)/shard_map/ppermute | solution.py:47
  76.2 8.3 %collective-permute-start.33 = (bf16[128,768]{1,0:T(8,128)(2,1)S(1)}, bf16[128,768]{1,0:T(8,128)(2,1)S(1)}, u32[]{:S(2)}, u32[]{:S(2)}) collective-permute-start(bf16[128,768]{1,0:T(8,128)(2,1)S(1)} %get-tuple-element.46), channel_id=1, source_target_pairs={{0,1},{1,0},{2,3},{3,2},{4,5},{5,4},{6,7},{7,6},{8,9},{9,8},{10,11... | collective-permute-start | bytes 589832 | tf_op jit(solution)/shard_map/ppermute | solution.py:47
  (16 other events, 101.3 us)

commit v6 on v4

--- a/solution.py
+++ b/solution.py
@@ -358,9 +358,9 @@
         there.append([send(after(array, corner_query), swap) for array in blocks[-1]])
         blocks += there
 
-        outs = apply_rows([corner_query, all_queries[0]], blocks, rows, BF)
-        outs += apply_rows([all_queries[1], query_normed], blocks, rows, F32)
-        back = [send(part, layer(*o)) for part, o in zip(outs[:-1], ((1, 1), (1, 0), (0, 1)))]
+        outs = apply_rows([corner_query, *all_queries], blocks, rows, BF)
+        back = [send(part, layer(*o)) for part, o in zip(outs, ((1, 1), (1, 0), (0, 1)))]
+        outs += apply_rows([query_normed], blocks, rows, F32)
         return call(total_kernel, [struct(queries.shape, BF)], outs[-1], mixed, *back, name="total")[0]
 
     in_specs = (

time: 81.7 us -> 82 us (level)
  transfers between devices with their start and end apart: 34 -> 34, of which waited for: 17 -> 17; matrix products, arithmetic and copies ran while one was open for 0% -> 0% of each run, Pallas kernels for 9% -> 8%
where the time goes in v6:
time: 82 us; the launch traced here: 81.8 us
  waiting for transfers between devices  36.5 us (45%)
  starting transfers between devices  31.9 us (39%)
  Pallas kernels  10.4 us (13%)
  local copies, waits for them, and re-layouts  2.88 us (4%)
    ppermute x34, waiting for transfers between devices, send(): return lax.ppermute(array, AXES, pairs)  36.5 us
    ppermute x34, starting transfers between devices, send(): return lax.ppermute(array, AXES, pairs)  31.9 us
    pallas_call x12, Pallas kernels, call(): pl.pallas_call(kernel, out_shape=list(outs), in_specs=[pl.BlockSpec(memor...  10.4 us
    unnamed x12, local copies, waits for them, and re-layouts  2.87 us
  transfers between devices with their start and end apart: 34, of which 17 were waited for; matrix products, arithmetic and copies ran while one was open for 0% of the time, Pallas kernels for 8%

profile of v6, /device:TPU:0, one launch (start us, length us, event | category | flops | bytes accessed | tf_op | source)
XLA Modules:
  0.0 81.8 jit_solution(13884488889701987044)
XLA Ops:
  0.0 4.0 %collective-permute-start = (bf16[3,48,768]{2,1,0:T(8,128)(2,1)}, bf16[3,48,768]{2,1,0:T(8,128)(2,1)S(1)}, u32[]{:S(2)}, u32[]{:S(2)}) collective-permute-start(bf16[3,48,768]{2,1,0:T(8,128)(2,1)} %weights_ref), channel_id=1, source_target_pairs={{0,4},{1,5},{2,6},{3,7},{4,0},{5,1},{6,2},{7,3},{8,12},{9,13},{10,... | collective-permute-start | bytes 663560 | tf_op jit(solution)/shard_map/ppermute | solution.py:47
  4.0 1.9 %prep.1.pair_ref = bf16[2,128,768]{2,1,0:T(8,128)(2,1)} custom-call(bf16[128,768]{1,0:T(8,128)(2,1)} %key_ref.1, bf16[128,768]{1,0:T(8,128)(2,1)} %value_ref.1, f32[1,128]{1,0:T(1,128)} %bitcast.4), custom_call_target="tpu_custom_call" | custom-call | bytes 786944 | tf_op jit(solution)/shard_map/prep/pallas_call | solution.py:57
  6.0 1.6 %collective-permute-start.7 = (bf16[2,128,768]{2,1,0:T(8,128)(2,1)}, bf16[2,128,768]{2,1,0:T(8,128)(2,1)S(1)}, u32[]{:S(2)}, u32[]{:S(2)}) collective-permute-start(bf16[2,128,768]{2,1,0:T(8,128)(2,1)} %prep.1.pair_ref), channel_id=1, source_target_pairs={{0,16},{1,17},{2,18},{3,19},{4,20},{5,21},{6,22},{7,23},{8,24},{9,... | collective-permute-start | bytes 1179656 | tf_op jit(solution)/shard_map/ppermute | solution.py:47
  7.5 1.5 %collective-permute-start.1 = (bf16[2,128,768]{2,1,0:T(8,128)(2,1)}, bf16[2,128,768]{2,1,0:T(8,128)(2,1)S(1)}, u32[]{:S(2)}, u32[]{:S(2)}) collective-permute-start(bf16[2,128,768]{2,1,0:T(8,128)(2,1)} %prep.1.pair_ref), channel_id=1, source_target_pairs={{0,1},{1,0},{2,3},{3,2},{4,5},{5,4},{6,7},{7,6},{8,9},{9,8},{10,11... | collective-permute-start | bytes 1179656 | tf_op jit(solution)/shard_map/ppermute | solution.py:47
  9.5 1.6 %collective-permute-start.5 = (bf16[3,48,768]{2,1,0:T(8,128)(2,1)}, bf16[3,48,768]{2,1,0:T(8,128)(2,1)S(1)}, u32[]{:S(2)}, u32[]{:S(2)}) collective-permute-start(bf16[3,48,768]{2,1,0:T(8,128)(2,1)} %weights_ref), channel_id=1, source_target_pairs={{0,2},{1,3},{2,0},{3,1},{4,6},{5,7},{6,4},{7,5},{8,10},{9,11},{10,... | collective-permute-start | bytes 663560 | tf_op jit(solution)/shard_map/ppermute | solution.py:47
  11.1 3.4 %collective-permute-done.refs_6_ = bf16[3,48,768]{2,1,0:T(8,128)(2,1)S(1)} collective-permute-done((bf16[3,48,768]{2,1,0:T(8,128)(2,1)}, bf16[3,48,768]{2,1,0:T(8,128)(2,1)S(1)}, u32[]{:S(2)}, u32[]{:S(2)}) %collective-permute-start) | collective-permute-done | bytes 221216 | tf_op jit(solution)/shard_map/ppermute | solution.py:47
  19.2 4.6 %collective-permute-done.6.refs_7_ = bf16[3,48,768]{2,1,0:T(8,128)(2,1)S(1)} collective-permute-done((bf16[3,48,768]{2,1,0:T(8,128)(2,1)S(1)}, bf16[3,48,768]{2,1,0:T(8,128)(2,1)S(1)}, u32[]{:S(2)}, u32[]{:S(2)}) %collective-permute-start.6) | collective-permute-done | bytes 221216 | tf_op jit(solution)/shard_map/ppermute | solution.py:47
  23.9 2.6 %collective-permute-done.1.refs_0_ = bf16[2,128,768]{2,1,0:T(8,128)(2,1)S(1)} collective-permute-done((bf16[2,128,768]{2,1,0:T(8,128)(2,1)}, bf16[2,128,768]{2,1,0:T(8,128)(2,1)S(1)}, u32[]{:S(2)}, u32[]{:S(2)}) %collective-permute-start.1) | collective-permute-done | bytes 393248 | tf_op jit(solution)/shard_map/ppermute | solution.py:47
  27.0 1.6 %gradient_part.1.refs_8_ = f32[576,768]{1,0:T(8,128)S(1)} custom-call(bf16[2,128,768]{2,1,0:T(8,128)(2,1)S(1)} %get-tuple-element.30.refs_0_, bf16[2,128,768]{2,1,0:T(8,128)(2,1)S(1)} %collective-permute-done.8.refs_1_, bf16[2,128,768]{2,1,0:T(8,128)(2,1)S(1)} %collective-permute-done.7.refs_2_, bf16[2,128,768]{2,1,0:T(8,128)(2,1)S(1)} %collective-permute-done.9.refs_3_, ...), custom_call_target="tpu_custom_call" | custom-call | flops 905969664 | bytes 4227072 | tf_op jit(solution)/shard_map/gradient_part/pallas_call | solution.py:57
  28.8 1.5 %gradient.1 = (bf16[2,80,768]{2,1,0:T(8,128)(2,1)S(1)}, f32[2,80,768]{2,1,0:T(8,128)S(1)}, bf16[2,64,768]{2,1,0:T(8,128)(2,1)S(1)}, f32[2,64,768]{2,1,0:T(8,128)S(1)}) custom-call(bf16[2,128,768]{2,1,0:T(8,128)(2,1)S(1)} %collective-permute-done.1.refs_0_, bf16[2,128,768]{2,1,0:T(8,128)(2,1)S(1)} %collective-permute-done.2.refs_1_, ...), custom_call_target="tpu_custom_call" | custom-call | flops 905969664 | bytes 5554176 | tf_op jit(solution)/shard_map/gradient/pallas_call | solution.py:57
  30.3 1.6 %collective-permute-start.10 = (bf16[2,80,768]{2,1,0:T(8,128)(2,1)S(1)}, bf16[2,80,768]{2,1,0:T(8,128)(2,1)S(1)}, u32[]{:S(2)}, u32[]{:S(2)}) collective-permute-start(bf16[2,80,768]{2,1,0:T(8,128)(2,1)S(1)} %get-tuple-element.31), channel_id=1, source_target_pairs={{0,2},{1,3},{2,0},{3,1},{4,6},{5,7},{6,4},{7,5},{8,10},{9,11},{10,... | collective-permute-start | bytes 737288 | tf_op jit(solution)/shard_map/ppermute | solution.py:47
  34.5 4.7 %collective-permute-done.10.arrived_ref = bf16[2,80,768]{2,1,0:T(8,128)(2,1)S(1)} collective-permute-done((bf16[2,80,768]{2,1,0:T(8,128)(2,1)S(1)}, bf16[2,80,768]{2,1,0:T(8,128)(2,1)S(1)}, u32[]{:S(2)}, u32[]{:S(2)}) %collective-permute-start.10) | collective-permute-done | bytes 245792 | tf_op jit(solution)/shard_map/ppermute | solution.py:47
  39.6 4.1 %collective-permute-done.12.arrived_ref = bf16[2,64,768]{2,1,0:T(8,128)(2,1)S(1)} collective-permute-done((bf16[2,64,768]{2,1,0:T(8,128)(2,1)S(1)}, bf16[2,64,768]{2,1,0:T(8,128)(2,1)S(1)}, u32[]{:S(2)}, u32[]{:S(2)}) %collective-permute-start.12) | collective-permute-done | bytes 196640 | tf_op jit(solution)/shard_map/ppermute | solution.py:47
  43.9 1.8 %collective-permute-start.28 = (bf16[128,768]{1,0:T(8,128)(2,1)S(1)}, bf16[128,768]{1,0:T(8,128)(2,1)S(1)}, u32[]{:S(2)}, u32[]{:S(2)}) collective-permute-start(bf16[128,768]{1,0:T(8,128)(2,1)S(1)} %get-tuple-element.41.refs_0_), channel_id=1, source_target_pairs={{0,17},{1,16},{2,19},{3,18},{4,21},{5,20},{6,23},{7,22},{8,25},{9,... | collective-permute-start | bytes 589832 | tf_op jit(solution)/shard_map/ppermute | solution.py:47
  45.7 2.0 %collective-permute-done.11.arrived_ref = bf16[1,80,768]{2,1,0:T(8,128)(2,1)S(1)} collective-permute-done((bf16[1,80,768]{2,1,0:T(8,128)(2,1)S(1)}, bf16[1,80,768]{2,1,0:T(8,128)(2,1)S(1)}, u32[]{:S(2)}, u32[]{:S(2)}) %collective-permute-start.11) | collective-permute-done | bytes 122912 | tf_op jit(solution)/shard_map/ppermute | solution.py:47
  48.8 3.4 %collective-permute-start.14 = (bf16[80,768]{1,0:T(8,128)(2,1)S(1)}, bf16[80,768]{1,0:T(8,128)(2,1)S(1)}, u32[]{:S(2)}, u32[]{:S(2)}) collective-permute-start(bf16[80,768]{1,0:T(8,128)(2,1)S(1)} %step.2.refs_1_.refs_3_), channel_id=1, source_target_pairs={{0,2},{1,3},{2,0},{3,1},{4,6},{5,7},{6,4},{7,5},{8,10},{9,11},{10,... | collective-permute-start | bytes 368648 | tf_op jit(solution)/shard_map/ppermute | solution.py:47
  53.1 4.9 %collective-permute-start.15 = (bf16[64,768]{1,0:T(8,128)(2,1)S(1)}, bf16[64,768]{1,0:T(8,128)(2,1)S(1)}, u32[]{:S(2)}, u32[]{:S(2)}) collective-permute-start(bf16[64,768]{1,0:T(8,128)(2,1)S(1)} %step.3.refs_2_.refs_4_), channel_id=1, source_target_pairs={{0,2},{1,3},{2,0},{3,1},{4,6},{5,7},{6,4},{7,5},{8,10},{9,11},{10,... | collective-permute-start | bytes 294920 | tf_op jit(solution)/shard_map/ppermute | solution.py:47
  58.0 2.4 %collective-permute-done.17.refs_6_.refs_8_ = bf16[64,768]{1,0:T(8,128)(2,1)S(1)} collective-permute-done((bf16[64,768]{1,0:T(8,128)(2,1)S(1)}, bf16[64,768]{1,0:T(8,128)(2,1)S(1)}, u32[]{:S(2)}, u32[]{:S(2)}) %collective-permute-start.17) | collective-permute-done | bytes 98336 | tf_op jit(solution)/shard_map/ppermute | solution.py:47
  61.9 1.5 %collective-permute-done.18.refs_7_.refs_9_ = bf16[80,768]{1,0:T(8,128)(2,1)S(1)} collective-permute-done((bf16[80,768]{1,0:T(8,128)(2,1)S(1)}, bf16[80,768]{1,0:T(8,128)(2,1)S(1)}, u32[]{:S(2)}, u32[]{:S(2)}) %collective-permute-start.18) | collective-permute-done | bytes 122912 | tf_op jit(solution)/shard_map/ppermute | solution.py:47
  63.9 1.8 %collective-permute-done.19.refs_8_.refs_10_ = bf16[64,768]{1,0:T(8,128)(2,1)S(1)} collective-permute-done((bf16[64,768]{1,0:T(8,128)(2,1)S(1)}, bf16[64,768]{1,0:T(8,128)(2,1)S(1)}, u32[]{:S(2)}, u32[]{:S(2)}) %collective-permute-start.19) | collective-permute-done | bytes 98336 | tf_op jit(solution)/shard_map/ppermute | solution.py:47
  68.7 2.1 %collective-permute-start.31 = (bf16[128,768]{1,0:T(8,128)(2,1)S(1)}, bf16[128,768]{1,0:T(8,128)(2,1)S(1)}, u32[]{:S(2)}, u32[]{:S(2)}) collective-permute-start(bf16[128,768]{1,0:T(8,128)(2,1)S(1)} %get-tuple-element.44), channel_id=1, source_target_pairs={{0,17},{1,16},{2,19},{3,18},{4,21},{5,20},{6,23},{7,22},{8,25},{9,... | collective-permute-start | bytes 589832 | tf_op jit(solution)/shard_map/ppermute | solution.py:47
  72.3 2.1 %attention.1.refs_1_ = f32[128,768]{1,0:T(8,128)S(1)} custom-call(bf16[128,768]{1,0:T(8,128)(2,1)S(1)} %copy-done.4, bf16[128,768]{1,0:T(8,128)(2,1)S(1)} %copy-done.1, bf16[128,768]{1,0:T(8,128)(2,1)S(1)} %copy-done.2), custom_call_target="tpu_custom_call" | custom-call | flops 50331648 | bytes 983040 | tf_op jit(solution)/shard_map/attention/pallas_call | solution.py:57
  75.1 2.4 %collective-permute-done.31.refs_2_ = bf16[128,768]{1,0:T(8,128)(2,1)S(1)} collective-permute-done((bf16[128,768]{1,0:T(8,128)(2,1)S(1)}, bf16[128,768]{1,0:T(8,128)(2,1)S(1)}, u32[]{:S(2)}, u32[]{:S(2)}) %collective-permute-start.31) | collective-permute-done | bytes 196640 | tf_op jit(solution)/shard_map/ppermute | solution.py:47
  77.5 3.5 %collective-permute-done.32.refs_3_ = bf16[128,768]{1,0:T(8,128)(2,1)S(1)} collective-permute-done((bf16[128,768]{1,0:T(8,128)(2,1)S(1)}, bf16[128,768]{1,0:T(8,128)(2,1)S(1)}, u32[]{:S(2)}, u32[]{:S(2)}) %collective-permute-start.32) | collective-permute-done | bytes 196640 | tf_op jit(solution)/shard_map/ppermute | solution.py:47
  (70 shorter events, 19.0 us)
Async XLA Ops:
  0.0 14.5 %collective-permute-start = (bf16[3,48,768]{2,1,0:T(8,128)(2,1)}, bf16[3,48,768]{2,1,0:T(8,128)(2,1)S(1)}, u32[]{:S(2)}, u32[]{:S(2)}) collective-permute-start(bf16[3,48,768]{2,1,0:T(8,128)(2,1)} %weights_ref), channel_id=1, source_target_pairs={{0,4},{1,5},{2,6},{3,7},{4,0},{5,1},{6,2},{7,3},{8,12},{9,13},{10,... | collective-permute-start | bytes 663560 | tf_op jit(solution)/shard_map/ppermute | solution.py:47
  6.0 12.3 %collective-permute-start.7 = (bf16[2,128,768]{2,1,0:T(8,128)(2,1)}, bf16[2,128,768]{2,1,0:T(8,128)(2,1)S(1)}, u32[]{:S(2)}, u32[]{:S(2)}) collective-permute-start(bf16[2,128,768]{2,1,0:T(8,128)(2,1)} %prep.1.pair_ref), channel_id=1, source_target_pairs={{0,16},{1,17},{2,18},{3,19},{4,20},{5,21},{6,22},{7,23},{8,24},{9,... | collective-permute-start | bytes 1179656 | tf_op jit(solution)/shard_map/ppermute | solution.py:47
  7.5 18.9 %collective-permute-start.1 = (bf16[2,128,768]{2,1,0:T(8,128)(2,1)}, bf16[2,128,768]{2,1,0:T(8,128)(2,1)S(1)}, u32[]{:S(2)}, u32[]{:S(2)}) collective-permute-start(bf16[2,128,768]{2,1,0:T(8,128)(2,1)} %prep.1.pair_ref), channel_id=1, source_target_pairs={{0,1},{1,0},{2,3},{3,2},{4,5},{5,4},{6,7},{7,6},{8,9},{9,8},{10,11... | collective-permute-start | bytes 1179656 | tf_op jit(solution)/shard_map/ppermute | solution.py:47
  9.1 17.4 %collective-permute-start.2 = (bf16[2,128,768]{2,1,0:T(8,128)(2,1)}, bf16[2,128,768]{2,1,0:T(8,128)(2,1)S(1)}, u32[]{:S(2)}, u32[]{:S(2)}) collective-permute-start(bf16[2,128,768]{2,1,0:T(8,128)(2,1)} %prep.1.pair_ref), channel_id=1, source_target_pairs={{0,17},{1,16},{2,19},{3,18},{4,21},{5,20},{6,23},{7,22},{8,25},{9,... | collective-permute-start | bytes 1179656 | tf_op jit(solution)/shard_map/ppermute | solution.py:47
  9.5 9.7 %collective-permute-start.5 = (bf16[3,48,768]{2,1,0:T(8,128)(2,1)}, bf16[3,48,768]{2,1,0:T(8,128)(2,1)S(1)}, u32[]{:S(2)}, u32[]{:S(2)}) collective-permute-start(bf16[3,48,768]{2,1,0:T(8,128)(2,1)} %weights_ref), channel_id=1, source_target_pairs={{0,2},{1,3},{2,0},{3,1},{4,6},{5,7},{6,4},{7,5},{8,10},{9,11},{10,... | collective-permute-start | bytes 663560 | tf_op jit(solution)/shard_map/ppermute | solution.py:47
  14.5 9.4 %collective-permute-start.6 = (bf16[3,48,768]{2,1,0:T(8,128)(2,1)S(1)}, bf16[3,48,768]{2,1,0:T(8,128)(2,1)S(1)}, u32[]{:S(2)}, u32[]{:S(2)}) collective-permute-start(bf16[3,48,768]{2,1,0:T(8,128)(2,1)S(1)} %collective-permute-done.refs_6_), channel_id=1, source_target_pairs={{0,2},{1,3},{2,0},{3,1},{4,6},{5,7},{6,4},{7,5},{8,10},{9,11},{10,... | collective-permute-start | bytes 663560 | tf_op jit(solution)/shard_map/ppermute | solution.py:47
  18.3 8.7 %collective-permute-start.9 = (bf16[2,128,768]{2,1,0:T(8,128)(2,1)S(1)}, bf16[2,128,768]{2,1,0:T(8,128)(2,1)S(1)}, u32[]{:S(2)}, u32[]{:S(2)}) collective-permute-start(bf16[2,128,768]{2,1,0:T(8,128)(2,1)S(1)} %collective-permute-done.7.refs_2_), channel_id=1, source_target_pairs={{0,8},{1,9},{2,10},{3,11},{4,12},{5,13},{6,14},{7,15},{8,0},{9,1},... | collective-permute-start | bytes 1179656 | tf_op jit(solution)/shard_map/ppermute | solution.py:47
  30.3 8.9 %collective-permute-start.10 = (bf16[2,80,768]{2,1,0:T(8,128)(2,1)S(1)}, bf16[2,80,768]{2,1,0:T(8,128)(2,1)S(1)}, u32[]{:S(2)}, u32[]{:S(2)}) collective-permute-start(bf16[2,80,768]{2,1,0:T(8,128)(2,1)S(1)} %get-tuple-element.31), channel_id=1, source_target_pairs={{0,2},{1,3},{2,0},{3,1},{4,6},{5,7},{6,4},{7,5},{8,10},{9,11},{10,... | collective-permute-start | bytes 737288 | tf_op jit(solution)/shard_map/ppermute | solution.py:47
  31.9 11.8 %collective-permute-start.12 = (bf16[2,64,768]{2,1,0:T(8,128)(2,1)S(1)}, bf16[2,64,768]{2,1,0:T(8,128)(2,1)S(1)}, u32[]{:S(2)}, u32[]{:S(2)}) collective-permute-start(bf16[2,64,768]{2,1,0:T(8,128)(2,1)S(1)} %get-tuple-element.37), channel_id=1, source_target_pairs={{0,2},{1,3},{2,0},{3,1},{4,6},{5,7},{6,4},{7,5},{8,10},{9,11},{10,... | collective-permute-start | bytes 589832 | tf_op jit(solution)/shard_map/ppermute | solution.py:47
  32.4 11.4 %collective-permute-start.26 = (bf16[128,768]{1,0:T(8,128)(2,1)S(1)}, bf16[128,768]{1,0:T(8,128)(2,1)S(1)}, u32[]{:S(2)}, u32[]{:S(2)}) collective-permute-start(bf16[128,768]{1,0:T(8,128)(2,1)S(1)} %get-tuple-element.41.refs_0_), channel_id=1, source_target_pairs={{0,16},{1,17},{2,18},{3,19},{4,20},{5,21},{6,22},{7,23},{8,24},{9,... | collective-permute-start | bytes 589832 | tf_op jit(solution)/shard_map/ppermute | solution.py:47
  33.1 10.8 %collective-permute-start.27 = (bf16[128,768]{1,0:T(8,128)(2,1)S(1)}, bf16[128,768]{1,0:T(8,128)(2,1)S(1)}, u32[]{:S(2)}, u32[]{:S(2)}) collective-permute-start(bf16[128,768]{1,0:T(8,128)(2,1)S(1)} %get-tuple-element.41.refs_0_), channel_id=1, source_target_pairs={{0,1},{1,0},{2,3},{3,2},{4,5},{5,4},{6,7},{7,6},{8,9},{9,8},{10,11... | collective-permute-start | bytes 589832 | tf_op jit(solution)/shard_map/ppermute | solution.py:47
  39.2 8.4 %collective-permute-start.11 = (bf16[1,80,768]{2,1,0:T(8,128)(2,1)S(1)}, bf16[1,80,768]{2,1,0:T(8,128)(2,1)S(1)}, u32[]{:S(2)}, u32[]{:S(2)}) collective-permute-start(bf16[1,80,768]{2,1,0:T(8,128)(2,1)S(1)} %get-tuple-element.35), channel_id=1, source_target_pairs={{0,4},{1,5},{2,6},{3,7},{4,0},{5,1},{6,2},{7,3},{8,12},{9,13},{10,... | collective-permute-start | bytes 368648 | tf_op jit(solution)/shard_map/ppermute | solution.py:47
  43.8 9.1 %collective-permute-start.13 = (bf16[1,64,768]{2,1,0:T(8,128)(2,1)S(1)}, bf16[1,64,768]{2,1,0:T(8,128)(2,1)S(1)}, u32[]{:S(2)}, u32[]{:S(2)}) collective-permute-start(bf16[1,64,768]{2,1,0:T(8,128)(2,1)S(1)} %get-tuple-element.39), channel_id=1, source_target_pairs={{0,4},{1,5},{2,6},{3,7},{4,0},{5,1},{6,2},{7,3},{8,12},{9,13},{10,... | collective-permute-start | bytes 294920 | tf_op jit(solution)/shard_map/ppermute | solution.py:47
  43.9 17.1 %collective-permute-start.28 = (bf16[128,768]{1,0:T(8,128)(2,1)S(1)}, bf16[128,768]{1,0:T(8,128)(2,1)S(1)}, u32[]{:S(2)}, u32[]{:S(2)}) collective-permute-start(bf16[128,768]{1,0:T(8,128)(2,1)S(1)} %get-tuple-element.41.refs_0_), channel_id=1, source_target_pairs={{0,17},{1,16},{2,19},{3,18},{4,21},{5,20},{6,23},{7,22},{8,25},{9,... | collective-permute-start | bytes 589832 | tf_op jit(solution)/shard_map/ppermute | solution.py:47
  47.8 10.2 %collective-permute-start.16 = (bf16[80,768]{1,0:T(8,128)(2,1)S(1)}, bf16[80,768]{1,0:T(8,128)(2,1)S(1)}, u32[]{:S(2)}, u32[]{:S(2)}) collective-permute-start(bf16[80,768]{1,0:T(8,128)(2,1)S(1)} %step.2.refs_1_.refs_3_), channel_id=1, source_target_pairs={{0,4},{1,5},{2,6},{3,7},{4,0},{5,1},{6,2},{7,3},{8,12},{9,13},{10,... | collective-permute-start | bytes 368648 | tf_op jit(solution)/shard_map/ppermute | solution.py:47
  48.8 11.6 %collective-permute-start.14 = (bf16[80,768]{1,0:T(8,128)(2,1)S(1)}, bf16[80,768]{1,0:T(8,128)(2,1)S(1)}, u32[]{:S(2)}, u32[]{:S(2)}) collective-permute-start(bf16[80,768]{1,0:T(8,128)(2,1)S(1)} %step.2.refs_1_.refs_3_), channel_id=1, source_target_pairs={{0,2},{1,3},{2,0},{3,1},{4,6},{5,7},{6,4},{7,5},{8,10},{9,11},{10,... | collective-permute-start | bytes 368648 | tf_op jit(solution)/shard_map/ppermute | solution.py:47
  53.0 7.4 %collective-permute-start.17 = (bf16[64,768]{1,0:T(8,128)(2,1)S(1)}, bf16[64,768]{1,0:T(8,128)(2,1)S(1)}, u32[]{:S(2)}, u32[]{:S(2)}) collective-permute-start(bf16[64,768]{1,0:T(8,128)(2,1)S(1)} %step.3.refs_2_.refs_4_), channel_id=1, source_target_pairs={{0,4},{1,5},{2,6},{3,7},{4,0},{5,1},{6,2},{7,3},{8,12},{9,13},{10,... | collective-permute-start | bytes 294920 | tf_op jit(solution)/shard_map/ppermute | solution.py:47
  53.1 8.8 %collective-permute-start.15 = (bf16[64,768]{1,0:T(8,128)(2,1)S(1)}, bf16[64,768]{1,0:T(8,128)(2,1)S(1)}, u32[]{:S(2)}, u32[]{:S(2)}) collective-permute-start(bf16[64,768]{1,0:T(8,128)(2,1)S(1)} %step.3.refs_2_.refs_4_), channel_id=1, source_target_pairs={{0,2},{1,3},{2,0},{3,1},{4,6},{5,7},{6,4},{7,5},{8,10},{9,11},{10,... | collective-permute-start | bytes 294920 | tf_op jit(solution)/shard_map/ppermute | solution.py:47
  58.0 5.4 %collective-permute-start.18 = (bf16[80,768]{1,0:T(8,128)(2,1)S(1)}, bf16[80,768]{1,0:T(8,128)(2,1)S(1)}, u32[]{:S(2)}, u32[]{:S(2)}) collective-permute-start(bf16[80,768]{1,0:T(8,128)(2,1)S(1)} %collective-permute-done.16.refs_5_.refs_7_), channel_id=1, source_target_pairs={{0,2},{1,3},{2,0},{3,1},{4,6},{5,7},{6,4},{7,5},{8,10},{9,11},{10,... | collective-permute-start | bytes 368648 | tf_op jit(solution)/shard_map/ppermute | solution.py:47
  60.4 5.3 %collective-permute-start.20 = (bf16[80,768]{1,0:T(8,128)(2,1)S(1)}, bf16[80,768]{1,0:T(8,128)(2,1)S(1)}, u32[]{:S(2)}, u32[]{:S(2)}) collective-permute-start(bf16[80,768]{1,0:T(8,128)(2,1)S(1)} %step.2.refs_1_.refs_3_), channel_id=1, source_target_pairs={{0,8},{1,9},{2,10},{3,11},{4,12},{5,13},{6,14},{7,15},{8,0},{9,1},... | collective-permute-start | bytes 368648 | tf_op jit(solution)/shard_map/ppermute | solution.py:47
  61.0 4.8 %collective-permute-start.19 = (bf16[64,768]{1,0:T(8,128)(2,1)S(1)}, bf16[64,768]{1,0:T(8,128)(2,1)S(1)}, u32[]{:S(2)}, u32[]{:S(2)}) collective-permute-start(bf16[64,768]{1,0:T(8,128)(2,1)S(1)} %collective-permute-done.17.refs_6_.refs_8_), channel_id=1, source_target_pairs={{0,2},{1,3},{2,0},{3,1},{4,6},{5,7},{6,4},{7,5},{8,10},{9,11},{10,... | collective-permute-start | bytes 294920 | tf_op jit(solution)/shard_map/ppermute | solution.py:47
  68.7 8.8 %collective-permute-start.31 = (bf16[128,768]{1,0:T(8,128)(2,1)S(1)}, bf16[128,768]{1,0:T(8,128)(2,1)S(1)}, u32[]{:S(2)}, u32[]{:S(2)}) collective-permute-start(bf16[128,768]{1,0:T(8,128)(2,1)S(1)} %get-tuple-element.44), channel_id=1, source_target_pairs={{0,17},{1,16},{2,19},{3,18},{4,21},{5,20},{6,23},{7,22},{8,25},{9,... | collective-permute-start | bytes 589832 | tf_op jit(solution)/shard_map/ppermute | solution.py:47
  70.8 10.1 %collective-permute-start.32 = (bf16[128,768]{1,0:T(8,128)(2,1)S(1)}, bf16[128,768]{1,0:T(8,128)(2,1)S(1)}, u32[]{:S(2)}, u32[]{:S(2)}) collective-permute-start(bf16[128,768]{1,0:T(8,128)(2,1)S(1)} %get-tuple-element.45), channel_id=1, source_target_pairs={{0,16},{1,17},{2,18},{3,19},{4,20},{5,21},{6,22},{7,23},{8,24},{9,... | collective-permute-start | bytes 589832 | tf_op jit(solution)/shard_map/ppermute | solution.py:47
  71.8 9.2 %collective-permute-start.33 = (bf16[128,768]{1,0:T(8,128)(2,1)S(1)}, bf16[128,768]{1,0:T(8,128)(2,1)S(1)}, u32[]{:S(2)}, u32[]{:S(2)}) collective-permute-start(bf16[128,768]{1,0:T(8,128)(2,1)S(1)} %get-tuple-element.46), channel_id=1, source_target_pairs={{0,1},{1,0},{2,3},{3,2},{4,5},{5,4},{6,7},{7,6},{8,9},{9,8},{10,11... | collective-permute-start | bytes 589832 | tf_op jit(solution)/shard_map/ppermute | solution.py:47
  (16 other events, 103.8 us)

commit v7 on v6

--- a/solution.py
+++ b/solution.py
@@ -147,22 +147,25 @@
     count = flat[0].shape[-2]
     number, rows = len(blocks), blocks[0].shape[1]
     aligned = rows % 16 == 0
-    if not aligned:
+    units = number * rows
+    given = before is not None
+    if given:
+        blocks = before
+    elif not aligned:
         blocks = [jnp.concatenate(blocks, axis=1)]
     size = blocks[0].shape[1]
-    units = number * rows
-    given = before is not None
 
     def kernel(*refs):
         token_refs = refs[:len(flat)]
         block_refs = refs[len(flat):len(flat) + len(blocks)]
-        weights = refs[-1]
-        total = refs[-2]
         if given:
-            base = refs[len(flat) + len(blocks)]
-        for i, ref in enumerate(block_refs):
-            for m in range(3):
-                weights[m * units + i * size:m * units + (i + 1) * size] = ref[m]
+            weights, base = block_refs
+            total = refs[-1]
+        else:
+            total, weights = refs[-2:]
+            for i, ref in enumerate(block_refs):
+                for m in range(3):
+                    weights[m * units + i * size:m * units + (i + 1) * size] = ref[m]
 
         def read(place):
             ref, part = token_refs[place[0]], place[1]
@@ -187,7 +190,7 @@
             total[:2 * units] = first
             total[2 * units:] = last
         if given and aligned:
-            out_refs = refs[len(flat) + len(blocks) + 1:-2]
+            out_refs = refs[len(flat) + len(blocks):-1]
             for m, row, span, chunk, place in pieces(rows):
                 for k in range(number):
                     source = total[m * units + k * rows + row:m * units + k * rows + row + span]
@@ -195,19 +198,21 @@
                     out[k // 2, place:place + span] = source.astype(out.dtype)
 
     edges = (cut(rows), 3 * rows - cut(rows))
-    scratch = [pltpu.VMEM((3 * units, D), BF)]
+    scratch = []
     outs = [struct((3 * units, D), F32)]
-    if given and aligned:
-        scratch = [pltpu.VMEM((3 * units, D), F32), *scratch]
+    if not given:
+        outs.append(struct((3 * units, D), BF))
+    elif aligned:
+        scratch = [pltpu.VMEM((3 * units, D), F32)]
         outs = [struct((number // 2, edge, D), kind) for edge in edges for kind in (BF, F32)]
     outs = call(
-        kernel, outs, *flat, *blocks, *([before] if given else []),
+        kernel, outs, *flat, *blocks,
         flops=12 * count * len(tokens) * units * D,
         scratch=scratch,
         name="gradient" if given else "gradient_part",
     )
     if not given:
-        return outs[0]
+        return outs[1], outs[0]
     if aligned:
         return outs[:2], outs[2:]
     total = outs[0].reshape(3, number, rows, D).swapaxes(0, 1).reshape(number, 3 * rows, D)
@@ -358,8 +363,8 @@
         there.append([send(after(array, corner_query), swap) for array in blocks[-1]])
         blocks += there
 
-        outs = apply_rows([corner_query, *all_queries], blocks, rows, BF)
-        back = [send(part, layer(*o)) for part, o in zip(outs, ((1, 1), (1, 0), (0, 1)))]
+        outs = apply_rows([*all_queries, corner_query], blocks, rows, BF)
+        back = [send(part, layer(*o)) for part, o in zip(outs, ((1, 0), (0, 1), (1, 1)))]
         outs += apply_rows([query_normed], blocks, rows, F32)
         return call(total_kernel, [struct(queries.shape, BF)], outs[-1], mixed, *back, name="total")[0]
 

time: 82 us -> 81.9 us (level)
  transfers between devices with their start and end apart: 34 -> 34, of which waited for: 17 -> 18; matrix products, arithmetic and copies ran while one was open for 0% -> 0% of each run, Pallas kernels for 8% -> 8%
where the time goes in v7:
time: 81.9 us; the launch traced here: 81.7 us
  waiting for transfers between devices  36.6 us (45%)
  starting transfers between devices  31.8 us (39%)
  Pallas kernels  10.3 us (13%)
  local copies, waits for them, and re-layouts  2.88 us (4%)
    ppermute x34, waiting for transfers between devices, send(): return lax.ppermute(array, AXES, pairs)  36.6 us
    ppermute x34, starting transfers between devices, send(): return lax.ppermute(array, AXES, pairs)  31.8 us
    pallas_call x12, Pallas kernels, call(): pl.pallas_call(kernel, out_shape=list(outs), in_specs=[pl.BlockSpec(memor...  10.3 us
    unnamed x12, local copies, waits for them, and re-layouts  2.87 us
  transfers between devices with their start and end apart: 34, of which 18 were waited for; matrix products, arithmetic and copies ran while one was open for 0% of the time, Pallas kernels for 8%

profile of v7, /device:TPU:0, one launch (start us, length us, event | category | flops | bytes accessed | tf_op | source)
XLA Modules:
  0.0 81.7 jit_solution(17127028825981958821)
XLA Ops:
  0.0 4.0 %collective-permute-start = (bf16[3,48,768]{2,1,0:T(8,128)(2,1)}, bf16[3,48,768]{2,1,0:T(8,128)(2,1)S(1)}, u32[]{:S(2)}, u32[]{:S(2)}) collective-permute-start(bf16[3,48,768]{2,1,0:T(8,128)(2,1)} %weights_ref), channel_id=1, source_target_pairs={{0,4},{1,5},{2,6},{3,7},{4,0},{5,1},{6,2},{7,3},{8,12},{9,13},{10,... | collective-permute-start | bytes 663560 | tf_op jit(solution)/shard_map/ppermute | solution.py:47
  4.0 1.9 %prep.1.pair_ref = bf16[2,128,768]{2,1,0:T(8,128)(2,1)} custom-call(bf16[128,768]{1,0:T(8,128)(2,1)} %key_ref.1, bf16[128,768]{1,0:T(8,128)(2,1)} %value_ref.1, f32[1,128]{1,0:T(1,128)} %bitcast.4), custom_call_target="tpu_custom_call" | custom-call | bytes 786944 | tf_op jit(solution)/shard_map/prep/pallas_call | solution.py:57
  6.0 1.6 %collective-permute-start.5 = (bf16[2,128,768]{2,1,0:T(8,128)(2,1)}, bf16[2,128,768]{2,1,0:T(8,128)(2,1)S(1)}, u32[]{:S(2)}, u32[]{:S(2)}) collective-permute-start(bf16[2,128,768]{2,1,0:T(8,128)(2,1)} %prep.1.pair_ref), channel_id=1, source_target_pairs={{0,16},{1,17},{2,18},{3,19},{4,20},{5,21},{6,22},{7,23},{8,24},{9,... | collective-permute-start | bytes 1179656 | tf_op jit(solution)/shard_map/ppermute | solution.py:47
  7.5 1.5 %collective-permute-start.1 = (bf16[2,128,768]{2,1,0:T(8,128)(2,1)}, bf16[2,128,768]{2,1,0:T(8,128)(2,1)S(1)}, u32[]{:S(2)}, u32[]{:S(2)}) collective-permute-start(bf16[2,128,768]{2,1,0:T(8,128)(2,1)} %prep.1.pair_ref), channel_id=1, source_target_pairs={{0,1},{1,0},{2,3},{3,2},{4,5},{5,4},{6,7},{7,6},{8,9},{9,8},{10,11... | collective-permute-start | bytes 1179656 | tf_op jit(solution)/shard_map/ppermute | solution.py:47
  9.5 1.6 %collective-permute-start.6 = (bf16[3,48,768]{2,1,0:T(8,128)(2,1)}, bf16[3,48,768]{2,1,0:T(8,128)(2,1)S(1)}, u32[]{:S(2)}, u32[]{:S(2)}) collective-permute-start(bf16[3,48,768]{2,1,0:T(8,128)(2,1)} %weights_ref), channel_id=1, source_target_pairs={{0,2},{1,3},{2,0},{3,1},{4,6},{5,7},{6,4},{7,5},{8,10},{9,11},{10,... | collective-permute-start | bytes 663560 | tf_op jit(solution)/shard_map/ppermute | solution.py:47
  11.1 3.4 %collective-permute-done.refs_6_ = bf16[3,48,768]{2,1,0:T(8,128)(2,1)S(1)} collective-permute-done((bf16[3,48,768]{2,1,0:T(8,128)(2,1)}, bf16[3,48,768]{2,1,0:T(8,128)(2,1)S(1)}, u32[]{:S(2)}, u32[]{:S(2)}) %collective-permute-start) | collective-permute-done | bytes 221216 | tf_op jit(solution)/shard_map/ppermute | solution.py:47
  19.2 4.6 %collective-permute-done.7.refs_7_ = bf16[3,48,768]{2,1,0:T(8,128)(2,1)S(1)} collective-permute-done((bf16[3,48,768]{2,1,0:T(8,128)(2,1)S(1)}, bf16[3,48,768]{2,1,0:T(8,128)(2,1)S(1)}, u32[]{:S(2)}, u32[]{:S(2)}) %collective-permute-start.7) | collective-permute-done | bytes 221216 | tf_op jit(solution)/shard_map/ppermute | solution.py:47
  23.9 2.6 %collective-permute-done.1.refs_0_ = bf16[2,128,768]{2,1,0:T(8,128)(2,1)S(1)} collective-permute-done((bf16[2,128,768]{2,1,0:T(8,128)(2,1)}, bf16[2,128,768]{2,1,0:T(8,128)(2,1)S(1)}, u32[]{:S(2)}, u32[]{:S(2)}) %collective-permute-start.1) | collective-permute-done | bytes 393248 | tf_op jit(solution)/shard_map/ppermute | solution.py:47
  27.0 1.5 %gradient_part.1 = (f32[576,768]{1,0:T(8,128)S(1)}, bf16[576,768]{1,0:T(8,128)(2,1)S(1)}) custom-call(bf16[2,128,768]{2,1,0:T(8,128)(2,1)S(1)} %get-tuple-element.31.refs_0_, bf16[2,128,768]{2,1,0:T(8,128)(2,1)S(1)} %collective-permute-done.8.refs_1_, bf16[2,128,768]{2,1,0:T(8,128)(2,1)S(1)} %collective-permute-done.5.refs_2_, ...), custom_call_target="tpu_custom_call" | custom-call | flops 905969664 | bytes 5111808 | tf_op jit(solution)/shard_map/gradient_part/pallas_call | solution.py:57
  28.8 1.5 %gradient.1 = (bf16[2,80,768]{2,1,0:T(8,128)(2,1)S(1)}, f32[2,80,768]{2,1,0:T(8,128)S(1)}, bf16[2,64,768]{2,1,0:T(8,128)(2,1)S(1)}, f32[2,64,768]{2,1,0:T(8,128)S(1)}) custom-call(bf16[2,128,768]{2,1,0:T(8,128)(2,1)S(1)} %collective-permute-done.1.refs_0_, bf16[2,128,768]{2,1,0:T(8,128)(2,1)S(1)} %collective-permute-done.2.refs_1_, ...), custom_call_target="tpu_custom_call" | custom-call | flops 905969664 | bytes 5554176 | tf_op jit(solution)/shard_map/gradient/pallas_call | solution.py:57
  30.3 1.6 %collective-permute-start.10 = (bf16[2,80,768]{2,1,0:T(8,128)(2,1)S(1)}, bf16[2,80,768]{2,1,0:T(8,128)(2,1)S(1)}, u32[]{:S(2)}, u32[]{:S(2)}) collective-permute-start(bf16[2,80,768]{2,1,0:T(8,128)(2,1)S(1)} %get-tuple-element.35), channel_id=1, source_target_pairs={{0,2},{1,3},{2,0},{3,1},{4,6},{5,7},{6,4},{7,5},{8,10},{9,11},{10,... | collective-permute-start | bytes 737288 | tf_op jit(solution)/shard_map/ppermute | solution.py:47
  34.4 4.7 %collective-permute-done.10.arrived_ref = bf16[2,80,768]{2,1,0:T(8,128)(2,1)S(1)} collective-permute-done((bf16[2,80,768]{2,1,0:T(8,128)(2,1)S(1)}, bf16[2,80,768]{2,1,0:T(8,128)(2,1)S(1)}, u32[]{:S(2)}, u32[]{:S(2)}) %collective-permute-start.10) | collective-permute-done | bytes 245792 | tf_op jit(solution)/shard_map/ppermute | solution.py:47
  39.6 4.1 %collective-permute-done.12.arrived_ref = bf16[2,64,768]{2,1,0:T(8,128)(2,1)S(1)} collective-permute-done((bf16[2,64,768]{2,1,0:T(8,128)(2,1)S(1)}, bf16[2,64,768]{2,1,0:T(8,128)(2,1)S(1)}, u32[]{:S(2)}, u32[]{:S(2)}) %collective-permute-start.12) | collective-permute-done | bytes 196640 | tf_op jit(solution)/shard_map/ppermute | solution.py:47
  43.8 1.8 %collective-permute-start.28 = (bf16[128,768]{1,0:T(8,128)(2,1)S(1)}, bf16[128,768]{1,0:T(8,128)(2,1)S(1)}, u32[]{:S(2)}, u32[]{:S(2)}) collective-permute-start(bf16[128,768]{1,0:T(8,128)(2,1)S(1)} %get-tuple-element.45.refs_0_), channel_id=1, source_target_pairs={{0,17},{1,16},{2,19},{3,18},{4,21},{5,20},{6,23},{7,22},{8,25},{9,... | collective-permute-start | bytes 589832 | tf_op jit(solution)/shard_map/ppermute | solution.py:47
  45.6 2.0 %collective-permute-done.11.arrived_ref = bf16[1,80,768]{2,1,0:T(8,128)(2,1)S(1)} collective-permute-done((bf16[1,80,768]{2,1,0:T(8,128)(2,1)S(1)}, bf16[1,80,768]{2,1,0:T(8,128)(2,1)S(1)}, u32[]{:S(2)}, u32[]{:S(2)}) %collective-permute-start.11) | collective-permute-done | bytes 122912 | tf_op jit(solution)/shard_map/ppermute | solution.py:47
  48.8 3.4 %collective-permute-start.14 = (bf16[80,768]{1,0:T(8,128)(2,1)S(1)}, bf16[80,768]{1,0:T(8,128)(2,1)S(1)}, u32[]{:S(2)}, u32[]{:S(2)}) collective-permute-start(bf16[80,768]{1,0:T(8,128)(2,1)S(1)} %step.2.refs_1_.refs_3_), channel_id=1, source_target_pairs={{0,2},{1,3},{2,0},{3,1},{4,6},{5,7},{6,4},{7,5},{8,10},{9,11},{10,... | collective-permute-start | bytes 368648 | tf_op jit(solution)/shard_map/ppermute | solution.py:47
  53.0 5.0 %collective-permute-start.15 = (bf16[64,768]{1,0:T(8,128)(2,1)S(1)}, bf16[64,768]{1,0:T(8,128)(2,1)S(1)}, u32[]{:S(2)}, u32[]{:S(2)}) collective-permute-start(bf16[64,768]{1,0:T(8,128)(2,1)S(1)} %step.3.refs_2_.refs_4_), channel_id=1, source_target_pairs={{0,2},{1,3},{2,0},{3,1},{4,6},{5,7},{6,4},{7,5},{8,10},{9,11},{10,... | collective-permute-start | bytes 294920 | tf_op jit(solution)/shard_map/ppermute | solution.py:47
  58.0 2.4 %collective-permute-done.17.refs_6_.refs_8_ = bf16[64,768]{1,0:T(8,128)(2,1)S(1)} collective-permute-done((bf16[64,768]{1,0:T(8,128)(2,1)S(1)}, bf16[64,768]{1,0:T(8,128)(2,1)S(1)}, u32[]{:S(2)}, u32[]{:S(2)}) %collective-permute-start.17) | collective-permute-done | bytes 98336 | tf_op jit(solution)/shard_map/ppermute | solution.py:47
  61.9 1.5 %collective-permute-done.18.refs_7_.refs_9_ = bf16[80,768]{1,0:T(8,128)(2,1)S(1)} collective-permute-done((bf16[80,768]{1,0:T(8,128)(2,1)S(1)}, bf16[80,768]{1,0:T(8,128)(2,1)S(1)}, u32[]{:S(2)}, u32[]{:S(2)}) %collective-permute-start.18) | collective-permute-done | bytes 122912 | tf_op jit(solution)/shard_map/ppermute | solution.py:47
  63.9 1.8 %collective-permute-done.19.refs_8_.refs_10_ = bf16[64,768]{1,0:T(8,128)(2,1)S(1)} collective-permute-done((bf16[64,768]{1,0:T(8,128)(2,1)S(1)}, bf16[64,768]{1,0:T(8,128)(2,1)S(1)}, u32[]{:S(2)}, u32[]{:S(2)}) %collective-permute-start.19) | collective-permute-done | bytes 98336 | tf_op jit(solution)/shard_map/ppermute | solution.py:47
  69.9 1.4 %collective-permute-start.32 = (bf16[128,768]{1,0:T(8,128)(2,1)S(1)}, bf16[128,768]{1,0:T(8,128)(2,1)S(1)}, u32[]{:S(2)}, u32[]{:S(2)}) collective-permute-start(bf16[128,768]{1,0:T(8,128)(2,1)S(1)} %get-tuple-element.49), channel_id=1, source_target_pairs={{0,1},{1,0},{2,3},{3,2},{4,5},{5,4},{6,7},{7,6},{8,9},{9,8},{10,11... | collective-permute-start | bytes 589832 | tf_op jit(solution)/shard_map/ppermute | solution.py:47
  72.3 2.1 %attention.1.refs_1_ = f32[128,768]{1,0:T(8,128)S(1)} custom-call(bf16[128,768]{1,0:T(8,128)(2,1)S(1)} %copy-done.4, bf16[128,768]{1,0:T(8,128)(2,1)S(1)} %copy-done.1, bf16[128,768]{1,0:T(8,128)(2,1)S(1)} %copy-done.2), custom_call_target="tpu_custom_call" | custom-call | flops 50331648 | bytes 983040 | tf_op jit(solution)/shard_map/attention/pallas_call | solution.py:57
  75.1 1.4 %collective-permute-done.31.refs_2_ = bf16[128,768]{1,0:T(8,128)(2,1)S(1)} collective-permute-done((bf16[128,768]{1,0:T(8,128)(2,1)S(1)}, bf16[128,768]{1,0:T(8,128)(2,1)S(1)}, u32[]{:S(2)}, u32[]{:S(2)}) %collective-permute-start.31) | collective-permute-done | bytes 196640 | tf_op jit(solution)/shard_map/ppermute | solution.py:47
  76.5 3.2 %collective-permute-done.32.refs_3_ = bf16[128,768]{1,0:T(8,128)(2,1)S(1)} collective-permute-done((bf16[128,768]{1,0:T(8,128)(2,1)S(1)}, bf16[128,768]{1,0:T(8,128)(2,1)S(1)}, u32[]{:S(2)}, u32[]{:S(2)}) %collective-permute-start.32) | collective-permute-done | bytes 196640 | tf_op jit(solution)/shard_map/ppermute | solution.py:47
  (70 shorter events, 20.8 us)
Async XLA Ops:
  0.0 14.5 %collective-permute-start = (bf16[3,48,768]{2,1,0:T(8,128)(2,1)}, bf16[3,48,768]{2,1,0:T(8,128)(2,1)S(1)}, u32[]{:S(2)}, u32[]{:S(2)}) collective-permute-start(bf16[3,48,768]{2,1,0:T(8,128)(2,1)} %weights_ref), channel_id=1, source_target_pairs={{0,4},{1,5},{2,6},{3,7},{4,0},{5,1},{6,2},{7,3},{8,12},{9,13},{10,... | collective-permute-start | bytes 663560 | tf_op jit(solution)/shard_map/ppermute | solution.py:47
  6.0 12.3 %collective-permute-start.5 = (bf16[2,128,768]{2,1,0:T(8,128)(2,1)}, bf16[2,128,768]{2,1,0:T(8,128)(2,1)S(1)}, u32[]{:S(2)}, u32[]{:S(2)}) collective-permute-start(bf16[2,128,768]{2,1,0:T(8,128)(2,1)} %prep.1.pair_ref), channel_id=1, source_target_pairs={{0,16},{1,17},{2,18},{3,19},{4,20},{5,21},{6,22},{7,23},{8,24},{9,... | collective-permute-start | bytes 1179656 | tf_op jit(solution)/shard_map/ppermute | solution.py:47
  7.5 18.9 %collective-permute-start.1 = (bf16[2,128,768]{2,1,0:T(8,128)(2,1)}, bf16[2,128,768]{2,1,0:T(8,128)(2,1)S(1)}, u32[]{:S(2)}, u32[]{:S(2)}) collective-permute-start(bf16[2,128,768]{2,1,0:T(8,128)(2,1)} %prep.1.pair_ref), channel_id=1, source_target_pairs={{0,1},{1,0},{2,3},{3,2},{4,5},{5,4},{6,7},{7,6},{8,9},{9,8},{10,11... | collective-permute-start | bytes 1179656 | tf_op jit(solution)/shard_map/ppermute | solution.py:47
  9.1 17.4 %collective-permute-start.2 = (bf16[2,128,768]{2,1,0:T(8,128)(2,1)}, bf16[2,128,768]{2,1,0:T(8,128)(2,1)S(1)}, u32[]{:S(2)}, u32[]{:S(2)}) collective-permute-start(bf16[2,128,768]{2,1,0:T(8,128)(2,1)} %prep.1.pair_ref), channel_id=1, source_target_pairs={{0,17},{1,16},{2,19},{3,18},{4,21},{5,20},{6,23},{7,22},{8,25},{9,... | collective-permute-start | bytes 1179656 | tf_op jit(solution)/shard_map/ppermute | solution.py:47
  9.5 9.7 %collective-permute-start.6 = (bf16[3,48,768]{2,1,0:T(8,128)(2,1)}, bf16[3,48,768]{2,1,0:T(8,128)(2,1)S(1)}, u32[]{:S(2)}, u32[]{:S(2)}) collective-permute-start(bf16[3,48,768]{2,1,0:T(8,128)(2,1)} %weights_ref), channel_id=1, source_target_pairs={{0,2},{1,3},{2,0},{3,1},{4,6},{5,7},{6,4},{7,5},{8,10},{9,11},{10,... | collective-permute-start | bytes 663560 | tf_op jit(solution)/shard_map/ppermute | solution.py:47
  14.5 9.4 %collective-permute-start.7 = (bf16[3,48,768]{2,1,0:T(8,128)(2,1)S(1)}, bf16[3,48,768]{2,1,0:T(8,128)(2,1)S(1)}, u32[]{:S(2)}, u32[]{:S(2)}) collective-permute-start(bf16[3,48,768]{2,1,0:T(8,128)(2,1)S(1)} %collective-permute-done.refs_6_), channel_id=1, source_target_pairs={{0,2},{1,3},{2,0},{3,1},{4,6},{5,7},{6,4},{7,5},{8,10},{9,11},{10,... | collective-permute-start | bytes 663560 | tf_op jit(solution)/shard_map/ppermute | solution.py:47
  18.3 8.7 %collective-permute-start.9 = (bf16[2,128,768]{2,1,0:T(8,128)(2,1)S(1)}, bf16[2,128,768]{2,1,0:T(8,128)(2,1)S(1)}, u32[]{:S(2)}, u32[]{:S(2)}) collective-permute-start(bf16[2,128,768]{2,1,0:T(8,128)(2,1)S(1)} %collective-permute-done.5.refs_2_), channel_id=1, source_target_pairs={{0,8},{1,9},{2,10},{3,11},{4,12},{5,13},{6,14},{7,15},{8,0},{9,1},... | collective-permute-start | bytes 1179656 | tf_op jit(solution)/shard_map/ppermute | solution.py:47
  30.3 8.9 %collective-permute-start.10 = (bf16[2,80,768]{2,1,0:T(8,128)(2,1)S(1)}, bf16[2,80,768]{2,1,0:T(8,128)(2,1)S(1)}, u32[]{:S(2)}, u32[]{:S(2)}) collective-permute-start(bf16[2,80,768]{2,1,0:T(8,128)(2,1)S(1)} %get-tuple-element.35), channel_id=1, source_target_pairs={{0,2},{1,3},{2,0},{3,1},{4,6},{5,7},{6,4},{7,5},{8,10},{9,11},{10,... | collective-permute-start | bytes 737288 | tf_op jit(solution)/shard_map/ppermute | solution.py:47
  31.9 11.8 %collective-permute-start.12 = (bf16[2,64,768]{2,1,0:T(8,128)(2,1)S(1)}, bf16[2,64,768]{2,1,0:T(8,128)(2,1)S(1)}, u32[]{:S(2)}, u32[]{:S(2)}) collective-permute-start(bf16[2,64,768]{2,1,0:T(8,128)(2,1)S(1)} %get-tuple-element.41), channel_id=1, source_target_pairs={{0,2},{1,3},{2,0},{3,1},{4,6},{5,7},{6,4},{7,5},{8,10},{9,11},{10,... | collective-permute-start | bytes 589832 | tf_op jit(solution)/shard_map/ppermute | solution.py:47
  32.4 11.4 %collective-permute-start.26 = (bf16[128,768]{1,0:T(8,128)(2,1)S(1)}, bf16[128,768]{1,0:T(8,128)(2,1)S(1)}, u32[]{:S(2)}, u32[]{:S(2)}) collective-permute-start(bf16[128,768]{1,0:T(8,128)(2,1)S(1)} %get-tuple-element.45.refs_0_), channel_id=1, source_target_pairs={{0,16},{1,17},{2,18},{3,19},{4,20},{5,21},{6,22},{7,23},{8,24},{9,... | collective-permute-start | bytes 589832 | tf_op jit(solution)/shard_map/ppermute | solution.py:47
  33.1 10.8 %collective-permute-start.27 = (bf16[128,768]{1,0:T(8,128)(2,1)S(1)}, bf16[128,768]{1,0:T(8,128)(2,1)S(1)}, u32[]{:S(2)}, u32[]{:S(2)}) collective-permute-start(bf16[128,768]{1,0:T(8,128)(2,1)S(1)} %get-tuple-element.45.refs_0_), channel_id=1, source_target_pairs={{0,1},{1,0},{2,3},{3,2},{4,5},{5,4},{6,7},{7,6},{8,9},{9,8},{10,11... | collective-permute-start | bytes 589832 | tf_op jit(solution)/shard_map/ppermute | solution.py:47
  39.2 8.4 %collective-permute-start.11 = (bf16[1,80,768]{2,1,0:T(8,128)(2,1)S(1)}, bf16[1,80,768]{2,1,0:T(8,128)(2,1)S(1)}, u32[]{:S(2)}, u32[]{:S(2)}) collective-permute-start(bf16[1,80,768]{2,1,0:T(8,128)(2,1)S(1)} %get-tuple-element.39), channel_id=1, source_target_pairs={{0,4},{1,5},{2,6},{3,7},{4,0},{5,1},{6,2},{7,3},{8,12},{9,13},{10,... | collective-permute-start | bytes 368648 | tf_op jit(solution)/shard_map/ppermute | solution.py:47
  43.7 9.1 %collective-permute-start.13 = (bf16[1,64,768]{2,1,0:T(8,128)(2,1)S(1)}, bf16[1,64,768]{2,1,0:T(8,128)(2,1)S(1)}, u32[]{:S(2)}, u32[]{:S(2)}) collective-permute-start(bf16[1,64,768]{2,1,0:T(8,128)(2,1)S(1)} %get-tuple-element.43), channel_id=1, source_target_pairs={{0,4},{1,5},{2,6},{3,7},{4,0},{5,1},{6,2},{7,3},{8,12},{9,13},{10,... | collective-permute-start | bytes 294920 | tf_op jit(solution)/shard_map/ppermute | solution.py:47
  43.8 17.1 %collective-permute-start.28 = (bf16[128,768]{1,0:T(8,128)(2,1)S(1)}, bf16[128,768]{1,0:T(8,128)(2,1)S(1)}, u32[]{:S(2)}, u32[]{:S(2)}) collective-permute-start(bf16[128,768]{1,0:T(8,128)(2,1)S(1)} %get-tuple-element.45.refs_0_), channel_id=1, source_target_pairs={{0,17},{1,16},{2,19},{3,18},{4,21},{5,20},{6,23},{7,22},{8,25},{9,... | collective-permute-start | bytes 589832 | tf_op jit(solution)/shard_map/ppermute | solution.py:47
  47.8 10.2 %collective-permute-start.16 = (bf16[80,768]{1,0:T(8,128)(2,1)S(1)}, bf16[80,768]{1,0:T(8,128)(2,1)S(1)}, u32[]{:S(2)}, u32[]{:S(2)}) collective-permute-start(bf16[80,768]{1,0:T(8,128)(2,1)S(1)} %step.2.refs_1_.refs_3_), channel_id=1, source_target_pairs={{0,4},{1,5},{2,6},{3,7},{4,0},{5,1},{6,2},{7,3},{8,12},{9,13},{10,... | collective-permute-start | bytes 368648 | tf_op jit(solution)/shard_map/ppermute | solution.py:47
  48.8 11.6 %collective-permute-start.14 = (bf16[80,768]{1,0:T(8,128)(2,1)S(1)}, bf16[80,768]{1,0:T(8,128)(2,1)S(1)}, u32[]{:S(2)}, u32[]{:S(2)}) collective-permute-start(bf16[80,768]{1,0:T(8,128)(2,1)S(1)} %step.2.refs_1_.refs_3_), channel_id=1, source_target_pairs={{0,2},{1,3},{2,0},{3,1},{4,6},{5,7},{6,4},{7,5},{8,10},{9,11},{10,... | collective-permute-start | bytes 368648 | tf_op jit(solution)/shard_map/ppermute | solution.py:47
  53.0 7.5 %collective-permute-start.17 = (bf16[64,768]{1,0:T(8,128)(2,1)S(1)}, bf16[64,768]{1,0:T(8,128)(2,1)S(1)}, u32[]{:S(2)}, u32[]{:S(2)}) collective-permute-start(bf16[64,768]{1,0:T(8,128)(2,1)S(1)} %step.3.refs_2_.refs_4_), channel_id=1, source_target_pairs={{0,4},{1,5},{2,6},{3,7},{4,0},{5,1},{6,2},{7,3},{8,12},{9,13},{10,... | collective-permute-start | bytes 294920 | tf_op jit(solution)/shard_map/ppermute | solution.py:47
  53.0 8.9 %collective-permute-start.15 = (bf16[64,768]{1,0:T(8,128)(2,1)S(1)}, bf16[64,768]{1,0:T(8,128)(2,1)S(1)}, u32[]{:S(2)}, u32[]{:S(2)}) collective-permute-start(bf16[64,768]{1,0:T(8,128)(2,1)S(1)} %step.3.refs_2_.refs_4_), channel_id=1, source_target_pairs={{0,2},{1,3},{2,0},{3,1},{4,6},{5,7},{6,4},{7,5},{8,10},{9,11},{10,... | collective-permute-start | bytes 294920 | tf_op jit(solution)/shard_map/ppermute | solution.py:47
  58.0 5.4 %collective-permute-start.18 = (bf16[80,768]{1,0:T(8,128)(2,1)S(1)}, bf16[80,768]{1,0:T(8,128)(2,1)S(1)}, u32[]{:S(2)}, u32[]{:S(2)}) collective-permute-start(bf16[80,768]{1,0:T(8,128)(2,1)S(1)} %collective-permute-done.16.refs_5_.refs_7_), channel_id=1, source_target_pairs={{0,2},{1,3},{2,0},{3,1},{4,6},{5,7},{6,4},{7,5},{8,10},{9,11},{10,... | collective-permute-start | bytes 368648 | tf_op jit(solution)/shard_map/ppermute | solution.py:47
  60.4 5.3 %collective-permute-start.20 = (bf16[80,768]{1,0:T(8,128)(2,1)S(1)}, bf16[80,768]{1,0:T(8,128)(2,1)S(1)}, u32[]{:S(2)}, u32[]{:S(2)}) collective-permute-start(bf16[80,768]{1,0:T(8,128)(2,1)S(1)} %step.2.refs_1_.refs_3_), channel_id=1, source_target_pairs={{0,8},{1,9},{2,10},{3,11},{4,12},{5,13},{6,14},{7,15},{8,0},{9,1},... | collective-permute-start | bytes 368648 | tf_op jit(solution)/shard_map/ppermute | solution.py:47
  60.9 4.8 %collective-permute-start.19 = (bf16[64,768]{1,0:T(8,128)(2,1)S(1)}, bf16[64,768]{1,0:T(8,128)(2,1)S(1)}, u32[]{:S(2)}, u32[]{:S(2)}) collective-permute-start(bf16[64,768]{1,0:T(8,128)(2,1)S(1)} %collective-permute-done.17.refs_6_.refs_8_), channel_id=1, source_target_pairs={{0,2},{1,3},{2,0},{3,1},{4,6},{5,7},{6,4},{7,5},{8,10},{9,11},{10,... | collective-permute-start | bytes 294920 | tf_op jit(solution)/shard_map/ppermute | solution.py:47
  68.7 7.8 %collective-permute-start.31 = (bf16[128,768]{1,0:T(8,128)(2,1)S(1)}, bf16[128,768]{1,0:T(8,128)(2,1)S(1)}, u32[]{:S(2)}, u32[]{:S(2)}) collective-permute-start(bf16[128,768]{1,0:T(8,128)(2,1)S(1)} %get-tuple-element.48), channel_id=1, source_target_pairs={{0,16},{1,17},{2,18},{3,19},{4,20},{5,21},{6,22},{7,23},{8,24},{9,... | collective-permute-start | bytes 589832 | tf_op jit(solution)/shard_map/ppermute | solution.py:47
  69.9 9.8 %collective-permute-start.32 = (bf16[128,768]{1,0:T(8,128)(2,1)S(1)}, bf16[128,768]{1,0:T(8,128)(2,1)S(1)}, u32[]{:S(2)}, u32[]{:S(2)}) collective-permute-start(bf16[128,768]{1,0:T(8,128)(2,1)S(1)} %get-tuple-element.49), channel_id=1, source_target_pairs={{0,1},{1,0},{2,3},{3,2},{4,5},{5,4},{6,7},{7,6},{8,9},{9,8},{10,11... | collective-permute-start | bytes 589832 | tf_op jit(solution)/shard_map/ppermute | solution.py:47
  71.3 9.6 %collective-permute-start.33 = (bf16[128,768]{1,0:T(8,128)(2,1)S(1)}, bf16[128,768]{1,0:T(8,128)(2,1)S(1)}, u32[]{:S(2)}, u32[]{:S(2)}) collective-permute-start(bf16[128,768]{1,0:T(8,128)(2,1)S(1)} %get-tuple-element.50), channel_id=1, source_target_pairs={{0,17},{1,16},{2,19},{3,18},{4,21},{5,20},{6,23},{7,22},{8,25},{9,... | collective-permute-start | bytes 589832 | tf_op jit(solution)/shard_map/ppermute | solution.py:47
  (16 other events, 103.7 us)

commit v8 on v7

--- a/solution.py
+++ b/solution.py
@@ -363,9 +363,9 @@
         there.append([send(after(array, corner_query), swap) for array in blocks[-1]])
         blocks += there
 
-        outs = apply_rows([*all_queries, corner_query], blocks, rows, BF)
+        outs = apply_rows(all_queries, blocks, rows, BF)
+        outs += apply_rows([corner_query, query_normed], blocks, rows, F32)
         back = [send(part, layer(*o)) for part, o in zip(outs, ((1, 0), (0, 1), (1, 1)))]
-        outs += apply_rows([query_normed], blocks, rows, F32)
         return call(total_kernel, [struct(queries.shape, BF)], outs[-1], mixed, *back, name="total")[0]
 
     in_specs = (

time: 81.9 us -> 81.7 us (level)
  transfers between devices with their start and end apart: 34 -> 34, of which waited for: 18 -> 18; matrix products, arithmetic and copies ran while one was open for 0% -> 0% of each run, Pallas kernels for 8% -> 9%
where the time goes in v8:
time: 81.7 us; the launch traced here: 81.4 us
  waiting for transfers between devices  36.2 us (44%)
  starting transfers between devices  32 us (39%)
  Pallas kernels  10.2 us (12%)
  local copies, waits for them, and re-layouts  2.89 us (4%)
    ppermute x34, waiting for transfers between devices, send(): return lax.ppermute(array, AXES, pairs)  36.2 us
    ppermute x34, starting transfers between devices, send(): return lax.ppermute(array, AXES, pairs)  32 us
    pallas_call x12, Pallas kernels, call(): pl.pallas_call(kernel, out_shape=list(outs), in_specs=[pl.BlockSpec(memor...  10.2 us
    unnamed x12, local copies, waits for them, and re-layouts  2.88 us
  transfers between devices with their start and end apart: 34, of which 18 were waited for; matrix products, arithmetic and copies ran while one was open for 0% of the time, Pallas kernels for 9%

profile of v8, /device:TPU:0, one launch (start us, length us, event | category | flops | bytes accessed | tf_op | source)
XLA Modules:
  0.0 81.4 jit_solution(16225786829590750446)
XLA Ops:
  0.0 4.0 %collective-permute-start = (bf16[3,48,768]{2,1,0:T(8,128)(2,1)}, bf16[3,48,768]{2,1,0:T(8,128)(2,1)S(1)}, u32[]{:S(2)}, u32[]{:S(2)}) collective-permute-start(bf16[3,48,768]{2,1,0:T(8,128)(2,1)} %weights_ref), channel_id=1, source_target_pairs={{0,4},{1,5},{2,6},{3,7},{4,0},{5,1},{6,2},{7,3},{8,12},{9,13},{10,... | collective-permute-start | bytes 663560 | tf_op jit(solution)/shard_map/ppermute | solution.py:47
  4.0 2.0 %prep.1.pair_ref = bf16[2,128,768]{2,1,0:T(8,128)(2,1)} custom-call(bf16[128,768]{1,0:T(8,128)(2,1)} %key_ref.1, bf16[128,768]{1,0:T(8,128)(2,1)} %value_ref.1, f32[1,128]{1,0:T(1,128)} %bitcast.4), custom_call_target="tpu_custom_call" | custom-call | bytes 786944 | tf_op jit(solution)/shard_map/prep/pallas_call | solution.py:57
  6.0 1.6 %collective-permute-start.5 = (bf16[2,128,768]{2,1,0:T(8,128)(2,1)}, bf16[2,128,768]{2,1,0:T(8,128)(2,1)S(1)}, u32[]{:S(2)}, u32[]{:S(2)}) collective-permute-start(bf16[2,128,768]{2,1,0:T(8,128)(2,1)} %prep.1.pair_ref), channel_id=1, source_target_pairs={{0,16},{1,17},{2,18},{3,19},{4,20},{5,21},{6,22},{7,23},{8,24},{9,... | collective-permute-start | bytes 1179656 | tf_op jit(solution)/shard_map/ppermute | solution.py:47
  7.6 1.5 %collective-permute-start.1 = (bf16[2,128,768]{2,1,0:T(8,128)(2,1)}, bf16[2,128,768]{2,1,0:T(8,128)(2,1)S(1)}, u32[]{:S(2)}, u32[]{:S(2)}) collective-permute-start(bf16[2,128,768]{2,1,0:T(8,128)(2,1)} %prep.1.pair_ref), channel_id=1, source_target_pairs={{0,1},{1,0},{2,3},{3,2},{4,5},{5,4},{6,7},{7,6},{8,9},{9,8},{10,11... | collective-permute-start | bytes 1179656 | tf_op jit(solution)/shard_map/ppermute | solution.py:47
  9.6 1.6 %collective-permute-start.6 = (bf16[3,48,768]{2,1,0:T(8,128)(2,1)}, bf16[3,48,768]{2,1,0:T(8,128)(2,1)S(1)}, u32[]{:S(2)}, u32[]{:S(2)}) collective-permute-start(bf16[3,48,768]{2,1,0:T(8,128)(2,1)} %weights_ref), channel_id=1, source_target_pairs={{0,2},{1,3},{2,0},{3,1},{4,6},{5,7},{6,4},{7,5},{8,10},{9,11},{10,... | collective-permute-start | bytes 663560 | tf_op jit(solution)/shard_map/ppermute | solution.py:47
  11.1 3.4 %collective-permute-done.refs_6_ = bf16[3,48,768]{2,1,0:T(8,128)(2,1)S(1)} collective-permute-done((bf16[3,48,768]{2,1,0:T(8,128)(2,1)}, bf16[3,48,768]{2,1,0:T(8,128)(2,1)S(1)}, u32[]{:S(2)}, u32[]{:S(2)}) %collective-permute-start) | collective-permute-done | bytes 221216 | tf_op jit(solution)/shard_map/ppermute | solution.py:47
  19.2 4.6 %collective-permute-done.7.refs_7_ = bf16[3,48,768]{2,1,0:T(8,128)(2,1)S(1)} collective-permute-done((bf16[3,48,768]{2,1,0:T(8,128)(2,1)S(1)}, bf16[3,48,768]{2,1,0:T(8,128)(2,1)S(1)}, u32[]{:S(2)}, u32[]{:S(2)}) %collective-permute-start.7) | collective-permute-done | bytes 221216 | tf_op jit(solution)/shard_map/ppermute | solution.py:47
  23.9 2.6 %collective-permute-done.1.refs_0_ = bf16[2,128,768]{2,1,0:T(8,128)(2,1)S(1)} collective-permute-done((bf16[2,128,768]{2,1,0:T(8,128)(2,1)}, bf16[2,128,768]{2,1,0:T(8,128)(2,1)S(1)}, u32[]{:S(2)}, u32[]{:S(2)}) %collective-permute-start.1) | collective-permute-done | bytes 393248 | tf_op jit(solution)/shard_map/ppermute | solution.py:47
  27.0 1.5 %gradient_part.1 = (f32[576,768]{1,0:T(8,128)S(1)}, bf16[576,768]{1,0:T(8,128)(2,1)S(1)}) custom-call(bf16[2,128,768]{2,1,0:T(8,128)(2,1)S(1)} %get-tuple-element.32.refs_0_, bf16[2,128,768]{2,1,0:T(8,128)(2,1)S(1)} %collective-permute-done.8.refs_1_, bf16[2,128,768]{2,1,0:T(8,128)(2,1)S(1)} %collective-permute-done.5.refs_2_, ...), custom_call_target="tpu_custom_call" | custom-call | flops 905969664 | bytes 5111808 | tf_op jit(solution)/shard_map/gradient_part/pallas_call | solution.py:57
  28.8 1.5 %gradient.1 = (bf16[2,80,768]{2,1,0:T(8,128)(2,1)S(1)}, f32[2,80,768]{2,1,0:T(8,128)S(1)}, bf16[2,64,768]{2,1,0:T(8,128)(2,1)S(1)}, f32[2,64,768]{2,1,0:T(8,128)S(1)}) custom-call(bf16[2,128,768]{2,1,0:T(8,128)(2,1)S(1)} %collective-permute-done.1.refs_0_, bf16[2,128,768]{2,1,0:T(8,128)(2,1)S(1)} %collective-permute-done.2.refs_1_, ...), custom_call_target="tpu_custom_call" | custom-call | flops 905969664 | bytes 5554176 | tf_op jit(solution)/shard_map/gradient/pallas_call | solution.py:57
  30.3 1.6 %collective-permute-start.13 = (bf16[2,80,768]{2,1,0:T(8,128)(2,1)S(1)}, bf16[2,80,768]{2,1,0:T(8,128)(2,1)S(1)}, u32[]{:S(2)}, u32[]{:S(2)}) collective-permute-start(bf16[2,80,768]{2,1,0:T(8,128)(2,1)S(1)} %get-tuple-element.36), channel_id=1, source_target_pairs={{0,2},{1,3},{2,0},{3,1},{4,6},{5,7},{6,4},{7,5},{8,10},{9,11},{10,... | collective-permute-start | bytes 737288 | tf_op jit(solution)/shard_map/ppermute | solution.py:47
  33.1 1.4 %collective-permute-start.11 = (bf16[128,768]{1,0:T(8,128)(2,1)S(1)}, bf16[128,768]{1,0:T(8,128)(2,1)S(1)}, u32[]{:S(2)}, u32[]{:S(2)}) collective-permute-start(bf16[128,768]{1,0:T(8,128)(2,1)S(1)} %get-tuple-element.38.refs_1_), channel_id=1, source_target_pairs={{0,1},{1,0},{2,3},{3,2},{4,5},{5,4},{6,7},{7,6},{8,9},{9,8},{10,11... | collective-permute-start | bytes 589832 | tf_op jit(solution)/shard_map/ppermute | solution.py:47
  34.4 4.7 %collective-permute-done.13.arrived_ref = bf16[2,80,768]{2,1,0:T(8,128)(2,1)S(1)} collective-permute-done((bf16[2,80,768]{2,1,0:T(8,128)(2,1)S(1)}, bf16[2,80,768]{2,1,0:T(8,128)(2,1)S(1)}, u32[]{:S(2)}, u32[]{:S(2)}) %collective-permute-start.13) | collective-permute-done | bytes 245792 | tf_op jit(solution)/shard_map/ppermute | solution.py:47
  39.6 4.1 %collective-permute-done.15.arrived_ref = bf16[2,64,768]{2,1,0:T(8,128)(2,1)S(1)} collective-permute-done((bf16[2,64,768]{2,1,0:T(8,128)(2,1)S(1)}, bf16[2,64,768]{2,1,0:T(8,128)(2,1)S(1)}, u32[]{:S(2)}, u32[]{:S(2)}) %collective-permute-start.15) | collective-permute-done | bytes 196640 | tf_op jit(solution)/shard_map/ppermute | solution.py:47
  43.9 1.8 %collective-permute-start.12 = (bf16[128,768]{1,0:T(8,128)(2,1)S(1)}, bf16[128,768]{1,0:T(8,128)(2,1)S(1)}, u32[]{:S(2)}, u32[]{:S(2)}) collective-permute-start(bf16[128,768]{1,0:T(8,128)(2,1)S(1)} %get-tuple-element.38.refs_1_), channel_id=1, source_target_pairs={{0,17},{1,16},{2,19},{3,18},{4,21},{5,20},{6,23},{7,22},{8,25},{9,... | collective-permute-start | bytes 589832 | tf_op jit(solution)/shard_map/ppermute | solution.py:47
  45.7 2.0 %collective-permute-done.14.arrived_ref = bf16[1,80,768]{2,1,0:T(8,128)(2,1)S(1)} collective-permute-done((bf16[1,80,768]{2,1,0:T(8,128)(2,1)S(1)}, bf16[1,80,768]{2,1,0:T(8,128)(2,1)S(1)}, u32[]{:S(2)}, u32[]{:S(2)}) %collective-permute-start.14) | collective-permute-done | bytes 122912 | tf_op jit(solution)/shard_map/ppermute | solution.py:47
  48.8 3.4 %collective-permute-start.17 = (bf16[80,768]{1,0:T(8,128)(2,1)S(1)}, bf16[80,768]{1,0:T(8,128)(2,1)S(1)}, u32[]{:S(2)}, u32[]{:S(2)}) collective-permute-start(bf16[80,768]{1,0:T(8,128)(2,1)S(1)} %step.2.refs_2_), channel_id=1, source_target_pairs={{0,2},{1,3},{2,0},{3,1},{4,6},{5,7},{6,4},{7,5},{8,10},{9,11},{10,... | collective-permute-start | bytes 368648 | tf_op jit(solution)/shard_map/ppermute | solution.py:47
  53.1 5.0 %collective-permute-start.18 = (bf16[64,768]{1,0:T(8,128)(2,1)S(1)}, bf16[64,768]{1,0:T(8,128)(2,1)S(1)}, u32[]{:S(2)}, u32[]{:S(2)}) collective-permute-start(bf16[64,768]{1,0:T(8,128)(2,1)S(1)} %step.3.refs_3_), channel_id=1, source_target_pairs={{0,2},{1,3},{2,0},{3,1},{4,6},{5,7},{6,4},{7,5},{8,10},{9,11},{10,... | collective-permute-start | bytes 294920 | tf_op jit(solution)/shard_map/ppermute | solution.py:47
  58.1 2.3 %collective-permute-done.20.refs_7_ = bf16[64,768]{1,0:T(8,128)(2,1)S(1)} collective-permute-done((bf16[64,768]{1,0:T(8,128)(2,1)S(1)}, bf16[64,768]{1,0:T(8,128)(2,1)S(1)}, u32[]{:S(2)}, u32[]{:S(2)}) %collective-permute-start.20) | collective-permute-done | bytes 98336 | tf_op jit(solution)/shard_map/ppermute | solution.py:47
  61.9 1.5 %collective-permute-done.21.refs_8_ = bf16[80,768]{1,0:T(8,128)(2,1)S(1)} collective-permute-done((bf16[80,768]{1,0:T(8,128)(2,1)S(1)}, bf16[80,768]{1,0:T(8,128)(2,1)S(1)}, u32[]{:S(2)}, u32[]{:S(2)}) %collective-permute-start.21) | collective-permute-done | bytes 122912 | tf_op jit(solution)/shard_map/ppermute | solution.py:47
  63.9 1.8 %collective-permute-done.22.refs_9_ = bf16[64,768]{1,0:T(8,128)(2,1)S(1)} collective-permute-done((bf16[64,768]{1,0:T(8,128)(2,1)S(1)}, bf16[64,768]{1,0:T(8,128)(2,1)S(1)}, u32[]{:S(2)}, u32[]{:S(2)}) %collective-permute-start.22) | collective-permute-done | bytes 98336 | tf_op jit(solution)/shard_map/ppermute | solution.py:47
  69.6 1.4 %collective-permute-start.32 = (bf16[128,768]{1,0:T(8,128)(2,1)S(1)}, bf16[128,768]{1,0:T(8,128)(2,1)S(1)}, u32[]{:S(2)}, u32[]{:S(2)}) collective-permute-start(bf16[128,768]{1,0:T(8,128)(2,1)S(1)} %get-tuple-element.51), channel_id=1, source_target_pairs={{0,1},{1,0},{2,3},{3,2},{4,5},{5,4},{6,7},{7,6},{8,9},{9,8},{10,11... | collective-permute-start | bytes 589832 | tf_op jit(solution)/shard_map/ppermute | solution.py:47
  73.0 2.1 %attention.1.refs_1_ = f32[128,768]{1,0:T(8,128)S(1)} custom-call(bf16[128,768]{1,0:T(8,128)(2,1)S(1)} %copy-done.4, bf16[128,768]{1,0:T(8,128)(2,1)S(1)} %copy-done.1, bf16[128,768]{1,0:T(8,128)(2,1)S(1)} %copy-done.2), custom_call_target="tpu_custom_call" | custom-call | flops 50331648 | bytes 983040 | tf_op jit(solution)/shard_map/attention/pallas_call | solution.py:57
  76.3 3.2 %collective-permute-done.32.refs_3_ = bf16[128,768]{1,0:T(8,128)(2,1)S(1)} collective-permute-done((bf16[128,768]{1,0:T(8,128)(2,1)S(1)}, bf16[128,768]{1,0:T(8,128)(2,1)S(1)}, u32[]{:S(2)}, u32[]{:S(2)}) %collective-permute-start.32) | collective-permute-done | bytes 196640 | tf_op jit(solution)/shard_map/ppermute | solution.py:47
  (70 shorter events, 20.7 us)
Async XLA Ops:
  0.0 14.5 %collective-permute-start = (bf16[3,48,768]{2,1,0:T(8,128)(2,1)}, bf16[3,48,768]{2,1,0:T(8,128)(2,1)S(1)}, u32[]{:S(2)}, u32[]{:S(2)}) collective-permute-start(bf16[3,48,768]{2,1,0:T(8,128)(2,1)} %weights_ref), channel_id=1, source_target_pairs={{0,4},{1,5},{2,6},{3,7},{4,0},{5,1},{6,2},{7,3},{8,12},{9,13},{10,... | collective-permute-start | bytes 663560 | tf_op jit(solution)/shard_map/ppermute | solution.py:47
  6.0 12.3 %collective-permute-start.5 = (bf16[2,128,768]{2,1,0:T(8,128)(2,1)}, bf16[2,128,768]{2,1,0:T(8,128)(2,1)S(1)}, u32[]{:S(2)}, u32[]{:S(2)}) collective-permute-start(bf16[2,128,768]{2,1,0:T(8,128)(2,1)} %prep.1.pair_ref), channel_id=1, source_target_pairs={{0,16},{1,17},{2,18},{3,19},{4,20},{5,21},{6,22},{7,23},{8,24},{9,... | collective-permute-start | bytes 1179656 | tf_op jit(solution)/shard_map/ppermute | solution.py:47
  7.6 18.9 %collective-permute-start.1 = (bf16[2,128,768]{2,1,0:T(8,128)(2,1)}, bf16[2,128,768]{2,1,0:T(8,128)(2,1)S(1)}, u32[]{:S(2)}, u32[]{:S(2)}) collective-permute-start(bf16[2,128,768]{2,1,0:T(8,128)(2,1)} %prep.1.pair_ref), channel_id=1, source_target_pairs={{0,1},{1,0},{2,3},{3,2},{4,5},{5,4},{6,7},{7,6},{8,9},{9,8},{10,11... | collective-permute-start | bytes 1179656 | tf_op jit(solution)/shard_map/ppermute | solution.py:47
  9.1 17.4 %collective-permute-start.2 = (bf16[2,128,768]{2,1,0:T(8,128)(2,1)}, bf16[2,128,768]{2,1,0:T(8,128)(2,1)S(1)}, u32[]{:S(2)}, u32[]{:S(2)}) collective-permute-start(bf16[2,128,768]{2,1,0:T(8,128)(2,1)} %prep.1.pair_ref), channel_id=1, source_target_pairs={{0,17},{1,16},{2,19},{3,18},{4,21},{5,20},{6,23},{7,22},{8,25},{9,... | collective-permute-start | bytes 1179656 | tf_op jit(solution)/shard_map/ppermute | solution.py:47
  9.6 9.7 %collective-permute-start.6 = (bf16[3,48,768]{2,1,0:T(8,128)(2,1)}, bf16[3,48,768]{2,1,0:T(8,128)(2,1)S(1)}, u32[]{:S(2)}, u32[]{:S(2)}) collective-permute-start(bf16[3,48,768]{2,1,0:T(8,128)(2,1)} %weights_ref), channel_id=1, source_target_pairs={{0,2},{1,3},{2,0},{3,1},{4,6},{5,7},{6,4},{7,5},{8,10},{9,11},{10,... | collective-permute-start | bytes 663560 | tf_op jit(solution)/shard_map/ppermute | solution.py:47
  14.5 9.4 %collective-permute-start.7 = (bf16[3,48,768]{2,1,0:T(8,128)(2,1)S(1)}, bf16[3,48,768]{2,1,0:T(8,128)(2,1)S(1)}, u32[]{:S(2)}, u32[]{:S(2)}) collective-permute-start(bf16[3,48,768]{2,1,0:T(8,128)(2,1)S(1)} %collective-permute-done.refs_6_), channel_id=1, source_target_pairs={{0,2},{1,3},{2,0},{3,1},{4,6},{5,7},{6,4},{7,5},{8,10},{9,11},{10,... | collective-permute-start | bytes 663560 | tf_op jit(solution)/shard_map/ppermute | solution.py:47
  18.3 8.7 %collective-permute-start.9 = (bf16[2,128,768]{2,1,0:T(8,128)(2,1)S(1)}, bf16[2,128,768]{2,1,0:T(8,128)(2,1)S(1)}, u32[]{:S(2)}, u32[]{:S(2)}) collective-permute-start(bf16[2,128,768]{2,1,0:T(8,128)(2,1)S(1)} %collective-permute-done.5.refs_2_), channel_id=1, source_target_pairs={{0,8},{1,9},{2,10},{3,11},{4,12},{5,13},{6,14},{7,15},{8,0},{9,1},... | collective-permute-start | bytes 1179656 | tf_op jit(solution)/shard_map/ppermute | solution.py:47
  30.3 8.9 %collective-permute-start.13 = (bf16[2,80,768]{2,1,0:T(8,128)(2,1)S(1)}, bf16[2,80,768]{2,1,0:T(8,128)(2,1)S(1)}, u32[]{:S(2)}, u32[]{:S(2)}) collective-permute-start(bf16[2,80,768]{2,1,0:T(8,128)(2,1)S(1)} %get-tuple-element.36), channel_id=1, source_target_pairs={{0,2},{1,3},{2,0},{3,1},{4,6},{5,7},{6,4},{7,5},{8,10},{9,11},{10,... | collective-permute-start | bytes 737288 | tf_op jit(solution)/shard_map/ppermute | solution.py:47
  31.9 11.8 %collective-permute-start.15 = (bf16[2,64,768]{2,1,0:T(8,128)(2,1)S(1)}, bf16[2,64,768]{2,1,0:T(8,128)(2,1)S(1)}, u32[]{:S(2)}, u32[]{:S(2)}) collective-permute-start(bf16[2,64,768]{2,1,0:T(8,128)(2,1)S(1)} %get-tuple-element.43), channel_id=1, source_target_pairs={{0,2},{1,3},{2,0},{3,1},{4,6},{5,7},{6,4},{7,5},{8,10},{9,11},{10,... | collective-permute-start | bytes 589832 | tf_op jit(solution)/shard_map/ppermute | solution.py:47
  32.4 11.5 %collective-permute-start.10 = (bf16[128,768]{1,0:T(8,128)(2,1)S(1)}, bf16[128,768]{1,0:T(8,128)(2,1)S(1)}, u32[]{:S(2)}, u32[]{:S(2)}) collective-permute-start(bf16[128,768]{1,0:T(8,128)(2,1)S(1)} %get-tuple-element.38.refs_1_), channel_id=1, source_target_pairs={{0,16},{1,17},{2,18},{3,19},{4,20},{5,21},{6,22},{7,23},{8,24},{9,... | collective-permute-start | bytes 589832 | tf_op jit(solution)/shard_map/ppermute | solution.py:47
  33.1 10.8 %collective-permute-start.11 = (bf16[128,768]{1,0:T(8,128)(2,1)S(1)}, bf16[128,768]{1,0:T(8,128)(2,1)S(1)}, u32[]{:S(2)}, u32[]{:S(2)}) collective-permute-start(bf16[128,768]{1,0:T(8,128)(2,1)S(1)} %get-tuple-element.38.refs_1_), channel_id=1, source_target_pairs={{0,1},{1,0},{2,3},{3,2},{4,5},{5,4},{6,7},{7,6},{8,9},{9,8},{10,11... | collective-permute-start | bytes 589832 | tf_op jit(solution)/shard_map/ppermute | solution.py:47
  39.2 8.4 %collective-permute-start.14 = (bf16[1,80,768]{2,1,0:T(8,128)(2,1)S(1)}, bf16[1,80,768]{2,1,0:T(8,128)(2,1)S(1)}, u32[]{:S(2)}, u32[]{:S(2)}) collective-permute-start(bf16[1,80,768]{2,1,0:T(8,128)(2,1)S(1)} %get-tuple-element.41), channel_id=1, source_target_pairs={{0,4},{1,5},{2,6},{3,7},{4,0},{5,1},{6,2},{7,3},{8,12},{9,13},{10,... | collective-permute-start | bytes 368648 | tf_op jit(solution)/shard_map/ppermute | solution.py:47
  43.8 9.1 %collective-permute-start.16 = (bf16[1,64,768]{2,1,0:T(8,128)(2,1)S(1)}, bf16[1,64,768]{2,1,0:T(8,128)(2,1)S(1)}, u32[]{:S(2)}, u32[]{:S(2)}) collective-permute-start(bf16[1,64,768]{2,1,0:T(8,128)(2,1)S(1)} %get-tuple-element.45), channel_id=1, source_target_pairs={{0,4},{1,5},{2,6},{3,7},{4,0},{5,1},{6,2},{7,3},{8,12},{9,13},{10,... | collective-permute-start | bytes 294920 | tf_op jit(solution)/shard_map/ppermute | solution.py:47
  43.9 17.1 %collective-permute-start.12 = (bf16[128,768]{1,0:T(8,128)(2,1)S(1)}, bf16[128,768]{1,0:T(8,128)(2,1)S(1)}, u32[]{:S(2)}, u32[]{:S(2)}) collective-permute-start(bf16[128,768]{1,0:T(8,128)(2,1)S(1)} %get-tuple-element.38.refs_1_), channel_id=1, source_target_pairs={{0,17},{1,16},{2,19},{3,18},{4,21},{5,20},{6,23},{7,22},{8,25},{9,... | collective-permute-start | bytes 589832 | tf_op jit(solution)/shard_map/ppermute | solution.py:47
  47.8 10.2 %collective-permute-start.19 = (bf16[80,768]{1,0:T(8,128)(2,1)S(1)}, bf16[80,768]{1,0:T(8,128)(2,1)S(1)}, u32[]{:S(2)}, u32[]{:S(2)}) collective-permute-start(bf16[80,768]{1,0:T(8,128)(2,1)S(1)} %step.2.refs_2_), channel_id=1, source_target_pairs={{0,4},{1,5},{2,6},{3,7},{4,0},{5,1},{6,2},{7,3},{8,12},{9,13},{10,... | collective-permute-start | bytes 368648 | tf_op jit(solution)/shard_map/ppermute | solution.py:47
  48.8 11.6 %collective-permute-start.17 = (bf16[80,768]{1,0:T(8,128)(2,1)S(1)}, bf16[80,768]{1,0:T(8,128)(2,1)S(1)}, u32[]{:S(2)}, u32[]{:S(2)}) collective-permute-start(bf16[80,768]{1,0:T(8,128)(2,1)S(1)} %step.2.refs_2_), channel_id=1, source_target_pairs={{0,2},{1,3},{2,0},{3,1},{4,6},{5,7},{6,4},{7,5},{8,10},{9,11},{10,... | collective-permute-start | bytes 368648 | tf_op jit(solution)/shard_map/ppermute | solution.py:47
  53.0 7.4 %collective-permute-start.20 = (bf16[64,768]{1,0:T(8,128)(2,1)S(1)}, bf16[64,768]{1,0:T(8,128)(2,1)S(1)}, u32[]{:S(2)}, u32[]{:S(2)}) collective-permute-start(bf16[64,768]{1,0:T(8,128)(2,1)S(1)} %step.3.refs_3_), channel_id=1, source_target_pairs={{0,4},{1,5},{2,6},{3,7},{4,0},{5,1},{6,2},{7,3},{8,12},{9,13},{10,... | collective-permute-start | bytes 294920 | tf_op jit(solution)/shard_map/ppermute | solution.py:47
  53.1 8.8 %collective-permute-start.18 = (bf16[64,768]{1,0:T(8,128)(2,1)S(1)}, bf16[64,768]{1,0:T(8,128)(2,1)S(1)}, u32[]{:S(2)}, u32[]{:S(2)}) collective-permute-start(bf16[64,768]{1,0:T(8,128)(2,1)S(1)} %step.3.refs_3_), channel_id=1, source_target_pairs={{0,2},{1,3},{2,0},{3,1},{4,6},{5,7},{6,4},{7,5},{8,10},{9,11},{10,... | collective-permute-start | bytes 294920 | tf_op jit(solution)/shard_map/ppermute | solution.py:47
  58.1 5.3 %collective-permute-start.21 = (bf16[80,768]{1,0:T(8,128)(2,1)S(1)}, bf16[80,768]{1,0:T(8,128)(2,1)S(1)}, u32[]{:S(2)}, u32[]{:S(2)}) collective-permute-start(bf16[80,768]{1,0:T(8,128)(2,1)S(1)} %collective-permute-done.19.refs_6_), channel_id=1, source_target_pairs={{0,2},{1,3},{2,0},{3,1},{4,6},{5,7},{6,4},{7,5},{8,10},{9,11},{10,... | collective-permute-start | bytes 368648 | tf_op jit(solution)/shard_map/ppermute | solution.py:47
  60.4 5.3 %collective-permute-start.23 = (bf16[80,768]{1,0:T(8,128)(2,1)S(1)}, bf16[80,768]{1,0:T(8,128)(2,1)S(1)}, u32[]{:S(2)}, u32[]{:S(2)}) collective-permute-start(bf16[80,768]{1,0:T(8,128)(2,1)S(1)} %step.2.refs_2_), channel_id=1, source_target_pairs={{0,8},{1,9},{2,10},{3,11},{4,12},{5,13},{6,14},{7,15},{8,0},{9,1},... | collective-permute-start | bytes 368648 | tf_op jit(solution)/shard_map/ppermute | solution.py:47
  60.9 4.8 %collective-permute-start.22 = (bf16[64,768]{1,0:T(8,128)(2,1)S(1)}, bf16[64,768]{1,0:T(8,128)(2,1)S(1)}, u32[]{:S(2)}, u32[]{:S(2)}) collective-permute-start(bf16[64,768]{1,0:T(8,128)(2,1)S(1)} %collective-permute-done.20.refs_7_), channel_id=1, source_target_pairs={{0,2},{1,3},{2,0},{3,1},{4,6},{5,7},{6,4},{7,5},{8,10},{9,11},{10,... | collective-permute-start | bytes 294920 | tf_op jit(solution)/shard_map/ppermute | solution.py:47
  68.4 7.8 %collective-permute-start.31 = (bf16[128,768]{1,0:T(8,128)(2,1)S(1)}, bf16[128,768]{1,0:T(8,128)(2,1)S(1)}, u32[]{:S(2)}, u32[]{:S(2)}) collective-permute-start(bf16[128,768]{1,0:T(8,128)(2,1)S(1)} %get-tuple-element.50), channel_id=1, source_target_pairs={{0,16},{1,17},{2,18},{3,19},{4,20},{5,21},{6,22},{7,23},{8,24},{9,... | collective-permute-start | bytes 589832 | tf_op jit(solution)/shard_map/ppermute | solution.py:47
  69.6 9.8 %collective-permute-start.32 = (bf16[128,768]{1,0:T(8,128)(2,1)S(1)}, bf16[128,768]{1,0:T(8,128)(2,1)S(1)}, u32[]{:S(2)}, u32[]{:S(2)}) collective-permute-start(bf16[128,768]{1,0:T(8,128)(2,1)S(1)} %get-tuple-element.51), channel_id=1, source_target_pairs={{0,1},{1,0},{2,3},{3,2},{4,5},{5,4},{6,7},{7,6},{8,9},{9,8},{10,11... | collective-permute-start | bytes 589832 | tf_op jit(solution)/shard_map/ppermute | solution.py:47
  71.9 8.7 %collective-permute-start.33 = (bf16[128,768]{1,0:T(8,128)(2,1)S(1)}, bf16[128,768]{1,0:T(8,128)(2,1)S(1)}, u32[]{:S(2)}, u32[]{:S(2)}) collective-permute-start(bf16[128,768]{1,0:T(8,128)(2,1)S(1)} %get-tuple-element.52), channel_id=1, source_target_pairs={{0,17},{1,16},{2,19},{3,18},{4,21},{5,20},{6,23},{7,22},{8,25},{9,... | collective-permute-start | bytes 589832 | tf_op jit(solution)/shard_map/ppermute | solution.py:47
  (16 other events, 89.8 us)
